TPU v7x, 32 devices: a whole 2x2x4 slice. The times are simulated.
32 devices in a mesh: bx: 4 (over x, core), by: 4 (over z), bz: 2 (over y).
Axes of the slice: x: 2, y: 2, z: 4, core: 2. Of those that a mesh axis runs over, the one named last changes fastest.
Arguments:
- density: float32 [64, 512, 512], P('bz', 'bx', 'by'), may hold values from 0.2 to 2
- material: int32 [64, 512, 512], P('bz', 'bx', 'by'), may hold values from 0 to 255
- color_table: bfloat16 [3, 256], replicated, may hold values from 0.049804688 to 1
- extinction_table: bfloat16 [256], replicated, may hold values from 0.099609375 to 4
- order: int32 [4, 4, 2], P('bx', 'by'), may hold values from 0 to 1, as said below
Outputs:
- image: float32 [4, 512, 512], P(None, ('bx', 'bz'), 'by')
Inputs may be any that keep to these rules, and one draw needn't show every extreme that they name: order[a, b, j] equals j XOR m for one number m of each brick column (a, b), the same for every slab j of that column.
All inputs are finite; a program needn't handle non-finite values.
Results may differ from a plain program's by a relative error of at most 0.0003.
Values sent between devices are 32-bit elements; how exact they have to be, the bound alone decides.
No kernel may reach another device: no remote copies, remote signals or barrier semaphores. Data moves between devices by JAX's collectives and lax.ppermute only.
A program may use at most 128 MiB of HBM per device.

v0:
```python
import functools
import math

import jax
import jax.numpy as jnp
from jax import lax
from jax.experimental import pallas as pl
from jax.experimental.pallas import tpu as pltpu
from jax.sharding import PartitionSpec as P

LANES = 128
SUBLANES = 8
PAD = 8
REACH = 2
COLOR_UNIT = 4096.0
EXTINCTION_UNIT = 2048.0
VMEM_LIMIT = 48 * 2**20

VMEM = pl.BlockSpec(memory_space=pltpu.VMEM)
SMEM = pl.BlockSpec(memory_space=pltpu.SMEM)
ANY = pl.BlockSpec(memory_space=pl.ANY)


def lane_index():
    return lax.broadcasted_iota(jnp.int32, (SUBLANES, LANES), 1)


def is_odd(axis):
    return jnp.bitwise_and(lax.axis_index(axis), 1) == 1


def swaps(count):
    first = [(i, i ^ 1) for i in range(count)]
    second = [(i, i + 1 if i % 2 else i - 1) for i in range(1, count - 1)]
    return first, second


def faces_kernel(counts, density, padded, y_out, xa, xb, za, zb, arrived):
    planes, rows, _ = density.shape
    parts = arrived.shape[0]
    step = rows // parts
    copies = [
        pltpu.make_async_copy(
            density.at[:, pl.ds(k * step, step), :],
            padded.at[pl.ds(REACH, planes), pl.ds(PAD + k * step, step), :],
            arrived.at[k],
        )
        for k in range(parts)
    ]
    for copy in copies:
        copy.start()
    slot = jnp.right_shift(lane_index(), 2)
    for k in range(parts):
        copies[k].wait()
        for tile in range(step // SUBLANES):
            row = k * step + tile * SUBLANES
            packed = jnp.zeros((SUBLANES, LANES), jnp.float32)
            for z in range(planes):
                plane = padded[REACH + z, PAD + row : PAD + row + SUBLANES, :]
                packed = jnp.where(slot == z, pltpu.roll(plane, (4 * z + REACH) % LANES, 1), packed)
            y_out[row : row + SUBLANES, :] = packed
    odd_x, odd_z = is_odd("bx"), is_odd("bz")
    low_x, high_x = PAD, PAD + rows - REACH
    low_z, high_z = REACH, planes
    for out, start in ((xa, jnp.where(odd_x, low_x, high_x)), (xb, jnp.where(odd_x, high_x, low_x))):
        for z in range(planes):
            out[REACH * z : REACH * (z + 1), :] = padded[REACH + z, pl.ds(start, REACH), :]
    for out, start in ((za, jnp.where(odd_z, low_z, high_z)), (zb, jnp.where(odd_z, high_z, low_z))):
        if out is zb and counts["bz"] == 2:
            continue
        for layer in range(REACH):
            out[layer] = padded[start + layer, PAD : PAD + rows, :]
    if counts["bz"] == 2:
        zb[...] = jnp.zeros(zb.shape, jnp.float32)


def faces(density, counts):
    planes, rows, cols = density.shape
    shape = lambda *dims: jax.ShapeDtypeStruct(dims, jnp.float32)
    z_rows = rows if counts["bz"] > 2 else SUBLANES
    return pl.pallas_call(
        functools.partial(faces_kernel, counts),
        out_shape=(
            shape(planes + 2 * REACH, rows + 2 * PAD, cols),
            shape(rows, LANES),
            shape(REACH * planes, cols),
            shape(REACH * planes, cols),
            shape(REACH, rows, cols),
            shape(REACH, z_rows, cols),
        ),
        in_specs=[ANY],
        out_specs=(VMEM,) * 6,
        scratch_shapes=[pltpu.SemaphoreType.DMA((4,))],
        compiler_params=pltpu.CompilerParams(vmem_limit_bytes=VMEM_LIMIT),
        name="faces",
    )(density)


def local_kernel(total_planes, order, padded, material, colors, extinction, lit, slope_y, through):
    planes, rows, _ = material.shape
    slabs = lax.axis_size("bz")
    backward = order[0, 0, 0] > order[0, 0, slabs - 1]
    k = jnp.bitwise_and(lax.broadcasted_iota(jnp.int32, (2 * LANES, LANES), 0), LANES - 1)
    gap = k - lax.broadcasted_iota(jnp.int32, (2 * LANES, LANES), 1)
    band = jnp.where(gap == 1, 8.0, jnp.where(gap == -1, -8.0, 0.0))
    band = band + jnp.where(gap == 2, -1.0, jnp.where(gap == -2, 1.0, 0.0))
    band = band.astype(jnp.bfloat16)

    def derive(step, carry):
        for z in (2 * step, 2 * step + 1):
            plane = padded[REACH + z, PAD : PAD + rows, :]
            coarse = plane.astype(jnp.bfloat16)
            fine = (plane - coarse.astype(jnp.float32)).astype(jnp.bfloat16)
            slope_y[z] = jnp.dot(
                jnp.concatenate([coarse, fine], axis=1), band, preferred_element_type=jnp.float32
            )
        return carry

    lax.fori_loop(0, planes // 2, derive, 0)

    color = (colors[...].astype(jnp.float32) * COLOR_UNIT).astype(jnp.int32)
    dense = (extinction[...].astype(jnp.float32) * EXTINCTION_UNIT).astype(jnp.int32)

    def halves(row):
        return [
            jnp.broadcast_to(row[:, start : start + LANES], (SUBLANES, LANES))
            for start in (0, LANES)
        ]

    red_green = halves(color[0:1] * 65536 + color[1:2])
    blue_dense = halves(color[2:3] * 65536 + dense)
    scale = -3.0 * math.log2(math.e) / (EXTINCTION_UNIT * total_planes)

    def take(table, low, upper):
        found = [jnp.take_along_axis(t, low, axis=1, mode="promise_in_bounds") for t in table]
        return jnp.where(upper, found[1], found[0])

    def tile(index, carry):
        row = pl.multiple_of(index * SUBLANES, SUBLANES)
        clear = jnp.ones((SUBLANES, LANES), jnp.float32)
        for visit in range(planes):
            z = jnp.where(backward, planes - 1 - visit, visit)
            density = padded[REACH + z, pl.ds(PAD + row, SUBLANES), :]
            label = material[z, pl.ds(row, SUBLANES), :]
            low = jnp.bitwise_and(label, LANES - 1)
            upper = label >= LANES
            rg = take(red_green, low, upper)
            be = take(blue_dense, low, upper)
            extinct = jnp.bitwise_and(be, 65535).astype(jnp.float32)
            after = clear * jnp.exp2(extinct * (density * scale))
            stopped = clear - after
            lit[0, z, pl.ds(row, SUBLANES), :] = stopped * jnp.right_shift(rg, 16).astype(jnp.float32)
            lit[1, z, pl.ds(row, SUBLANES), :] = stopped * jnp.bitwise_and(rg, 65535).astype(jnp.float32)
            lit[2, z, pl.ds(row, SUBLANES), :] = stopped * jnp.right_shift(be, 16).astype(jnp.float32)
            clear = after
        through[pl.ds(row, SUBLANES), :] = clear
        return carry

    lax.fori_loop(0, rows // SUBLANES, tile, 0)


def local(order, padded, material, colors, extinction, total_planes):
    planes, rows, cols = material.shape
    shape = lambda *dims: jax.ShapeDtypeStruct(dims, jnp.float32)
    return pl.pallas_call(
        functools.partial(local_kernel, total_planes),
        out_shape=(shape(3, planes, rows, cols), shape(planes, rows, cols), shape(rows, cols)),
        in_specs=[SMEM] + [VMEM] * 4,
        out_specs=(VMEM,) * 3,
        compiler_params=pltpu.CompilerParams(vmem_limit_bytes=VMEM_LIMIT),
        cost_estimate=pl.CostEstimate(flops=20 * planes * rows * cols, bytes_accessed=2**22, transcendentals=planes * rows * cols),
        name="local",
    )(order, padded, material, colors, extinction)


def put_halo(padded, xa, xb, za, zb, ya, yb, edge, planes, rows):
    odd_x, odd_y, odd_z = is_odd("bx"), is_odd("by"), is_odd("bz")
    for z in range(planes):
        first, second = xa[REACH * z : REACH * (z + 1), :], xb[REACH * z : REACH * (z + 1), :]
        padded[REACH + z, PAD - REACH : PAD, :] = jnp.where(odd_x, first, second)
        padded[REACH + z, PAD + rows : PAD + rows + REACH, :] = jnp.where(odd_x, second, first)
    for layer in range(REACH):
        first = za[layer]
        second = zb[layer] if zb.shape == za.shape else jnp.zeros_like(first)
        padded[layer, PAD : PAD + rows, :] = jnp.where(odd_z, first, second)
        padded[REACH + planes + layer, PAD : PAD + rows, :] = jnp.where(odd_z, second, first)
    side = jnp.bitwise_and(lane_index(), 3)
    for row in range(0, rows, SUBLANES):
        first, second = ya[row : row + SUBLANES, :], yb[row : row + SUBLANES, :]
        near = jnp.where((side < 2) == odd_y, first, second)
        ahead1, ahead2 = pltpu.roll(near, LANES - 1, 1), pltpu.roll(near, LANES - 2, 1)
        behind1, behind2 = pltpu.roll(near, 1, 1), pltpu.roll(near, 2, 1)
        edge[row : row + SUBLANES, :] = jnp.where(
            side == 0,
            -ahead2,
            jnp.where(
                side == 1,
                8.0 * ahead1 - ahead2,
                jnp.where(side == 2, behind2 - 8.0 * behind1, behind2),
            ),
        )


def shade_kernel(padded_in, xa, xb, za, zb, ya, yb, lit, slope_y, through, padded, give, keep, edge):
    _, planes, rows, _ = lit.shape
    del padded_in
    put_halo(padded, xa, xb, za, zb, ya, yb, edge, planes, rows)
    slabs = lax.axis_size("bz")
    block_rows = rows // slabs
    my_half = jnp.bitwise_and(lax.axis_index("bz"), 1)
    lane = lane_index()
    at_edge = jnp.logical_or(lane < REACH, lane >= LANES - REACH)
    for out, half in ((give, 1 - my_half), (keep, my_half)):

        def tile(index, carry, out=out, half=half):
            to = pl.multiple_of(index * SUBLANES, SUBLANES)
            group = lax.div(to, block_rows)
            row = (group + half) * block_rows + to
            row = pl.multiple_of(row, SUBLANES)
            beside = edge[pl.ds(row, SUBLANES), :]
            sums = [jnp.zeros((SUBLANES, LANES), jnp.float32) for _ in range(3)]
            for z in range(planes):
                at = lambda dz, dx: padded[REACH + z + dz, pl.ds(PAD + row + dx, SUBLANES), :]
                sz = 8.0 * (at(1, 0) - at(-1, 0)) - (at(2, 0) - at(-2, 0))
                sx = 8.0 * (at(0, 1) - at(0, -1)) - (at(0, 2) - at(0, -2))
                outer = pltpu.roll(beside, (-4 * z - REACH) % LANES, 1)
                sy = slope_y[z, pl.ds(row, SUBLANES), :] + jnp.where(at_edge, outer, 0.0)
                size = sx * sx + sy * sy + sz * sz
                facing = jnp.abs(0.432 * sx + 0.54 * sy + 0.576 * sz)
                shading = 0.1 + facing * lax.rsqrt(jnp.maximum(size, 36.0))
                for c in range(3):
                    sums[c] = sums[c] + shading * lit[c, z, pl.ds(row, SUBLANES), :]
            for c in range(3):
                out[c, pl.ds(to, SUBLANES), :] = sums[c] * (1.0 / COLOR_UNIT)
            out[3, pl.ds(to, SUBLANES), :] = through[pl.ds(row, SUBLANES), :]
            return carry

        lax.fori_loop(0, rows // 2 // SUBLANES, tile, 0)


def shade(padded, halos, lit, slope_y, through):
    _, planes, rows, cols = lit.shape
    shape = lambda *dims: jax.ShapeDtypeStruct(dims, jnp.float32)
    return pl.pallas_call(
        shade_kernel,
        out_shape=(
            shape(*padded.shape),
            shape(4, rows // 2, cols),
            shape(4, rows // 2, cols),
        ),
        in_specs=[VMEM] * 10,
        out_specs=(VMEM,) * 3,
        scratch_shapes=[pltpu.VMEM((rows, LANES), jnp.float32)],
        input_output_aliases={0: 0},
        compiler_params=pltpu.CompilerParams(vmem_limit_bytes=VMEM_LIMIT),
        name="shade",
    )(padded, *halos, lit, slope_y, through)


def blend_kernel(bit, last, order, mine, other, out):
    rank = jnp.bitwise_xor(lax.axis_index("bz"), order[0, 0, 0])
    in_front = jnp.bitwise_and(jnp.right_shift(rank, bit), 1) == 0
    clear = jnp.where(in_front, mine[3], other[3])
    for c in range(3):
        front = jnp.where(in_front, mine[c], other[c])
        back = jnp.where(in_front, other[c], mine[c])
        out[c] = front + clear * back
    product = mine[3] * other[3]
    out[3] = 1.0 - product if last else product


def blend(order, mine, other, bit, last):
    return pl.pallas_call(
        functools.partial(blend_kernel, bit, last),
        out_shape=jax.ShapeDtypeStruct(mine.shape, jnp.float32),
        in_specs=[SMEM, VMEM, VMEM],
        out_specs=VMEM,
        compiler_params=pltpu.CompilerParams(vmem_limit_bytes=VMEM_LIMIT),
        name="blend",
    )(order, mine, other)


def shards(density, material, color_table, extinction_table, order):
    planes, rows, cols = density.shape
    counts = {axis: lax.axis_size(axis) for axis in ("bx", "by", "bz")}
    slabs = counts["bz"]
    padded, y_own, xa, xb, za, zb = faces(density, counts)
    pairs = {axis: swaps(counts[axis]) for axis in counts}
    xa = lax.ppermute(xa, "bx", pairs["bx"][0])
    xb = lax.ppermute(xb, "bx", pairs["bx"][1])
    za = lax.ppermute(za, "bz", pairs["bz"][0])
    if slabs > 2:
        zb = lax.ppermute(zb, "bz", pairs["bz"][1])
    ya = lax.ppermute(y_own, "by", pairs["by"][0])
    yb = lax.ppermute(y_own, "by", pairs["by"][1])
    lit, slope_y, through = local(
        order, padded, material, color_table, extinction_table.reshape(1, -1), planes * slabs
    )
    _, give, keep = shade(padded, (xa, xb, za, zb, ya, yb), lit, slope_y, through)
    block_rows = rows // slabs
    levels = slabs.bit_length() - 1
    my_slab = lax.axis_index("bz")
    for bit in range(levels):
        flip = [(i, i ^ (1 << bit)) for i in range(slabs)]
        received = lax.ppermute(give, "bz", flip)
        holding = blend(order, keep, received, bit, bit == levels - 1)
        if bit < levels - 1:
            paired = holding.reshape(4, -1, 2, block_rows, cols)
            half = jnp.bitwise_and(jnp.right_shift(my_slab, bit + 1), 1)
            take = lambda which: lax.dynamic_index_in_dim(paired, which, 2, keepdims=False)
            keep, give = (take(which).reshape(4, -1, cols) for which in (half, 1 - half))
    return holding


def solution(mesh):
    placed = (P("bz", "bx", "by"), P("bz", "bx", "by"), P(), P(), P("bx", "by", None))
    return jax.shard_map(
        shards, mesh=mesh, in_specs=placed, out_specs=P(None, ("bx", "bz"), "by"), check_vma=False
    )
```

profile of v0, /device:TPU:1, one launch (start us, length us, event | category | flops | bytes accessed | tf_op | source)
XLA Modules:
  0.0 40.6 jit_solution(16842345560790355767)
XLA Ops:
  0.0 0.0 copy-start.3
  0.0 1.6 %copy-done.3 = f32[32,128,128]{2,1,0:T(8,128)S(1)} copy-done((f32[32,128,128]{2,1,0:T(8,128)S(1)}, f32[32,128,128]{2,1,0:T(8,128)}, u32[]{:S(2)}) %copy-start.3) | copy-done | bytes 2097176
  1.6 0.0 copy-start.2
  1.6 1.0 %faces.1 = (f32[36,144,128]{2,1,0:T(8,128)S(1)}, f32[128,128]{1,0:T(8,128)S(1)}, f32[64,128]{1,0:T(8,128)S(1)}, f32[64,128]{1,0:T(8,128)S(1)}, f32[2,128,128]{2,1,0:T(8,128)S(1)}, /*index=5*/f32[2,8,128]{2,1,0:T(8,128)S(1)}) custom-call(f32[32,128,128]{2,1,0:T(8,128)S(1)} %copy-done.3), custom_call_target="tpu_custom_call" | custom-call | tf_op jit(solution)/shard_map/faces/pallas_call | solution.py:81
  2.6 0.0 copy-start
  2.6 1.6 %copy-done = f32[36,144,128]{2,1,0:T(8,128)} copy-done((f32[36,144,128]{2,1,0:T(8,128)}, f32[36,144,128]{2,1,0:T(8,128)S(1)}, u32[]{:S(2)}) %copy-start) | copy-done | bytes 2654232
  4.2 0.0 copy-start.1
  4.2 2.1 %collective-permute-start.2 = (f32[2,128,128]{2,1,0:T(8,128)S(1)}, f32[2,128,128]{2,1,0:T(8,128)S(1)}, u32[]{:S(2)}, u32[]{:S(2)}) collective-permute-start(f32[2,128,128]{2,1,0:T(8,128)S(1)} %get-tuple-element.19), channel_id=1, source_target_pairs={{0,1},{1,0},{2,3},{3,2},{4,5},{5,4},{6,7},{7,6},{8,9},{9,8},{10,11... | collective-permute-start | bytes 393224 | tf_op jit(solution)/shard_map/ppermute | solution.py:291
  6.3 0.7 %collective-permute-start.4 = (f32[128,128]{1,0:T(8,128)S(1)}, f32[128,128]{1,0:T(8,128)S(1)}, u32[]{:S(2)}, u32[]{:S(2)}) collective-permute-start(f32[128,128]{1,0:T(8,128)S(1)} %get-tuple-element.21), channel_id=1, source_target_pairs={{2,4},{4,2},{3,5},{5,3},{10,12},{12,10},{11,13},{13,11},{18,20},{2... | collective-permute-start | bytes 196616 | tf_op jit(solution)/shard_map/ppermute | solution.py:295
  6.9 3.9 %collective-permute-start.3 = (f32[128,128]{1,0:T(8,128)S(1)}, f32[128,128]{1,0:T(8,128)S(1)}, u32[]{:S(2)}, u32[]{:S(2)}) collective-permute-start(f32[128,128]{1,0:T(8,128)S(1)} %get-tuple-element.21), channel_id=1, source_target_pairs={{0,2},{2,0},{4,6},{6,4},{1,3},{3,1},{5,7},{7,5},{8,10},{10,8},{12,... | collective-permute-start | bytes 196616 | tf_op jit(solution)/shard_map/ppermute | solution.py:294
  10.8 1.5 %collective-permute-start = (f32[64,128]{1,0:T(8,128)S(1)}, f32[64,128]{1,0:T(8,128)S(1)}, u32[]{:S(2)}, u32[]{:S(2)}) collective-permute-start(f32[64,128]{1,0:T(8,128)S(1)} %get-tuple-element.17), channel_id=1, source_target_pairs={{0,8},{8,0},{16,24},{24,16},{1,9},{9,1},{17,25},{25,17},{2,10},{10... | collective-permute-start | bytes 98312 | tf_op jit(solution)/shard_map/ppermute | solution.py:289
  12.3 3.0 %collective-permute-start.1 = (f32[64,128]{1,0:T(8,128)S(1)}, f32[64,128]{1,0:T(8,128)S(1)}, u32[]{:S(2)}, u32[]{:S(2)}) collective-permute-start(f32[64,128]{1,0:T(8,128)S(1)} %get-tuple-element.18), channel_id=1, source_target_pairs={{8,16},{16,8},{9,17},{17,9},{10,18},{18,10},{11,19},{19,11},{12,20... | collective-permute-start | bytes 98312 | tf_op jit(solution)/shard_map/ppermute | solution.py:290
  15.4 0.7 %reshape.3.extinction = bf16[1,256]{1,0:T(2,128)(2,1)S(1)} reshape(bf16[256]{0:T(256)(128)(2,1)} %param.8) | data formatting | bytes 1024 | tf_op jit(solution)/shard_map/reshape | solution.py:297
  16.0 0.0 copy-done.2
  16.0 0.0 copy-start.4
  16.0 0.7 %copy-done.4 = bf16[3,256]{1,0:T(4,128)(2,1)S(1)} copy-done((bf16[3,256]{1,0:T(4,128)(2,1)S(1)}, bf16[3,256]{1,0:T(4,128)(2,1)}, u32[]{:S(2)}) %copy-start.4) | copy-done | bytes 1560
  16.7 0.0 copy-start.5
  16.7 0.7 %copy-done.5 = s32[1,1,2]{2,1,0:T(1,128)S(1)} copy-done((s32[1,1,2]{2,1,0:T(1,128)S(1)}, s32[1,1,2]{2,1,0:T(1,128)}, u32[]{:S(2)}) %copy-start.5) | copy-done | bytes 32
  17.4 12.4 %local.1 = (f32[3,32,128,128]{3,2,1,0:T(8,128)}, f32[32,128,128]{2,1,0:T(8,128)S(1)}, f32[128,128]{1,0:T(8,128)S(1)}) custom-call(s32[1,1,2]{2,1,0:T(1,128)S(1)} %copy-done.5, f32[36,144,128]{2,1,0:T(8,128)} %copy-done, s32[32,128,128]{2,1,0:T(8,128)S(1)} %copy-done.2, bf16[3,256]{1,0:T(4,128)(2,1)S(1)} %copy-done.4, bf16[1,256]{1,0:T(2,128)(2,1)S(1)} %reshape.3.extinction), custom_call_target="tpu_custom_call" | custom-call | flops 10485760 | bytes 4194304 | tf_op jit(solution)/shard_map/local/pallas_call | solution.py:165
  29.7 0.0 collective-permute-done.xa
  29.7 0.0 collective-permute-done.1.xb
  29.7 0.0 collective-permute-done.4.yb
  29.7 0.0 collective-permute-done.3.ya
  29.8 0.0 collective-permute-done.2.za
  29.8 0.0 copy-done.1
  29.8 5.8 %shade.1 = (f32[36,144,128]{2,1,0:T(8,128)S(1)}, f32[4,64,128]{2,1,0:T(8,128)S(1)}, f32[4,64,128]{2,1,0:T(8,128)S(1)}) custom-call(f32[36,144,128]{2,1,0:T(8,128)S(1)} %copy-done.1, f32[64,128]{1,0:T(8,128)S(1)} %collective-permute-done.xa, f32[64,128]{1,0:T(8,128)S(1)} %collective-permute-done.1.xb, ...), custom_call_target="tpu_custom_call", output_to_operand_aliasing={{0}: (0, {})} | custom-call | tf_op jit(solution)/shard_map/shade/pallas_call | solution.py:244
  35.5 0.4 %collective-permute-start.5 = (f32[4,64,128]{2,1,0:T(8,128)S(1)}, f32[4,64,128]{2,1,0:T(8,128)S(1)}, u32[]{:S(2)}, u32[]{:S(2)}) collective-permute-start(f32[4,64,128]{2,1,0:T(8,128)S(1)} %get-tuple-element.26), channel_id=1, source_target_pairs={{0,1},{1,0},{2,3},{3,2},{4,5},{5,4},{6,7},{7,6},{8,9},{9,8},{10,11... | collective-permute-start | bytes 393224 | tf_op jit(solution)/shard_map/ppermute | solution.py:305
  36.0 3.5 %collective-permute-done.5.other = f32[4,64,128]{2,1,0:T(8,128)S(1)} collective-permute-done((f32[4,64,128]{2,1,0:T(8,128)S(1)}, f32[4,64,128]{2,1,0:T(8,128)S(1)}, u32[]{:S(2)}, u32[]{:S(2)}) %collective-permute-start.5) | collective-permute-done | bytes 131104 | tf_op jit(solution)/shard_map/ppermute | solution.py:305
  39.4 1.2 %blend.1 = f32[4,64,128]{2,1,0:T(8,128)} custom-call(s32[1,1,2]{2,1,0:T(1,128)S(1)} %copy-done.5, f32[4,64,128]{2,1,0:T(8,128)S(1)} %get-tuple-element.25.mine, f32[4,64,128]{2,1,0:T(8,128)S(1)} %collective-permute-done.5.other), custom_call_target="tpu_custom_call" | custom-call | tf_op jit(solution)/shard_map/blend/pallas_call | solution.py:273
Async XLA Ops:
  0.0 1.6 %copy-start.3 = (f32[32,128,128]{2,1,0:T(8,128)S(1)}, f32[32,128,128]{2,1,0:T(8,128)}, u32[]{:S(2)}) copy-start(f32[32,128,128]{2,1,0:T(8,128)} %density.1) | copy-start | bytes 6291460
  1.6 14.4 %copy-start.2 = (s32[32,128,128]{2,1,0:T(8,128)S(1)}, s32[32,128,128]{2,1,0:T(8,128)}, u32[]{:S(2)}) copy-start(s32[32,128,128]{2,1,0:T(8,128)} %material.1) | copy-start | bytes 6291460
  2.6 1.6 %copy-start = (f32[36,144,128]{2,1,0:T(8,128)}, f32[36,144,128]{2,1,0:T(8,128)S(1)}, u32[]{:S(2)}) copy-start(f32[36,144,128]{2,1,0:T(8,128)S(1)} %get-tuple-element.16.padded.padded_in) | copy-start | bytes 7962628
  4.2 25.6 %copy-start.1 = (f32[36,144,128]{2,1,0:T(8,128)S(1)}, f32[36,144,128]{2,1,0:T(8,128)}, u32[]{:S(2)}) copy-start(f32[36,144,128]{2,1,0:T(8,128)} %copy-done) | copy-start | bytes 7962628
  4.2 25.6 %collective-permute-start.2 = (f32[2,128,128]{2,1,0:T(8,128)S(1)}, f32[2,128,128]{2,1,0:T(8,128)S(1)}, u32[]{:S(2)}, u32[]{:S(2)}) collective-permute-start(f32[2,128,128]{2,1,0:T(8,128)S(1)} %get-tuple-element.19), channel_id=1, source_target_pairs={{0,1},{1,0},{2,3},{3,2},{4,5},{5,4},{6,7},{7,6},{8,9},{9,8},{10,11... | collective-permute-start | bytes 393224 | tf_op jit(solution)/shard_map/ppermute | solution.py:291
  6.3 23.5 %collective-permute-start.4 = (f32[128,128]{1,0:T(8,128)S(1)}, f32[128,128]{1,0:T(8,128)S(1)}, u32[]{:S(2)}, u32[]{:S(2)}) collective-permute-start(f32[128,128]{1,0:T(8,128)S(1)} %get-tuple-element.21), channel_id=1, source_target_pairs={{2,4},{4,2},{3,5},{5,3},{10,12},{12,10},{11,13},{13,11},{18,20},{2... | collective-permute-start | bytes 196616 | tf_op jit(solution)/shard_map/ppermute | solution.py:295
  6.9 22.8 %collective-permute-start.3 = (f32[128,128]{1,0:T(8,128)S(1)}, f32[128,128]{1,0:T(8,128)S(1)}, u32[]{:S(2)}, u32[]{:S(2)}) collective-permute-start(f32[128,128]{1,0:T(8,128)S(1)} %get-tuple-element.21), channel_id=1, source_target_pairs={{0,2},{2,0},{4,6},{6,4},{1,3},{3,1},{5,7},{7,5},{8,10},{10,8},{12,... | collective-permute-start | bytes 196616 | tf_op jit(solution)/shard_map/ppermute | solution.py:294
  10.8 18.9 %collective-permute-start = (f32[64,128]{1,0:T(8,128)S(1)}, f32[64,128]{1,0:T(8,128)S(1)}, u32[]{:S(2)}, u32[]{:S(2)}) collective-permute-start(f32[64,128]{1,0:T(8,128)S(1)} %get-tuple-element.17), channel_id=1, source_target_pairs={{0,8},{8,0},{16,24},{24,16},{1,9},{9,1},{17,25},{25,17},{2,10},{10... | collective-permute-start | bytes 98312 | tf_op jit(solution)/shard_map/ppermute | solution.py:289
  12.3 17.4 %collective-permute-start.1 = (f32[64,128]{1,0:T(8,128)S(1)}, f32[64,128]{1,0:T(8,128)S(1)}, u32[]{:S(2)}, u32[]{:S(2)}) collective-permute-start(f32[64,128]{1,0:T(8,128)S(1)} %get-tuple-element.18), channel_id=1, source_target_pairs={{8,16},{16,8},{9,17},{17,9},{10,18},{18,10},{11,19},{19,11},{12,20... | collective-permute-start | bytes 98312 | tf_op jit(solution)/shard_map/ppermute | solution.py:290
  16.0 0.7 %copy-start.4 = (bf16[3,256]{1,0:T(4,128)(2,1)S(1)}, bf16[3,256]{1,0:T(4,128)(2,1)}, u32[]{:S(2)}) copy-start(bf16[3,256]{1,0:T(4,128)(2,1)} %colors.1) | copy-start | bytes 4612
  16.7 0.7 %copy-start.5 = (s32[1,1,2]{2,1,0:T(1,128)S(1)}, s32[1,1,2]{2,1,0:T(1,128)}, u32[]{:S(2)}) copy-start(s32[1,1,2]{2,1,0:T(1,128)} %order.3) | copy-start | bytes 28
  35.5 3.9 %collective-permute-start.5 = (f32[4,64,128]{2,1,0:T(8,128)S(1)}, f32[4,64,128]{2,1,0:T(8,128)S(1)}, u32[]{:S(2)}, u32[]{:S(2)}) collective-permute-start(f32[4,64,128]{2,1,0:T(8,128)S(1)} %get-tuple-element.26), channel_id=1, source_target_pairs={{0,1},{1,0},{2,3},{3,2},{4,5},{5,4},{6,7},{7,6},{8,9},{9,8},{10,11... | collective-permute-start | bytes 393224 | tf_op jit(solution)/shard_map/ppermute | solution.py:305
where the time goes:
time: 40.9 us; the launch traced here: 40.6 us
  Pallas kernels  20.4 us (50%)
  starting transfers between devices  11.6 us (28%)
  local copies, waits for them, and re-layouts  5.15 us (13%)
  waiting for transfers between devices  3.47 us (8%)
    pallas_call x1, Pallas kernels, local(): pl.pallas_call(functools.partial(local_kernel, total_planes), out_shape=(...  12.4 us
    pallas_call x1, Pallas kernels, shade(): pl.pallas_call(shade_kernel, out_shape=(shape(*padded.shape), shape(4, ro...  5.76 us
    unnamed x12, local copies, waits for them, and re-layouts  4.49 us
    ppermute x1, starting transfers between devices, shards(): ya = lax.ppermute(y_own, 'by', pairs['by'][0])  3.9 us
    ppermute x1, waiting for transfers between devices, shards(): received = lax.ppermute(give, 'bz', flip)  3.46 us
    ppermute x1, starting transfers between devices, shards(): xb = lax.ppermute(xb, 'bx', pairs['bx'][1])  3 us
    ppermute x1, starting transfers between devices, shards(): za = lax.ppermute(za, 'bz', pairs['bz'][0])  2.07 us
    ppermute x1, starting transfers between devices, shards(): xa = lax.ppermute(xa, 'bx', pairs['bx'][0])  1.52 us
  transfers between devices with their start and end apart: 6, of which 1 were waited for; matrix products, arithmetic and copies ran while one was open for 2% of the time, Pallas kernels for 30%

commit v1 on v0

v1 whole, which is shorter than its diff:
```python
import functools
import math

import jax
import jax.numpy as jnp
from jax import lax
from jax.experimental import pallas as pl
from jax.experimental.pallas import tpu as pltpu
from jax.sharding import PartitionSpec as P

LANES = 128
SUBLANES = 8
PAD = 8
REACH = 2
COLOR_UNIT = 4096.0
EXTINCTION_UNIT = 2048.0
VMEM_LIMIT = 12 * 2**20
FACES_LIMIT = 58 * 2**20

VMEM = pl.BlockSpec(memory_space=pltpu.VMEM)
HBM = pl.BlockSpec(memory_space=pltpu.HBM)


def lane_index():
    return lax.broadcasted_iota(jnp.int32, (SUBLANES, LANES), 1)


def is_odd(axis):
    return jnp.bitwise_and(lax.axis_index(axis), 1) == 1


def swaps(count):
    first = [(i, i ^ 1) for i in range(count)]
    second = [(i, i + 1 if i % 2 else i - 1) for i in range(1, count - 1)]
    return first, second


def faces_kernel(counts, order, density, colors, extinction, padded, y_out, xa, xb, za, zb, tables, flags, place, hues, thick, arrived):
    planes, rows, _ = density.shape
    parts = arrived.shape[0] - 3
    step = rows // parts
    copies = [
        pltpu.make_async_copy(
            density.at[:, pl.ds(k * step, step), :],
            padded.at[pl.ds(REACH, planes), pl.ds(PAD + k * step, step), :],
            arrived.at[k],
        )
        for k in range(parts)
    ]
    small = [
        pltpu.make_async_copy(source, target, arrived.at[parts + k])
        for k, (source, target) in enumerate(((order, place), (colors, hues), (extinction, thick)))
    ]
    for copy in copies + small:
        copy.start()
    slot = jnp.right_shift(lane_index(), 2)
    for k in range(parts):
        copies[k].wait()
        for tile in range(step // SUBLANES):
            row = k * step + tile * SUBLANES
            packed = jnp.zeros((SUBLANES, LANES), jnp.float32)
            for z in range(planes):
                plane = padded[REACH + z, PAD + row : PAD + row + SUBLANES, :]
                packed = jnp.where(slot == z, pltpu.roll(plane, (4 * z + REACH) % LANES, 1), packed)
            y_out[row : row + SUBLANES, :] = packed
    odd_x, odd_z = is_odd("bx"), is_odd("bz")
    low_x, high_x = PAD, PAD + rows - REACH
    low_z, high_z = REACH, planes
    for out, start in ((xa, jnp.where(odd_x, low_x, high_x)), (xb, jnp.where(odd_x, high_x, low_x))):
        for z in range(planes):
            out[REACH * z : REACH * (z + 1), :] = padded[REACH + z, pl.ds(start, REACH), :]
    for out, start in ((za, jnp.where(odd_z, low_z, high_z)), (zb, jnp.where(odd_z, high_z, low_z))):
        if out is zb and counts["bz"] == 2:
            continue
        for layer in range(REACH):
            out[layer] = padded[start + layer, PAD : PAD + rows, :]
    if counts["bz"] == 2:
        zb[...] = jnp.zeros(zb.shape, jnp.float32)
    for copy in small:
        copy.wait()
    slabs = counts["bz"]
    backward = (place[0, 0, 0] > place[0, 0, slabs - 1]).astype(jnp.float32)
    rank = jnp.bitwise_xor(lax.axis_index("bz"), place[0, 0, 0])
    flags[0] = jnp.full((SUBLANES, LANES), backward, jnp.float32)
    for bit in range(slabs.bit_length() - 1):
        behind = jnp.bitwise_and(jnp.right_shift(rank, bit), 1).astype(jnp.float32)
        flags[1 + bit] = jnp.full((SUBLANES, LANES), behind, jnp.float32)
    color = (hues[...].astype(jnp.float32) * COLOR_UNIT).astype(jnp.int32)
    dense = (thick[...].astype(jnp.float32) * EXTINCTION_UNIT).astype(jnp.int32)
    for k, table in enumerate((color[0:1] * 65536 + color[1:2], color[2:3] * 65536 + dense)):
        for part in range(2):
            tables[2 * k + part] = jnp.broadcast_to(
                table[:, part * LANES : (part + 1) * LANES], (SUBLANES, LANES)
            )


def faces(order, density, colors, extinction, counts):
    planes, rows, cols = density.shape
    shape = lambda *dims: jax.ShapeDtypeStruct(dims, jnp.float32)
    z_rows = rows if counts["bz"] > 2 else SUBLANES
    return pl.pallas_call(
        functools.partial(faces_kernel, counts),
        out_shape=(
            shape(planes + 2 * REACH, rows + 2 * PAD, cols),
            shape(rows, LANES),
            shape(REACH * planes, cols),
            shape(REACH * planes, cols),
            shape(REACH, rows, cols),
            shape(REACH, z_rows, cols),
            jax.ShapeDtypeStruct((4, SUBLANES, LANES), jnp.int32),
            shape(counts["bz"].bit_length(), SUBLANES, LANES),
        ),
        in_specs=[HBM] * 4,
        out_specs=(VMEM,) * 8,
        scratch_shapes=[
            pltpu.SMEM(order.shape, jnp.int32),
            pltpu.VMEM(colors.shape, colors.dtype),
            pltpu.VMEM(extinction.shape, extinction.dtype),
            pltpu.SemaphoreType.DMA((7,)),
        ],
        compiler_params=pltpu.CompilerParams(vmem_limit_bytes=FACES_LIMIT),
        name="faces",
    )(order, density, colors, extinction)


def local_kernel(total_planes, padded, material, tables, flags, lit, slope_y, through):
    planes, rows, _ = material.shape
    backward = jnp.max(flags[0]) > 0.5
    k = jnp.bitwise_and(lax.broadcasted_iota(jnp.int32, (2 * LANES, LANES), 0), LANES - 1)
    gap = k - lax.broadcasted_iota(jnp.int32, (2 * LANES, LANES), 1)
    band = jnp.where(gap == 1, 8.0, jnp.where(gap == -1, -8.0, 0.0))
    band = band + jnp.where(gap == 2, -1.0, jnp.where(gap == -2, 1.0, 0.0))
    band = band.astype(jnp.bfloat16)
    scale = -3.0 * math.log2(math.e) / (EXTINCTION_UNIT * total_planes)

    def take(first, low, upper):
        found = [
            jnp.take_along_axis(tables[first + k], low, axis=1, mode="promise_in_bounds")
            for k in range(2)
        ]
        return jnp.where(upper, found[1], found[0])

    def tile(index, carry):
        top = pl.multiple_of(index * 2 * SUBLANES, 2 * SUBLANES)
        coarse, fine = [], []
        for z in range(planes):
            plane = padded[REACH + z, pl.ds(PAD + top, 2 * SUBLANES), :]
            rounded = plane.astype(jnp.bfloat16)
            coarse.append(rounded)
            fine.append((plane - rounded.astype(jnp.float32)).astype(jnp.bfloat16))
        both = jnp.concatenate(
            [jnp.concatenate(coarse, axis=0), jnp.concatenate(fine, axis=0)], axis=1
        )
        slopes = jnp.dot(both, band, preferred_element_type=jnp.float32)
        for z in range(planes):
            slope_y[z, pl.ds(top, 2 * SUBLANES), :] = slopes[2 * SUBLANES * z : 2 * SUBLANES * (z + 1)]
        for part in range(2):
            row = pl.multiple_of(top + part * SUBLANES, SUBLANES)
            clear = jnp.ones((SUBLANES, LANES), jnp.float32)
            for visit in range(planes):
                z = jnp.where(backward, planes - 1 - visit, visit)
                density = padded[REACH + z, pl.ds(PAD + row, SUBLANES), :]
                label = material[z, pl.ds(row, SUBLANES), :]
                low = jnp.bitwise_and(label, LANES - 1)
                upper = label >= LANES
                rg = take(0, low, upper)
                be = take(2, low, upper)
                extinct = jnp.bitwise_and(be, 65535).astype(jnp.float32)
                after = clear * jnp.exp2(extinct * (density * scale))
                stopped = clear - after
                here = (z, pl.ds(row, SUBLANES), slice(None))
                lit[(0, *here)] = stopped * jnp.right_shift(rg, 16).astype(jnp.float32)
                lit[(1, *here)] = stopped * jnp.bitwise_and(rg, 65535).astype(jnp.float32)
                lit[(2, *here)] = stopped * jnp.right_shift(be, 16).astype(jnp.float32)
                clear = after
            through[pl.ds(row, SUBLANES), :] = clear
        return carry

    lax.fori_loop(0, rows // SUBLANES // 2, tile, 0)


def local(padded, material, tables, flags, total_planes):
    planes, rows, cols = material.shape
    shape = lambda *dims: jax.ShapeDtypeStruct(dims, jnp.float32)
    return pl.pallas_call(
        functools.partial(local_kernel, total_planes),
        out_shape=(shape(3, planes, rows, cols), shape(planes, rows, cols), shape(rows, cols)),
        in_specs=[VMEM] * 4,
        out_specs=(VMEM,) * 3,
        compiler_params=pltpu.CompilerParams(vmem_limit_bytes=VMEM_LIMIT),
        cost_estimate=pl.CostEstimate(
            flops=20 * planes * rows * cols,
            bytes_accessed=2**22,
            transcendentals=planes * rows * cols,
        ),
        name="local",
    )(padded, material, tables, flags)


def put_halo(padded, xa, xb, za, zb, ya, yb, edge, planes, rows):
    odd_x, odd_y, odd_z = is_odd("bx"), is_odd("by"), is_odd("bz")
    for z in range(planes):
        first, second = xa[REACH * z : REACH * (z + 1), :], xb[REACH * z : REACH * (z + 1), :]
        padded[REACH + z, PAD - REACH : PAD, :] = jnp.where(odd_x, first, second)
        padded[REACH + z, PAD + rows : PAD + rows + REACH, :] = jnp.where(odd_x, second, first)
    for layer in range(REACH):
        first = za[layer]
        second = zb[layer] if zb.shape == za.shape else jnp.zeros_like(first)
        padded[layer, PAD : PAD + rows, :] = jnp.where(odd_z, first, second)
        padded[REACH + planes + layer, PAD : PAD + rows, :] = jnp.where(odd_z, second, first)
    side = jnp.bitwise_and(lane_index(), 3)
    for row in range(0, rows, SUBLANES):
        first, second = ya[row : row + SUBLANES, :], yb[row : row + SUBLANES, :]
        near = jnp.where((side < 2) == odd_y, first, second)
        ahead1, ahead2 = pltpu.roll(near, LANES - 1, 1), pltpu.roll(near, LANES - 2, 1)
        behind1, behind2 = pltpu.roll(near, 1, 1), pltpu.roll(near, 2, 1)
        edge[row : row + SUBLANES, :] = jnp.where(
            side == 0,
            -ahead2,
            jnp.where(
                side == 1,
                8.0 * ahead1 - ahead2,
                jnp.where(side == 2, behind2 - 8.0 * behind1, behind2),
            ),
        )


def shade_half(padded, edge, lit, slope_y, through, out, giving):
    _, planes, rows, _ = lit.shape
    block_rows = rows // lax.axis_size("bz")
    half = jnp.bitwise_and(lax.axis_index("bz") + (1 if giving else 0), 1)
    lane = lane_index()
    at_edge = jnp.logical_or(lane < REACH, lane >= LANES - REACH)

    def pair(index, carry):
        for part in range(2):
            to = pl.multiple_of((2 * index + part) * SUBLANES, SUBLANES)
            group = lax.div(to, block_rows)
            row = pl.multiple_of((group + half) * block_rows + to, SUBLANES)
            beside = edge[pl.ds(row, SUBLANES), :]
            sums = [jnp.zeros((SUBLANES, LANES), jnp.float32) for _ in range(3)]
            for z in range(planes):
                at = lambda dz, dx: padded[REACH + z + dz, pl.ds(PAD + row + dx, SUBLANES), :]
                sz = 8.0 * (at(1, 0) - at(-1, 0)) - (at(2, 0) - at(-2, 0))
                sx = 8.0 * (at(0, 1) - at(0, -1)) - (at(0, 2) - at(0, -2))
                outer = pltpu.roll(beside, (-4 * z - REACH) % LANES, 1)
                sy = slope_y[z, pl.ds(row, SUBLANES), :] + jnp.where(at_edge, outer, 0.0)
                size = sx * sx + sy * sy + sz * sz
                facing = jnp.abs(0.432 * sx + 0.54 * sy + 0.576 * sz)
                shading = 0.1 + facing * lax.rsqrt(jnp.maximum(size, 36.0))
                for c in range(3):
                    sums[c] = sums[c] + shading * lit[c, z, pl.ds(row, SUBLANES), :]
            for c in range(3):
                out[c, pl.ds(to, SUBLANES), :] = sums[c] * (1.0 / COLOR_UNIT)
            out[3, pl.ds(to, SUBLANES), :] = through[pl.ds(row, SUBLANES), :]
        return carry

    lax.fori_loop(0, rows // 4 // SUBLANES, pair, 0)


def shade_give_kernel(padded_in, xa, xb, za, zb, ya, yb, lit, slope_y, through, padded, edge, give):
    _, planes, rows, _ = lit.shape
    del padded_in
    put_halo(padded, xa, xb, za, zb, ya, yb, edge, planes, rows)
    shade_half(padded, edge, lit, slope_y, through, give, True)


def shade_keep_kernel(padded, edge, lit, slope_y, through, keep):
    shade_half(padded, edge, lit, slope_y, through, keep, False)


def shade_give(padded, halos, lit, slope_y, through):
    _, _, rows, cols = lit.shape
    shape = lambda *dims: jax.ShapeDtypeStruct(dims, jnp.float32)
    return pl.pallas_call(
        shade_give_kernel,
        out_shape=(shape(*padded.shape), shape(rows, LANES), shape(4, rows // 2, cols)),
        in_specs=[VMEM] * 10,
        out_specs=(VMEM,) * 3,
        input_output_aliases={0: 0},
        compiler_params=pltpu.CompilerParams(vmem_limit_bytes=VMEM_LIMIT),
        name="shade_give",
    )(padded, *halos, lit, slope_y, through)


def shade_keep(padded, edge, lit, slope_y, through):
    _, planes, rows, cols = lit.shape
    return pl.pallas_call(
        shade_keep_kernel,
        out_shape=jax.ShapeDtypeStruct((4, rows // 2, cols), jnp.float32),
        in_specs=[VMEM] * 5,
        out_specs=VMEM,
        compiler_params=pltpu.CompilerParams(vmem_limit_bytes=VMEM_LIMIT),
        cost_estimate=pl.CostEstimate(
            flops=20 * planes * rows * cols, bytes_accessed=2**22, transcendentals=0
        ),
        name="shade_keep",
    )(padded, edge, lit, slope_y, through)


def blend_kernel(bit, last, flags, mine, other, out):
    clear_mine, clear_other = mine[3], other[3]
    behind = jnp.broadcast_to(flags[1 + bit, 0:1, :], clear_mine.shape) > 0.5
    clear = jnp.where(behind, clear_other, clear_mine)
    for c in range(3):
        front = jnp.where(behind, other[c], mine[c])
        back = jnp.where(behind, mine[c], other[c])
        out[c] = front + clear * back
    product = clear_mine * clear_other
    out[3] = 1.0 - product if last else product


def blend(flags, mine, other, bit, last):
    return pl.pallas_call(
        functools.partial(blend_kernel, bit, last),
        out_shape=jax.ShapeDtypeStruct(mine.shape, jnp.float32),
        in_specs=[VMEM] * 3,
        out_specs=VMEM,
        compiler_params=pltpu.CompilerParams(vmem_limit_bytes=VMEM_LIMIT),
        name="blend",
    )(flags, mine, other)


def shards(density, material, color_table, extinction_table, order):
    planes, rows, cols = density.shape
    counts = {axis: lax.axis_size(axis) for axis in ("bx", "by", "bz")}
    slabs = counts["bz"]
    padded, y_own, xa, xb, za, zb, tables, flags = faces(
        order, density, color_table, extinction_table, counts
    )
    pairs = {axis: swaps(counts[axis]) for axis in counts}
    xa = lax.ppermute(xa, "bx", pairs["bx"][0])
    xb = lax.ppermute(xb, "bx", pairs["bx"][1])
    za = lax.ppermute(za, "bz", pairs["bz"][0])
    if slabs > 2:
        zb = lax.ppermute(zb, "bz", pairs["bz"][1])
    ya = lax.ppermute(y_own, "by", pairs["by"][0])
    yb = lax.ppermute(y_own, "by", pairs["by"][1])
    lit, slope_y, through = local(padded, material, tables, flags, planes * slabs)
    halos = (xa, xb, za, zb, ya, yb)
    padded, edge, give = shade_give(padded, halos, lit, slope_y, through)
    keep = shade_keep(padded, edge, lit, slope_y, through)
    block_rows = rows // slabs
    levels = slabs.bit_length() - 1
    my_slab = lax.axis_index("bz")
    for bit in range(levels):
        flip = [(i, i ^ (1 << bit)) for i in range(slabs)]
        received = lax.ppermute(give, "bz", flip)
        holding = blend(flags, keep, received, bit, bit == levels - 1)
        if bit < levels - 1:
            paired = holding.reshape(4, -1, 2, block_rows, cols)
            half = jnp.bitwise_and(jnp.right_shift(my_slab, bit + 1), 1)
            take = lambda which: lax.dynamic_index_in_dim(paired, which, 2, keepdims=False)
            keep, give = (take(which).reshape(4, -1, cols) for which in (half, 1 - half))
    return holding


def solution(mesh):
    placed = (P("bz", "bx", "by"), P("bz", "bx", "by"), P(), P(), P("bx", "by", None))
    return jax.shard_map(
        shards, mesh=mesh, in_specs=placed, out_specs=P(None, ("bx", "bz"), "by"), check_vma=False
    )
```

time: 40.9 us -> 29.3 us (0.72)
  Pallas kernels: 20.4 us -> 11.9 us
  local copies, waits for them, and re-layouts: 5.15 us -> 3.17 us
  waiting for transfers between devices: 3.47 us -> 2.3 us
    pallas_call x1, Pallas kernels: 12.4 us -> 4.8 us  [local(): pl.pallas_call(functools.partial(local_kernel, total_planes), out_shape=(...]
    pallas_call x1 -> x2, Pallas kernels: 5.76 us -> 2.79 us  [the longest x1 1.48 us: shade_give(): pl.pallas_call(shade_give_kernel, out_shape=(shape(*padded.shape), shape(...]
    pallas_call x1, Pallas kernels: 1.03 us -> 3.68 us  [faces(): pl.pallas_call(functools.partial(faces_kernel, counts), out_shape=(shape(...]
    unnamed x12, local copies, waits for them, and re-layouts: 4.49 us -> 3.17 us
    ppermute x1, waiting for transfers between devices: 3.46 us -> 2.28 us  [shards(): received = lax.ppermute(give, 'bz', flip)]
    reshape x1 -> x0, local copies, waits for them, and re-layouts: 0.66 us -> none  [shards(): extinction_table.reshape(1, -1)]
    pallas_call x1, Pallas kernels: 1.22 us -> 0.67 us  [blend(): pl.pallas_call(functools.partial(blend_kernel, bit, last), out_shape=jax....]
  transfers between devices with their start and end apart: 6 -> 6, of which waited for: 1 -> 1; matrix products, arithmetic and copies ran while one was open for 2% -> 0% of each run, Pallas kernels for 30% -> 21%
where the time goes in v1:
time: 29.3 us; the launch traced here: 29 us
  Pallas kernels  11.9 us (41%)
  starting transfers between devices  11.5 us (39%)
  local copies, waits for them, and re-layouts  3.17 us (11%)
  waiting for transfers between devices  2.3 us (8%)
    pallas_call x1, Pallas kernels, local(): pl.pallas_call(functools.partial(local_kernel, total_planes), out_shape=(...  4.8 us
    ppermute x1, starting transfers between devices, shards(): ya = lax.ppermute(y_own, 'by', pairs['by'][0])  3.9 us
    pallas_call x1, Pallas kernels, faces(): pl.pallas_call(functools.partial(faces_kernel, counts), out_shape=(shape(...  3.68 us
    unnamed x12, local copies, waits for them, and re-layouts  3.17 us
    ppermute x1, starting transfers between devices, shards(): xb = lax.ppermute(xb, 'bx', pairs['bx'][1])  3 us
    ppermute x1, waiting for transfers between devices, shards(): received = lax.ppermute(give, 'bz', flip)  2.28 us
    ppermute x1, starting transfers between devices, shards(): za = lax.ppermute(za, 'bz', pairs['bz'][0])  2.13 us
    ppermute x1, starting transfers between devices, shards(): xa = lax.ppermute(xa, 'bx', pairs['bx'][0])  1.52 us
  transfers between devices with their start and end apart: 6, of which 1 were waited for; matrix products, arithmetic and copies ran while one was open for 0% of the time, Pallas kernels for 21%

profile of v1, /device:TPU:1, one launch (start us, length us, event | category | flops | bytes accessed | tf_op | source)
XLA Modules:
  0.0 29.0 jit_solution(3218447970801049751)
XLA Ops:
  0.0 0.0 copy-start.1
  0.0 3.7 %faces.1 = (f32[36,144,128]{2,1,0:T(8,128)}, f32[128,128]{1,0:T(8,128)}, f32[64,128]{1,0:T(8,128)}, f32[64,128]{1,0:T(8,128)}, f32[2,128,128]{2,1,0:T(8,128)}, /...) custom-call(s32[1,1,2]{2,1,0:T(1,128)} %order.1, f32[32,128,128]{2,1,0:T(8,128)} %density.1, ...), custom_call_target="tpu_custom_call" | custom-call | tf_op jit(solution)/shard_map/faces/pallas_call | solution.py:101
  3.7 0.0 copy-start.5
  3.7 2.1 %collective-permute-start.2 = (f32[2,128,128]{2,1,0:T(8,128)}, f32[2,128,128]{2,1,0:T(8,128)S(1)}, u32[]{:S(2)}, u32[]{:S(2)}) collective-permute-start(f32[2,128,128]{2,1,0:T(8,128)} %get-tuple-element.23), channel_id=1, source_target_pairs={{0,1},{1,0},{2,3},{3,2},{4,5},{5,4},{6,7},{7,6},{8,9},{9,8},{10,11... | collective-permute-start | bytes 393224 | tf_op jit(solution)/shard_map/ppermute | solution.py:334
  5.8 0.7 %collective-permute-start.4 = (f32[128,128]{1,0:T(8,128)}, f32[128,128]{1,0:T(8,128)S(1)}, u32[]{:S(2)}, u32[]{:S(2)}) collective-permute-start(f32[128,128]{1,0:T(8,128)} %get-tuple-element.25), channel_id=1, source_target_pairs={{2,4},{4,2},{3,5},{5,3},{10,12},{12,10},{11,13},{13,11},{18,20},{2... | collective-permute-start | bytes 196616 | tf_op jit(solution)/shard_map/ppermute | solution.py:338
  6.5 3.9 %collective-permute-start.3 = (f32[128,128]{1,0:T(8,128)}, f32[128,128]{1,0:T(8,128)S(1)}, u32[]{:S(2)}, u32[]{:S(2)}) collective-permute-start(f32[128,128]{1,0:T(8,128)} %get-tuple-element.25), channel_id=1, source_target_pairs={{0,2},{2,0},{4,6},{6,4},{1,3},{3,1},{5,7},{7,5},{8,10},{10,8},{12,... | collective-permute-start | bytes 196616 | tf_op jit(solution)/shard_map/ppermute | solution.py:337
  10.4 1.5 %collective-permute-start = (f32[64,128]{1,0:T(8,128)}, f32[64,128]{1,0:T(8,128)S(1)}, u32[]{:S(2)}, u32[]{:S(2)}) collective-permute-start(f32[64,128]{1,0:T(8,128)} %get-tuple-element.21), channel_id=1, source_target_pairs={{0,8},{8,0},{16,24},{24,16},{1,9},{9,1},{17,25},{25,17},{2,10},{10... | collective-permute-start | bytes 98312 | tf_op jit(solution)/shard_map/ppermute | solution.py:332
  11.9 3.0 %collective-permute-start.1 = (f32[64,128]{1,0:T(8,128)}, f32[64,128]{1,0:T(8,128)S(1)}, u32[]{:S(2)}, u32[]{:S(2)}) collective-permute-start(f32[64,128]{1,0:T(8,128)} %get-tuple-element.22), channel_id=1, source_target_pairs={{8,16},{16,8},{9,17},{17,9},{10,18},{18,10},{11,19},{19,11},{12,20... | collective-permute-start | bytes 98312 | tf_op jit(solution)/shard_map/ppermute | solution.py:333
  14.9 0.0 copy-done.1
  14.9 0.0 copy-start
  14.9 1.7 %copy-done = f32[36,144,128]{2,1,0:T(8,128)S(1)} copy-done((f32[36,144,128]{2,1,0:T(8,128)S(1)}, f32[36,144,128]{2,1,0:T(8,128)}, u32[]{:S(2)}) %copy-start) | copy-done | bytes 2654232
  16.7 0.0 copy-start.2
  16.7 0.7 %copy-done.2 = f32[2,8,128]{2,1,0:T(8,128)S(1)} copy-done((f32[2,8,128]{2,1,0:T(8,128)S(1)}, f32[2,8,128]{2,1,0:T(8,128)}, u32[]{:S(2)}) %copy-start.2) | copy-done | bytes 8216
  17.4 0.0 copy-start.4
  17.4 0.7 %copy-done.4 = s32[4,8,128]{2,1,0:T(8,128)S(1)} copy-done((s32[4,8,128]{2,1,0:T(8,128)S(1)}, s32[4,8,128]{2,1,0:T(8,128)}, u32[]{:S(2)}) %copy-start.4) | copy-done | bytes 16408
  18.1 4.8 %local.1 = (f32[3,32,128,128]{3,2,1,0:T(8,128)S(1)}, f32[32,128,128]{2,1,0:T(8,128)S(1)}, f32[128,128]{1,0:T(8,128)S(1)}) custom-call(f32[36,144,128]{2,1,0:T(8,128)S(1)} %copy-done, s32[32,128,128]{2,1,0:T(8,128)S(1)} %copy-done.1, s32[4,8,128]{2,1,0:T(8,128)S(1)} %copy-done.4, f32[2,8,128]{2,1,0:T(8,128)S(1)} %copy-done.2), custom_call_target="tpu_custom_call" | custom-call | flops 10485760 | bytes 4194304 | tf_op jit(solution)/shard_map/local/pallas_call | solution.py:185
  22.9 0.0 collective-permute-done.xa
  22.9 0.0 collective-permute-done.1.xb
  22.9 0.0 collective-permute-done.4.yb
  22.9 0.0 collective-permute-done.3.ya
  22.9 0.0 collective-permute-done.2.za
  22.9 0.0 copy-done.5
  23.0 1.5 %shade_give.1 = (f32[36,144,128]{2,1,0:T(8,128)S(1)}, f32[128,128]{1,0:T(8,128)S(1)}, f32[4,64,128]{2,1,0:T(8,128)S(1)}) custom-call(f32[36,144,128]{2,1,0:T(8,128)S(1)} %copy-done, f32[64,128]{1,0:T(8,128)S(1)} %collective-permute-done.xa, f32[64,128]{1,0:T(8,128)S(1)} %collective-permute-done.1.xb, ...), custom_call_target="tpu_custom_call", output_to_operand_aliasing={{0}: (0, {})} | custom-call | tf_op jit(solution)/shard_map/shade_give/pallas_call | solution.py:275
  24.4 0.3 collective-permute-start.5
  24.7 0.0 copy-start.3
  24.7 1.3 %shade_keep.1.mine = f32[4,64,128]{2,1,0:T(8,128)S(1)} custom-call(f32[36,144,128]{2,1,0:T(8,128)S(1)} %get-tuple-element.30.padded, f32[128,128]{1,0:T(8,128)S(1)} %get-tuple-element.31.edge, f32[3,32,128,128]{3,2,1,0:T(8,128)S(1)} %get-tuple-element.27.lit, f32[32,128,128]{2,1,0:T(8,128)S(1)} %get-tuple-element.28.slope_y, ...), custom_call_target="tpu_custom_call" | custom-call | flops 10485760 | bytes 4194304 | tf_op jit(solution)/shard_map/shade_keep/pallas_call | solution.py:288
  26.0 2.3 %collective-permute-done.5.other = f32[4,64,128]{2,1,0:T(8,128)S(1)} collective-permute-done((f32[4,64,128]{2,1,0:T(8,128)S(1)}, f32[4,64,128]{2,1,0:T(8,128)S(1)}, u32[]{:S(2)}, u32[]{:S(2)}) %collective-permute-start.5) | collective-permute-done | bytes 131104 | tf_op jit(solution)/shard_map/ppermute | solution.py:348
  28.3 0.0 copy-done.3
  28.3 0.7 %blend.1 = f32[4,64,128]{2,1,0:T(8,128)} custom-call(f32[2,8,128]{2,1,0:T(8,128)S(1)} %copy-done.3, f32[4,64,128]{2,1,0:T(8,128)S(1)} %shade_keep.1.mine, f32[4,64,128]{2,1,0:T(8,128)S(1)} %collective-permute-done.5.other), custom_call_target="tpu_custom_call" | custom-call | tf_op jit(solution)/shard_map/blend/pallas_call | solution.py:314
Async XLA Ops:
  0.0 14.9 %copy-start.1 = (s32[32,128,128]{2,1,0:T(8,128)S(1)}, s32[32,128,128]{2,1,0:T(8,128)}, u32[]{:S(2)}) copy-start(s32[32,128,128]{2,1,0:T(8,128)} %material.1) | copy-start | bytes 6291460
  3.7 19.3 %copy-start.5 = (f32[2,8,128]{2,1,0:T(8,128)S(1)}, f32[2,8,128]{2,1,0:T(8,128)}, u32[]{:S(2)}) copy-start(f32[2,8,128]{2,1,0:T(8,128)} %get-tuple-element.24.zb) | copy-start | bytes 24580
  3.7 19.2 %collective-permute-start.2 = (f32[2,128,128]{2,1,0:T(8,128)}, f32[2,128,128]{2,1,0:T(8,128)S(1)}, u32[]{:S(2)}, u32[]{:S(2)}) collective-permute-start(f32[2,128,128]{2,1,0:T(8,128)} %get-tuple-element.23), channel_id=1, source_target_pairs={{0,1},{1,0},{2,3},{3,2},{4,5},{5,4},{6,7},{7,6},{8,9},{9,8},{10,11... | collective-permute-start | bytes 393224 | tf_op jit(solution)/shard_map/ppermute | solution.py:334
  5.8 17.1 %collective-permute-start.4 = (f32[128,128]{1,0:T(8,128)}, f32[128,128]{1,0:T(8,128)S(1)}, u32[]{:S(2)}, u32[]{:S(2)}) collective-permute-start(f32[128,128]{1,0:T(8,128)} %get-tuple-element.25), channel_id=1, source_target_pairs={{2,4},{4,2},{3,5},{5,3},{10,12},{12,10},{11,13},{13,11},{18,20},{2... | collective-permute-start | bytes 196616 | tf_op jit(solution)/shard_map/ppermute | solution.py:338
  6.5 16.4 %collective-permute-start.3 = (f32[128,128]{1,0:T(8,128)}, f32[128,128]{1,0:T(8,128)S(1)}, u32[]{:S(2)}, u32[]{:S(2)}) collective-permute-start(f32[128,128]{1,0:T(8,128)} %get-tuple-element.25), channel_id=1, source_target_pairs={{0,2},{2,0},{4,6},{6,4},{1,3},{3,1},{5,7},{7,5},{8,10},{10,8},{12,... | collective-permute-start | bytes 196616 | tf_op jit(solution)/shard_map/ppermute | solution.py:337
  10.4 12.5 %collective-permute-start = (f32[64,128]{1,0:T(8,128)}, f32[64,128]{1,0:T(8,128)S(1)}, u32[]{:S(2)}, u32[]{:S(2)}) collective-permute-start(f32[64,128]{1,0:T(8,128)} %get-tuple-element.21), channel_id=1, source_target_pairs={{0,8},{8,0},{16,24},{24,16},{1,9},{9,1},{17,25},{25,17},{2,10},{10... | collective-permute-start | bytes 98312 | tf_op jit(solution)/shard_map/ppermute | solution.py:332
  11.9 11.0 %collective-permute-start.1 = (f32[64,128]{1,0:T(8,128)}, f32[64,128]{1,0:T(8,128)S(1)}, u32[]{:S(2)}, u32[]{:S(2)}) collective-permute-start(f32[64,128]{1,0:T(8,128)} %get-tuple-element.22), channel_id=1, source_target_pairs={{8,16},{16,8},{9,17},{17,9},{10,18},{18,10},{11,19},{19,11},{12,20... | collective-permute-start | bytes 98312 | tf_op jit(solution)/shard_map/ppermute | solution.py:333
  14.9 1.8 %copy-start = (f32[36,144,128]{2,1,0:T(8,128)S(1)}, f32[36,144,128]{2,1,0:T(8,128)}, u32[]{:S(2)}) copy-start(f32[36,144,128]{2,1,0:T(8,128)} %get-tuple-element.20.padded.padded_in) | copy-start | bytes 7962628
  16.7 0.7 %copy-start.2 = (f32[2,8,128]{2,1,0:T(8,128)S(1)}, f32[2,8,128]{2,1,0:T(8,128)}, u32[]{:S(2)}) copy-start(f32[2,8,128]{2,1,0:T(8,128)} %get-tuple-element.19.flags) | copy-start | bytes 24580
  17.4 0.7 %copy-start.4 = (s32[4,8,128]{2,1,0:T(8,128)S(1)}, s32[4,8,128]{2,1,0:T(8,128)}, u32[]{:S(2)}) copy-start(s32[4,8,128]{2,1,0:T(8,128)} %get-tuple-element.26.tables) | copy-start | bytes 49156
  24.4 3.9 %collective-permute-start.5 = (f32[4,64,128]{2,1,0:T(8,128)S(1)}, f32[4,64,128]{2,1,0:T(8,128)S(1)}, u32[]{:S(2)}, u32[]{:S(2)}) collective-permute-start(f32[4,64,128]{2,1,0:T(8,128)S(1)} %get-tuple-element.32), channel_id=1, source_target_pairs={{0,1},{1,0},{2,3},{3,2},{4,5},{5,4},{6,7},{7,6},{8,9},{9,8},{10,11... | collective-permute-start | bytes 393224 | tf_op jit(solution)/shard_map/ppermute | solution.py:348
  24.7 3.6 %copy-start.3 = (f32[2,8,128]{2,1,0:T(8,128)S(1)}, f32[2,8,128]{2,1,0:T(8,128)}, u32[]{:S(2)}) copy-start(f32[2,8,128]{2,1,0:T(8,128)} %get-tuple-element.19.flags) | copy-start | bytes 24580

commit v2 on v1

--- a/solution.py
+++ b/solution.py
@@ -15,7 +15,6 @@
 COLOR_UNIT = 4096.0
 EXTINCTION_UNIT = 2048.0
 VMEM_LIMIT = 12 * 2**20
-FACES_LIMIT = 58 * 2**20
 
 VMEM = pl.BlockSpec(memory_space=pltpu.VMEM)
 HBM = pl.BlockSpec(memory_space=pltpu.HBM)
@@ -96,7 +95,7 @@
 
 def faces(order, density, colors, extinction, counts):
     planes, rows, cols = density.shape
-    shape = lambda *dims: jax.ShapeDtypeStruct(dims, jnp.float32)
+    shape = lambda *dims: pltpu.VMEM(dims, jnp.float32)
     z_rows = rows if counts["bz"] > 2 else SUBLANES
     return pl.pallas_call(
         functools.partial(faces_kernel, counts),
@@ -107,7 +106,7 @@
             shape(REACH * planes, cols),
             shape(REACH, rows, cols),
             shape(REACH, z_rows, cols),
-            jax.ShapeDtypeStruct((4, SUBLANES, LANES), jnp.int32),
+            pltpu.VMEM((4, SUBLANES, LANES), jnp.int32),
             shape(counts["bz"].bit_length(), SUBLANES, LANES),
         ),
         in_specs=[HBM] * 4,
@@ -118,9 +117,9 @@
             pltpu.VMEM(extinction.shape, extinction.dtype),
             pltpu.SemaphoreType.DMA((7,)),
         ],
-        compiler_params=pltpu.CompilerParams(vmem_limit_bytes=FACES_LIMIT),
+        compiler_params=pltpu.CompilerParams(vmem_limit_bytes=VMEM_LIMIT),
         name="faces",
-    )(order, density, colors, extinction)
+    )(*(pltpu.with_memory_space_constraint(a, pltpu.HBM) for a in (order, density, colors, extinction)))
 
 
 def local_kernel(total_planes, padded, material, tables, flags, lit, slope_y, through):

time: 29.3 us -> 24.4 us (0.83)
  local copies, waits for them, and re-layouts: 3.17 us -> 0.01 us
  Pallas kernels: 11.9 us -> 10.3 us
    unnamed x12 -> x2, local copies, waits for them, and re-layouts: 3.17 us -> 0.01 us
    pallas_call x1, Pallas kernels: 3.68 us -> 2.11 us  [faces(): pl.pallas_call(functools.partial(faces_kernel, counts), out_shape=(shape(...]
  transfers between devices with their start and end apart: 6 -> 6, of which waited for: 1 -> 1; matrix products, arithmetic and copies ran while one was open for 0% -> 0% of each run, Pallas kernels for 21% -> 25%
where the time goes in v2:
time: 24.4 us; the launch traced here: 24.2 us
  starting transfers between devices  11.5 us (47%)
  Pallas kernels  10.3 us (42%)
  waiting for transfers between devices  2.34 us (10%)
    pallas_call x1, Pallas kernels, local(): pl.pallas_call(functools.partial(local_kernel, total_planes), out_shape=(...  4.8 us
    ppermute x1, starting transfers between devices, shards(): ya = lax.ppermute(y_own, 'by', pairs['by'][0])  3.9 us
    ppermute x1, starting transfers between devices, shards(): xb = lax.ppermute(xb, 'bx', pairs['bx'][1])  3 us
    ppermute x1, waiting for transfers between devices, shards(): received = lax.ppermute(give, 'bz', flip)  2.33 us
    ppermute x1, starting transfers between devices, shards(): za = lax.ppermute(za, 'bz', pairs['bz'][0])  2.13 us
    pallas_call x1, Pallas kernels, faces(): pl.pallas_call(functools.partial(faces_kernel, counts), out_shape=(shape(...  2.11 us
    ppermute x1, starting transfers between devices, shards(): xa = lax.ppermute(xa, 'bx', pairs['bx'][0])  1.52 us
    pallas_call x1, Pallas kernels, shade_give(): pl.pallas_call(shade_give_kernel, out_shape=(shape(*padded.shape), shape(...  1.42 us
  transfers between devices with their start and end apart: 6, of which 1 were waited for; matrix products, arithmetic and copies ran while one was open for 0% of the time, Pallas kernels for 25%

profile of v2, /device:TPU:1, one launch (start us, length us, event | category | flops | bytes accessed | tf_op | source)
XLA Modules:
  0.0 24.2 jit_solution(13003570197610525203)
XLA Ops:
  0.0 0.0 copy-start
  0.0 2.1 %faces.1 = (f32[36,144,128]{2,1,0:T(8,128)S(1)}, f32[128,128]{1,0:T(8,128)S(1)}, f32[64,128]{1,0:T(8,128)S(1)}, f32[64,128]{1,0:T(8,128)S(1)}, f32[2,128,128]{2,...) custom-call(s32[1,1,2]{2,1,0:T(1,128)} %order.1, ...), custom_call_target="tpu_custom_call" | custom-call | tf_op jit(solution)/shard_map/faces/pallas_call | solution.py:100
  2.1 2.1 %collective-permute-start.2 = (f32[2,128,128]{2,1,0:T(8,128)S(1)}, f32[2,128,128]{2,1,0:T(8,128)S(1)}, u32[]{:S(2)}, u32[]{:S(2)}) collective-permute-start(f32[2,128,128]{2,1,0:T(8,128)S(1)} %get-tuple-element.23), channel_id=1, source_target_pairs={{0,1},{1,0},{2,3},{3,2},{4,5},{5,4},{6,7},{7,6},{8,9},{9,8},{10,11... | collective-permute-start | bytes 393224 | tf_op jit(solution)/shard_map/ppermute | solution.py:333
  4.3 0.7 %collective-permute-start.4 = (f32[128,128]{1,0:T(8,128)S(1)}, f32[128,128]{1,0:T(8,128)S(1)}, u32[]{:S(2)}, u32[]{:S(2)}) collective-permute-start(f32[128,128]{1,0:T(8,128)S(1)} %get-tuple-element.25), channel_id=1, source_target_pairs={{2,4},{4,2},{3,5},{5,3},{10,12},{12,10},{11,13},{13,11},{18,20},{2... | collective-permute-start | bytes 196616 | tf_op jit(solution)/shard_map/ppermute | solution.py:337
  4.9 3.9 %collective-permute-start.3 = (f32[128,128]{1,0:T(8,128)S(1)}, f32[128,128]{1,0:T(8,128)S(1)}, u32[]{:S(2)}, u32[]{:S(2)}) collective-permute-start(f32[128,128]{1,0:T(8,128)S(1)} %get-tuple-element.25), channel_id=1, source_target_pairs={{0,2},{2,0},{4,6},{6,4},{1,3},{3,1},{5,7},{7,5},{8,10},{10,8},{12,... | collective-permute-start | bytes 196616 | tf_op jit(solution)/shard_map/ppermute | solution.py:336
  8.8 1.5 %collective-permute-start = (f32[64,128]{1,0:T(8,128)S(1)}, f32[64,128]{1,0:T(8,128)S(1)}, u32[]{:S(2)}, u32[]{:S(2)}) collective-permute-start(f32[64,128]{1,0:T(8,128)S(1)} %get-tuple-element.21), channel_id=1, source_target_pairs={{0,8},{8,0},{16,24},{24,16},{1,9},{9,1},{17,25},{25,17},{2,10},{10... | collective-permute-start | bytes 98312 | tf_op jit(solution)/shard_map/ppermute | solution.py:331
  10.3 3.0 %collective-permute-start.1 = (f32[64,128]{1,0:T(8,128)S(1)}, f32[64,128]{1,0:T(8,128)S(1)}, u32[]{:S(2)}, u32[]{:S(2)}) collective-permute-start(f32[64,128]{1,0:T(8,128)S(1)} %get-tuple-element.22), channel_id=1, source_target_pairs={{8,16},{16,8},{9,17},{17,9},{10,18},{18,10},{11,19},{19,11},{12,20... | collective-permute-start | bytes 98312 | tf_op jit(solution)/shard_map/ppermute | solution.py:332
  13.3 0.0 copy-done
  13.3 4.8 %local.1 = (f32[3,32,128,128]{3,2,1,0:T(8,128)S(1)}, f32[32,128,128]{2,1,0:T(8,128)S(1)}, f32[128,128]{1,0:T(8,128)S(1)}) custom-call(f32[36,144,128]{2,1,0:T(8,128)S(1)} %get-tuple-element.20.padded.padded_in, s32[32,128,128]{2,1,0:T(8,128)S(1)} %copy-done, s32[4,8,128]{2,1,0:T(8,128)S(1)} %get-tuple-element.26.tables, f32[2,8,128]{2,1,0:T(8,128)S(1)} %get-tuple-element.19.flags), custom_call_target="tpu_custom_call" | custom-call | flops 10485760 | bytes 4194304 | tf_op jit(solution)/shard_map/local/pallas_call | solution.py:184
  18.2 0.0 collective-permute-done.xa
  18.2 0.0 collective-permute-done.1.xb
  18.2 0.0 collective-permute-done.4.yb
  18.2 0.0 collective-permute-done.3.ya
  18.2 0.0 collective-permute-done.2.za
  18.2 1.4 %shade_give.1 = (f32[36,144,128]{2,1,0:T(8,128)S(1)}, f32[128,128]{1,0:T(8,128)S(1)}, f32[4,64,128]{2,1,0:T(8,128)S(1)}) custom-call(f32[36,144,128]{2,1,0:T(8,128)S(1)} %get-tuple-element.20.padded.padded_in, f32[64,128]{1,0:T(8,128)S(1)} %collective-permute-done.xa, f32[64,128]{1,0:T(8,128)S(1)} %collective-permute-done.1.xb, ...), custom_call_target="tpu_custom_call", output_to_operand_aliasing={{0}: (0, {})} | custom-call | tf_op jit(solution)/shard_map/shade_give/pallas_call | solution.py:274
  19.6 0.3 %collective-permute-start.5 = (f32[4,64,128]{2,1,0:T(8,128)S(1)}, f32[4,64,128]{2,1,0:T(8,128)S(1)}, u32[]{:S(2)}, u32[]{:S(2)}) collective-permute-start(f32[4,64,128]{2,1,0:T(8,128)S(1)} %get-tuple-element.32), channel_id=1, source_target_pairs={{0,1},{1,0},{2,3},{3,2},{4,5},{5,4},{6,7},{7,6},{8,9},{9,8},{10,11... | collective-permute-start | bytes 393224 | tf_op jit(solution)/shard_map/ppermute | solution.py:347
  19.9 1.3 %shade_keep.1.mine = f32[4,64,128]{2,1,0:T(8,128)S(1)} custom-call(f32[36,144,128]{2,1,0:T(8,128)S(1)} %get-tuple-element.30.padded, f32[128,128]{1,0:T(8,128)S(1)} %get-tuple-element.31.edge, f32[3,32,128,128]{3,2,1,0:T(8,128)S(1)} %get-tuple-element.27.lit, f32[32,128,128]{2,1,0:T(8,128)S(1)} %get-tuple-element.28.slope_y, ...), custom_call_target="tpu_custom_call" | custom-call | flops 10485760 | bytes 4194304 | tf_op jit(solution)/shard_map/shade_keep/pallas_call | solution.py:287
  21.2 2.3 %collective-permute-done.5.other = f32[4,64,128]{2,1,0:T(8,128)S(1)} collective-permute-done((f32[4,64,128]{2,1,0:T(8,128)S(1)}, f32[4,64,128]{2,1,0:T(8,128)S(1)}, u32[]{:S(2)}, u32[]{:S(2)}) %collective-permute-start.5) | collective-permute-done | bytes 131104 | tf_op jit(solution)/shard_map/ppermute | solution.py:347
  23.5 0.7 %blend.1 = f32[4,64,128]{2,1,0:T(8,128)} custom-call(f32[2,8,128]{2,1,0:T(8,128)S(1)} %get-tuple-element.19.flags, f32[4,64,128]{2,1,0:T(8,128)S(1)} %shade_keep.1.mine, f32[4,64,128]{2,1,0:T(8,128)S(1)} %collective-permute-done.5.other), custom_call_target="tpu_custom_call" | custom-call | tf_op jit(solution)/shard_map/blend/pallas_call | solution.py:313
Async XLA Ops:
  0.0 13.3 %copy-start = (s32[32,128,128]{2,1,0:T(8,128)S(1)}, s32[32,128,128]{2,1,0:T(8,128)}, u32[]{:S(2)}) copy-start(s32[32,128,128]{2,1,0:T(8,128)} %material.1) | copy-start | bytes 6291460
  2.1 16.1 %collective-permute-start.2 = (f32[2,128,128]{2,1,0:T(8,128)S(1)}, f32[2,128,128]{2,1,0:T(8,128)S(1)}, u32[]{:S(2)}, u32[]{:S(2)}) collective-permute-start(f32[2,128,128]{2,1,0:T(8,128)S(1)} %get-tuple-element.23), channel_id=1, source_target_pairs={{0,1},{1,0},{2,3},{3,2},{4,5},{5,4},{6,7},{7,6},{8,9},{9,8},{10,11... | collective-permute-start | bytes 393224 | tf_op jit(solution)/shard_map/ppermute | solution.py:333
  4.3 13.9 %collective-permute-start.4 = (f32[128,128]{1,0:T(8,128)S(1)}, f32[128,128]{1,0:T(8,128)S(1)}, u32[]{:S(2)}, u32[]{:S(2)}) collective-permute-start(f32[128,128]{1,0:T(8,128)S(1)} %get-tuple-element.25), channel_id=1, source_target_pairs={{2,4},{4,2},{3,5},{5,3},{10,12},{12,10},{11,13},{13,11},{18,20},{2... | collective-permute-start | bytes 196616 | tf_op jit(solution)/shard_map/ppermute | solution.py:337
  4.9 13.3 %collective-permute-start.3 = (f32[128,128]{1,0:T(8,128)S(1)}, f32[128,128]{1,0:T(8,128)S(1)}, u32[]{:S(2)}, u32[]{:S(2)}) collective-permute-start(f32[128,128]{1,0:T(8,128)S(1)} %get-tuple-element.25), channel_id=1, source_target_pairs={{0,2},{2,0},{4,6},{6,4},{1,3},{3,1},{5,7},{7,5},{8,10},{10,8},{12,... | collective-permute-start | bytes 196616 | tf_op jit(solution)/shard_map/ppermute | solution.py:336
  8.8 9.3 %collective-permute-start = (f32[64,128]{1,0:T(8,128)S(1)}, f32[64,128]{1,0:T(8,128)S(1)}, u32[]{:S(2)}, u32[]{:S(2)}) collective-permute-start(f32[64,128]{1,0:T(8,128)S(1)} %get-tuple-element.21), channel_id=1, source_target_pairs={{0,8},{8,0},{16,24},{24,16},{1,9},{9,1},{17,25},{25,17},{2,10},{10... | collective-permute-start | bytes 98312 | tf_op jit(solution)/shard_map/ppermute | solution.py:331
  10.3 7.8 %collective-permute-start.1 = (f32[64,128]{1,0:T(8,128)S(1)}, f32[64,128]{1,0:T(8,128)S(1)}, u32[]{:S(2)}, u32[]{:S(2)}) collective-permute-start(f32[64,128]{1,0:T(8,128)S(1)} %get-tuple-element.22), channel_id=1, source_target_pairs={{8,16},{16,8},{9,17},{17,9},{10,18},{18,10},{11,19},{19,11},{12,20... | collective-permute-start | bytes 98312 | tf_op jit(solution)/shard_map/ppermute | solution.py:332
  19.6 3.9 %collective-permute-start.5 = (f32[4,64,128]{2,1,0:T(8,128)S(1)}, f32[4,64,128]{2,1,0:T(8,128)S(1)}, u32[]{:S(2)}, u32[]{:S(2)}) collective-permute-start(f32[4,64,128]{2,1,0:T(8,128)S(1)} %get-tuple-element.32), channel_id=1, source_target_pairs={{0,1},{1,0},{2,3},{3,2},{4,5},{5,4},{6,7},{7,6},{8,9},{9,8},{10,11... | collective-permute-start | bytes 393224 | tf_op jit(solution)/shard_map/ppermute | solution.py:347

commit v3 on v2

--- a/solution.py
+++ b/solution.py
@@ -10,6 +10,7 @@
 
 LANES = 128
 SUBLANES = 8
+TILE = 16
 PAD = 8
 REACH = 2
 COLOR_UNIT = 4096.0
@@ -122,68 +123,109 @@
     )(*(pltpu.with_memory_space_constraint(a, pltpu.HBM) for a in (order, density, colors, extinction)))
 
 
-def local_kernel(total_planes, padded, material, tables, flags, lit, slope_y, through):
-    planes, rows, _ = material.shape
-    backward = jnp.max(flags[0]) > 0.5
+def half_rows(tile_rows, index, rows, giving):
+    block_rows = rows // lax.axis_size("bz")
+    half = jnp.bitwise_and(lax.axis_index("bz") + (1 if giving else 0), 1)
+    to = pl.multiple_of(index * tile_rows, tile_rows)
+    row = (lax.div(to, block_rows) + half) * block_rows + to
+    return to, pl.multiple_of(row, tile_rows)
+
+
+def band_matrix():
     k = jnp.bitwise_and(lax.broadcasted_iota(jnp.int32, (2 * LANES, LANES), 0), LANES - 1)
     gap = k - lax.broadcasted_iota(jnp.int32, (2 * LANES, LANES), 1)
     band = jnp.where(gap == 1, 8.0, jnp.where(gap == -1, -8.0, 0.0))
     band = band + jnp.where(gap == 2, -1.0, jnp.where(gap == -2, 1.0, 0.0))
-    band = band.astype(jnp.bfloat16)
-    scale = -3.0 * math.log2(math.e) / (EXTINCTION_UNIT * total_planes)
-
-    def take(first, low, upper):
-        found = [
-            jnp.take_along_axis(tables[first + k], low, axis=1, mode="promise_in_bounds")
-            for k in range(2)
-        ]
-        return jnp.where(upper, found[1], found[0])
+    return band.astype(jnp.bfloat16)
+
+
+def slopes_along_y(padded, band, row, planes):
+    coarse, fine = [], []
+    for z in range(planes):
+        plane = padded[REACH + z, pl.ds(PAD + row, TILE), :]
+        rounded = plane.astype(jnp.bfloat16)
+        coarse.append(rounded)
+        fine.append((plane - rounded.astype(jnp.float32)).astype(jnp.bfloat16))
+    both = jnp.concatenate([jnp.concatenate(coarse, axis=0), jnp.concatenate(fine, axis=0)], axis=1)
+    return jnp.dot(both, band, preferred_element_type=jnp.float32)
+
+
+def take(tables, first, low, upper):
+    found = [
+        jnp.take_along_axis(tables[first + k], low, axis=1, mode="promise_in_bounds")
+        for k in range(2)
+    ]
+    return jnp.where(upper, found[1], found[0])
+
+
+def absorb(padded, material, tables, z, row, clear, scale):
+    density = padded[REACH + z, pl.ds(PAD + row, SUBLANES), :]
+    label = material[z, pl.ds(row, SUBLANES), :]
+    low = jnp.bitwise_and(label, LANES - 1)
+    upper = label >= LANES
+    rg = take(tables, 0, low, upper)
+    be = take(tables, 2, low, upper)
+    extinct = jnp.bitwise_and(be, 65535).astype(jnp.float32)
+    after = clear * jnp.exp2(extinct * (density * scale))
+    stopped = clear - after
+    whole = (jnp.right_shift(rg, 16), jnp.bitwise_and(rg, 65535), jnp.right_shift(be, 16))
+    return [stopped * part.astype(jnp.float32) for part in whole], after
+
+
+def shading_at(padded, slope_y, beside, at_edge, z, row):
+    at = lambda dz, dx: padded[REACH + z + dz, pl.ds(PAD + row + dx, SUBLANES), :]
+    sz = 8.0 * (at(1, 0) - at(-1, 0)) - (at(2, 0) - at(-2, 0))
+    sx = 8.0 * (at(0, 1) - at(0, -1)) - (at(0, 2) - at(0, -2))
+    outer = pltpu.roll(beside, jnp.bitwise_and(-4 * z - REACH, LANES - 1), 1)
+    sy = slope_y + jnp.where(at_edge, outer, 0.0)
+    size = sx * sx + sy * sy + sz * sz
+    facing = jnp.abs(0.432 * sx + 0.54 * sy + 0.576 * sz)
+    return 0.1 + facing * lax.rsqrt(jnp.maximum(size, 36.0))
+
+
+def edge_lanes():
+    lane = lane_index()
+    return jnp.logical_or(lane < REACH, lane >= LANES - REACH)
+
+
+def scale_of(total_planes):
+    return -3.0 * math.log2(math.e) / (EXTINCTION_UNIT * total_planes)
+
+
+def local_give_kernel(total_planes, padded, material, tables, flags, lit, slope_y, through):
+    planes, rows, _ = material.shape
+    backward = jnp.max(flags[0]) > 0.5
+    band = band_matrix()
+    scale = scale_of(total_planes)
 
     def tile(index, carry):
-        top = pl.multiple_of(index * 2 * SUBLANES, 2 * SUBLANES)
-        coarse, fine = [], []
+        to, row = half_rows(TILE, index, rows, True)
+        slopes = slopes_along_y(padded, band, row, planes)
         for z in range(planes):
-            plane = padded[REACH + z, pl.ds(PAD + top, 2 * SUBLANES), :]
-            rounded = plane.astype(jnp.bfloat16)
-            coarse.append(rounded)
-            fine.append((plane - rounded.astype(jnp.float32)).astype(jnp.bfloat16))
-        both = jnp.concatenate(
-            [jnp.concatenate(coarse, axis=0), jnp.concatenate(fine, axis=0)], axis=1
-        )
-        slopes = jnp.dot(both, band, preferred_element_type=jnp.float32)
-        for z in range(planes):
-            slope_y[z, pl.ds(top, 2 * SUBLANES), :] = slopes[2 * SUBLANES * z : 2 * SUBLANES * (z + 1)]
-        for part in range(2):
-            row = pl.multiple_of(top + part * SUBLANES, SUBLANES)
+            slope_y[z, pl.ds(to, TILE), :] = slopes[TILE * z : TILE * (z + 1)]
+        for part in range(0, TILE, SUBLANES):
             clear = jnp.ones((SUBLANES, LANES), jnp.float32)
             for visit in range(planes):
                 z = jnp.where(backward, planes - 1 - visit, visit)
-                density = padded[REACH + z, pl.ds(PAD + row, SUBLANES), :]
-                label = material[z, pl.ds(row, SUBLANES), :]
-                low = jnp.bitwise_and(label, LANES - 1)
-                upper = label >= LANES
-                rg = take(0, low, upper)
-                be = take(2, low, upper)
-                extinct = jnp.bitwise_and(be, 65535).astype(jnp.float32)
-                after = clear * jnp.exp2(extinct * (density * scale))
-                stopped = clear - after
-                here = (z, pl.ds(row, SUBLANES), slice(None))
-                lit[(0, *here)] = stopped * jnp.right_shift(rg, 16).astype(jnp.float32)
-                lit[(1, *here)] = stopped * jnp.bitwise_and(rg, 65535).astype(jnp.float32)
-                lit[(2, *here)] = stopped * jnp.right_shift(be, 16).astype(jnp.float32)
-                clear = after
-            through[pl.ds(row, SUBLANES), :] = clear
+                light, clear = absorb(padded, material, tables, z, row + part, clear, scale)
+                for c in range(3):
+                    lit[c, z, pl.ds(to + part, SUBLANES), :] = light[c]
+            through[pl.ds(to + part, SUBLANES), :] = clear
         return carry
 
-    lax.fori_loop(0, rows // SUBLANES // 2, tile, 0)
-
-
-def local(padded, material, tables, flags, total_planes):
+    lax.fori_loop(0, rows // 2 // TILE, tile, 0)
+
+
+def local_give(padded, material, tables, flags, total_planes):
     planes, rows, cols = material.shape
-    shape = lambda *dims: jax.ShapeDtypeStruct(dims, jnp.float32)
+    shape = lambda *dims: pltpu.VMEM(dims, jnp.float32)
     return pl.pallas_call(
-        functools.partial(local_kernel, total_planes),
-        out_shape=(shape(3, planes, rows, cols), shape(planes, rows, cols), shape(rows, cols)),
+        functools.partial(local_give_kernel, total_planes),
+        out_shape=(
+            shape(3, planes, rows // 2, cols),
+            shape(planes, rows // 2, cols),
+            shape(rows // 2, cols),
+        ),
         in_specs=[VMEM] * 4,
         out_specs=(VMEM,) * 3,
         compiler_params=pltpu.CompilerParams(vmem_limit_bytes=VMEM_LIMIT),
@@ -192,7 +234,7 @@
             bytes_accessed=2**22,
             transcendentals=planes * rows * cols,
         ),
-        name="local",
+        name="local_give",
     )(padded, material, tables, flags)
 
 
@@ -224,56 +266,37 @@
         )
 
 
-def shade_half(padded, edge, lit, slope_y, through, out, giving):
-    _, planes, rows, _ = lit.shape
-    block_rows = rows // lax.axis_size("bz")
-    half = jnp.bitwise_and(lax.axis_index("bz") + (1 if giving else 0), 1)
-    lane = lane_index()
-    at_edge = jnp.logical_or(lane < REACH, lane >= LANES - REACH)
-
-    def pair(index, carry):
-        for part in range(2):
-            to = pl.multiple_of((2 * index + part) * SUBLANES, SUBLANES)
-            group = lax.div(to, block_rows)
-            row = pl.multiple_of((group + half) * block_rows + to, SUBLANES)
-            beside = edge[pl.ds(row, SUBLANES), :]
+def shade_give_kernel(padded_in, xa, xb, za, zb, ya, yb, lit, slope_y, through, padded, edge, give):
+    _, planes, half, _ = lit.shape
+    rows = 2 * half
+    del padded_in
+    put_halo(padded, xa, xb, za, zb, ya, yb, edge, planes, rows)
+    at_edge = edge_lanes()
+
+    def tile(index, carry):
+        to, row = half_rows(TILE, index, rows, True)
+        for part in range(0, TILE, SUBLANES):
+            beside = edge[pl.ds(row + part, SUBLANES), :]
+            place = pl.ds(to + part, SUBLANES)
             sums = [jnp.zeros((SUBLANES, LANES), jnp.float32) for _ in range(3)]
             for z in range(planes):
-                at = lambda dz, dx: padded[REACH + z + dz, pl.ds(PAD + row + dx, SUBLANES), :]
-                sz = 8.0 * (at(1, 0) - at(-1, 0)) - (at(2, 0) - at(-2, 0))
-                sx = 8.0 * (at(0, 1) - at(0, -1)) - (at(0, 2) - at(0, -2))
-                outer = pltpu.roll(beside, (-4 * z - REACH) % LANES, 1)
-                sy = slope_y[z, pl.ds(row, SUBLANES), :] + jnp.where(at_edge, outer, 0.0)
-                size = sx * sx + sy * sy + sz * sz
-                facing = jnp.abs(0.432 * sx + 0.54 * sy + 0.576 * sz)
-                shading = 0.1 + facing * lax.rsqrt(jnp.maximum(size, 36.0))
+                shading = shading_at(padded, slope_y[z, place, :], beside, at_edge, z, row + part)
                 for c in range(3):
-                    sums[c] = sums[c] + shading * lit[c, z, pl.ds(row, SUBLANES), :]
+                    sums[c] = sums[c] + shading * lit[c, z, place, :]
             for c in range(3):
-                out[c, pl.ds(to, SUBLANES), :] = sums[c] * (1.0 / COLOR_UNIT)
-            out[3, pl.ds(to, SUBLANES), :] = through[pl.ds(row, SUBLANES), :]
+                give[c, place, :] = sums[c] * (1.0 / COLOR_UNIT)
+            give[3, place, :] = through[place, :]
         return carry
 
-    lax.fori_loop(0, rows // 4 // SUBLANES, pair, 0)
-
-
-def shade_give_kernel(padded_in, xa, xb, za, zb, ya, yb, lit, slope_y, through, padded, edge, give):
-    _, planes, rows, _ = lit.shape
-    del padded_in
-    put_halo(padded, xa, xb, za, zb, ya, yb, edge, planes, rows)
-    shade_half(padded, edge, lit, slope_y, through, give, True)
-
-
-def shade_keep_kernel(padded, edge, lit, slope_y, through, keep):
-    shade_half(padded, edge, lit, slope_y, through, keep, False)
+    lax.fori_loop(0, half // TILE, tile, 0)
 
 
 def shade_give(padded, halos, lit, slope_y, through):
-    _, _, rows, cols = lit.shape
-    shape = lambda *dims: jax.ShapeDtypeStruct(dims, jnp.float32)
+    _, _, half, cols = lit.shape
+    shape = lambda *dims: pltpu.VMEM(dims, jnp.float32)
     return pl.pallas_call(
         shade_give_kernel,
-        out_shape=(shape(*padded.shape), shape(rows, LANES), shape(4, rows // 2, cols)),
+        out_shape=(shape(*padded.shape), shape(2 * half, LANES), shape(4, half, cols)),
         in_specs=[VMEM] * 10,
         out_specs=(VMEM,) * 3,
         input_output_aliases={0: 0},
@@ -282,19 +305,52 @@
     )(padded, *halos, lit, slope_y, through)
 
 
-def shade_keep(padded, edge, lit, slope_y, through):
-    _, planes, rows, cols = lit.shape
+def keep_kernel(total_planes, padded, edge, material, tables, flags, keep, slope_y):
+    planes, rows, _ = material.shape
+    backward = jnp.max(flags[0]) > 0.5
+    band = band_matrix()
+    scale = scale_of(total_planes)
+    at_edge = edge_lanes()
+
+    def tile(index, carry):
+        to, row = half_rows(TILE, index, rows, False)
+        slope_y[...] = slopes_along_y(padded, band, row, planes).reshape(planes, TILE, LANES)
+        for part in range(0, TILE, SUBLANES):
+            beside = edge[pl.ds(row + part, SUBLANES), :]
+            place = pl.ds(to + part, SUBLANES)
+            clear = jnp.ones((SUBLANES, LANES), jnp.float32)
+            sums = [jnp.zeros((SUBLANES, LANES), jnp.float32) for _ in range(3)]
+            for visit in range(planes):
+                z = jnp.where(backward, planes - 1 - visit, visit)
+                slope = slope_y[z, part : part + SUBLANES, :]
+                light, clear = absorb(padded, material, tables, z, row + part, clear, scale)
+                shading = shading_at(padded, slope, beside, at_edge, z, row + part)
+                for c in range(3):
+                    sums[c] = sums[c] + shading * light[c]
+            for c in range(3):
+                keep[c, place, :] = sums[c] * (1.0 / COLOR_UNIT)
+            keep[3, place, :] = clear
+        return carry
+
+    lax.fori_loop(0, rows // 2 // TILE, tile, 0)
+
+
+def shade_keep(padded, edge, material, tables, flags, total_planes):
+    planes, rows, cols = material.shape
     return pl.pallas_call(
-        shade_keep_kernel,
-        out_shape=jax.ShapeDtypeStruct((4, rows // 2, cols), jnp.float32),
+        functools.partial(keep_kernel, total_planes),
+        out_shape=pltpu.VMEM((4, rows // 2, cols), jnp.float32),
         in_specs=[VMEM] * 5,
         out_specs=VMEM,
+        scratch_shapes=[pltpu.VMEM((planes, TILE, LANES), jnp.float32)],
         compiler_params=pltpu.CompilerParams(vmem_limit_bytes=VMEM_LIMIT),
         cost_estimate=pl.CostEstimate(
-            flops=20 * planes * rows * cols, bytes_accessed=2**22, transcendentals=0
+            flops=40 * planes * rows * cols,
+            bytes_accessed=2**22,
+            transcendentals=planes * rows * cols,
         ),
-        name="shade_keep",
-    )(padded, edge, lit, slope_y, through)
+        name="keep",
+    )(padded, edge, material, tables, flags)
 
 
 def blend_kernel(bit, last, flags, mine, other, out):
@@ -335,10 +391,10 @@
         zb = lax.ppermute(zb, "bz", pairs["bz"][1])
     ya = lax.ppermute(y_own, "by", pairs["by"][0])
     yb = lax.ppermute(y_own, "by", pairs["by"][1])
-    lit, slope_y, through = local(padded, material, tables, flags, planes * slabs)
+    lit, slope_y, through = local_give(padded, material, tables, flags, planes * slabs)
     halos = (xa, xb, za, zb, ya, yb)
     padded, edge, give = shade_give(padded, halos, lit, slope_y, through)
-    keep = shade_keep(padded, edge, lit, slope_y, through)
+    keep = shade_keep(padded, edge, material, tables, flags, planes * slabs)
     block_rows = rows // slabs
     levels = slabs.bit_length() - 1
     my_slab = lax.axis_index("bz")

time: 24.4 us -> 22 us (0.902)
  waiting for transfers between devices: 2.34 us -> 0.44 us
  Pallas kernels: 10.3 us -> 9.82 us
    ppermute x1, waiting for transfers between devices: 2.33 us -> 0.43 us  [shards(): received = lax.ppermute(give, 'bz', flip)]
    pallas_call x2, Pallas kernels: 6.05 us -> 5.64 us  [the longest x1 3.16 us: shade_keep(): pl.pallas_call(functools.partial(keep_kernel, total_planes), out_shape=pl...]
  transfers between devices with their start and end apart: 6 -> 6, of which waited for: 1 -> 1; matrix products, arithmetic and copies ran while one was open for 0% -> 0% of each run, Pallas kernels for 25% -> 26%
where the time goes in v3:
time: 22 us; the launch traced here: 21.8 us
  starting transfers between devices  11.5 us (52%)
  Pallas kernels  9.82 us (45%)
  waiting for transfers between devices  0.44 us (2%)
    ppermute x1, starting transfers between devices, shards(): ya = lax.ppermute(y_own, 'by', pairs['by'][0])  3.9 us
    pallas_call x1, Pallas kernels, shade_keep(): pl.pallas_call(functools.partial(keep_kernel, total_planes), out_shape=pl...  3.16 us
    ppermute x1, starting transfers between devices, shards(): xb = lax.ppermute(xb, 'bx', pairs['bx'][1])  3 us
    pallas_call x1, Pallas kernels, local_give(): pl.pallas_call(functools.partial(local_give_kernel, total_planes), out_sh...  2.48 us
    ppermute x1, starting transfers between devices, shards(): za = lax.ppermute(za, 'bz', pairs['bz'][0])  2.13 us
    pallas_call x1, Pallas kernels, faces(): pl.pallas_call(functools.partial(faces_kernel, counts), out_shape=(shape(...  2.11 us
    ppermute x1, starting transfers between devices, shards(): xa = lax.ppermute(xa, 'bx', pairs['bx'][0])  1.52 us
    pallas_call x1, Pallas kernels, shade_give(): pl.pallas_call(shade_give_kernel, out_shape=(shape(*padded.shape), shape(...  1.4 us
  transfers between devices with their start and end apart: 6, of which 1 were waited for; matrix products, arithmetic and copies ran while one was open for 0% of the time, Pallas kernels for 26%

profile of v3, /device:TPU:1, one launch (start us, length us, event | category | flops | bytes accessed | tf_op | source)
XLA Modules:
  0.0 21.8 jit_solution(17824440747441594185)
XLA Ops:
  0.0 0.0 copy-start
  0.0 2.1 %faces.1 = (f32[36,144,128]{2,1,0:T(8,128)S(1)}, f32[128,128]{1,0:T(8,128)S(1)}, f32[64,128]{1,0:T(8,128)S(1)}, f32[64,128]{1,0:T(8,128)S(1)}, f32[2,128,128]{2,...) custom-call(s32[1,1,2]{2,1,0:T(1,128)} %order.1, ...), custom_call_target="tpu_custom_call" | custom-call | tf_op jit(solution)/shard_map/faces/pallas_call | solution.py:101
  2.1 2.1 %collective-permute-start.2 = (f32[2,128,128]{2,1,0:T(8,128)S(1)}, f32[2,128,128]{2,1,0:T(8,128)S(1)}, u32[]{:S(2)}, u32[]{:S(2)}) collective-permute-start(f32[2,128,128]{2,1,0:T(8,128)S(1)} %get-tuple-element.23), channel_id=1, source_target_pairs={{0,1},{1,0},{2,3},{3,2},{4,5},{5,4},{6,7},{7,6},{8,9},{9,8},{10,11... | collective-permute-start | bytes 393224 | tf_op jit(solution)/shard_map/ppermute | solution.py:389
  4.3 0.7 %collective-permute-start.4 = (f32[128,128]{1,0:T(8,128)S(1)}, f32[128,128]{1,0:T(8,128)S(1)}, u32[]{:S(2)}, u32[]{:S(2)}) collective-permute-start(f32[128,128]{1,0:T(8,128)S(1)} %get-tuple-element.25), channel_id=1, source_target_pairs={{2,4},{4,2},{3,5},{5,3},{10,12},{12,10},{11,13},{13,11},{18,20},{2... | collective-permute-start | bytes 196616 | tf_op jit(solution)/shard_map/ppermute | solution.py:393
  4.9 3.9 %collective-permute-start.3 = (f32[128,128]{1,0:T(8,128)S(1)}, f32[128,128]{1,0:T(8,128)S(1)}, u32[]{:S(2)}, u32[]{:S(2)}) collective-permute-start(f32[128,128]{1,0:T(8,128)S(1)} %get-tuple-element.25), channel_id=1, source_target_pairs={{0,2},{2,0},{4,6},{6,4},{1,3},{3,1},{5,7},{7,5},{8,10},{10,8},{12,... | collective-permute-start | bytes 196616 | tf_op jit(solution)/shard_map/ppermute | solution.py:392
  8.8 1.5 %collective-permute-start = (f32[64,128]{1,0:T(8,128)S(1)}, f32[64,128]{1,0:T(8,128)S(1)}, u32[]{:S(2)}, u32[]{:S(2)}) collective-permute-start(f32[64,128]{1,0:T(8,128)S(1)} %get-tuple-element.21), channel_id=1, source_target_pairs={{0,8},{8,0},{16,24},{24,16},{1,9},{9,1},{17,25},{25,17},{2,10},{10... | collective-permute-start | bytes 98312 | tf_op jit(solution)/shard_map/ppermute | solution.py:387
  10.3 3.0 %collective-permute-start.1 = (f32[64,128]{1,0:T(8,128)S(1)}, f32[64,128]{1,0:T(8,128)S(1)}, u32[]{:S(2)}, u32[]{:S(2)}) collective-permute-start(f32[64,128]{1,0:T(8,128)S(1)} %get-tuple-element.22), channel_id=1, source_target_pairs={{8,16},{16,8},{9,17},{17,9},{10,18},{18,10},{11,19},{19,11},{12,20... | collective-permute-start | bytes 98312 | tf_op jit(solution)/shard_map/ppermute | solution.py:388
  13.3 0.0 copy-done
  13.3 2.5 %local_give.1 = (f32[3,32,64,128]{3,2,1,0:T(8,128)S(1)}, f32[32,64,128]{2,1,0:T(8,128)S(1)}, f32[64,128]{1,0:T(8,128)S(1)}) custom-call(f32[36,144,128]{2,1,0:T(8,128)S(1)} %get-tuple-element.20.padded.padded_in, s32[32,128,128]{2,1,0:T(8,128)S(1)} %copy-done, s32[4,8,128]{2,1,0:T(8,128)S(1)} %get-tuple-element.26.tables, ...), custom_call_target="tpu_custom_call" | custom-call | flops 10485760 | bytes 4194304 | tf_op jit(solution)/shard_map/local_give/pallas_call | solution.py:222
  15.8 0.0 collective-permute-done.xa
  15.8 0.0 collective-permute-done.1.xb
  15.8 0.0 collective-permute-done.4.yb
  15.9 0.0 collective-permute-done.3.ya
  15.9 0.0 collective-permute-done.2.za
  15.9 1.4 %shade_give.1 = (f32[36,144,128]{2,1,0:T(8,128)S(1)}, f32[128,128]{1,0:T(8,128)S(1)}, f32[4,64,128]{2,1,0:T(8,128)S(1)}) custom-call(f32[36,144,128]{2,1,0:T(8,128)S(1)} %get-tuple-element.20.padded.padded_in, f32[64,128]{1,0:T(8,128)S(1)} %collective-permute-done.xa, f32[64,128]{1,0:T(8,128)S(1)} %collective-permute-done.1.xb, ...), custom_call_target="tpu_custom_call", output_to_operand_aliasing={{0}: (0, {})} | custom-call | tf_op jit(solution)/shard_map/shade_give/pallas_call | solution.py:297
  17.3 0.3 %collective-permute-start.5 = (f32[4,64,128]{2,1,0:T(8,128)S(1)}, f32[4,64,128]{2,1,0:T(8,128)S(1)}, u32[]{:S(2)}, u32[]{:S(2)}) collective-permute-start(f32[4,64,128]{2,1,0:T(8,128)S(1)} %get-tuple-element.32), channel_id=1, source_target_pairs={{0,1},{1,0},{2,3},{3,2},{4,5},{5,4},{6,7},{7,6},{8,9},{9,8},{10,11... | collective-permute-start | bytes 393224 | tf_op jit(solution)/shard_map/ppermute | solution.py:403
  17.6 3.2 %keep.1.mine = f32[4,64,128]{2,1,0:T(8,128)S(1)} custom-call(f32[36,144,128]{2,1,0:T(8,128)S(1)} %get-tuple-element.30.padded, f32[128,128]{1,0:T(8,128)S(1)} %get-tuple-element.31.edge, s32[32,128,128]{2,1,0:T(8,128)S(1)} %copy-done, s32[4,8,128]{2,1,0:T(8,128)S(1)} %get-tuple-element.26.tables, f32[2,8,128]{2,1,0:T(8,128)S(1)} %get-tuple-element.19.flags), custom_call_target="tpu_custom_call" | custom-call | flops 20971520 | bytes 4194304 | tf_op jit(solution)/shard_map/keep/pallas_call | solution.py:340
  20.7 0.4 %collective-permute-done.5.other = f32[4,64,128]{2,1,0:T(8,128)S(1)} collective-permute-done((f32[4,64,128]{2,1,0:T(8,128)S(1)}, f32[4,64,128]{2,1,0:T(8,128)S(1)}, u32[]{:S(2)}, u32[]{:S(2)}) %collective-permute-start.5) | collective-permute-done | bytes 131104 | tf_op jit(solution)/shard_map/ppermute | solution.py:403
  21.2 0.7 %blend.1 = f32[4,64,128]{2,1,0:T(8,128)} custom-call(f32[2,8,128]{2,1,0:T(8,128)S(1)} %get-tuple-element.19.flags, f32[4,64,128]{2,1,0:T(8,128)S(1)} %keep.1.mine, f32[4,64,128]{2,1,0:T(8,128)S(1)} %collective-permute-done.5.other), custom_call_target="tpu_custom_call" | custom-call | tf_op jit(solution)/shard_map/blend/pallas_call | solution.py:369
Async XLA Ops:
  0.0 13.3 %copy-start = (s32[32,128,128]{2,1,0:T(8,128)S(1)}, s32[32,128,128]{2,1,0:T(8,128)}, u32[]{:S(2)}) copy-start(s32[32,128,128]{2,1,0:T(8,128)} %material.3) | copy-start | bytes 6291460
  2.1 13.8 %collective-permute-start.2 = (f32[2,128,128]{2,1,0:T(8,128)S(1)}, f32[2,128,128]{2,1,0:T(8,128)S(1)}, u32[]{:S(2)}, u32[]{:S(2)}) collective-permute-start(f32[2,128,128]{2,1,0:T(8,128)S(1)} %get-tuple-element.23), channel_id=1, source_target_pairs={{0,1},{1,0},{2,3},{3,2},{4,5},{5,4},{6,7},{7,6},{8,9},{9,8},{10,11... | collective-permute-start | bytes 393224 | tf_op jit(solution)/shard_map/ppermute | solution.py:389
  4.3 11.6 %collective-permute-start.4 = (f32[128,128]{1,0:T(8,128)S(1)}, f32[128,128]{1,0:T(8,128)S(1)}, u32[]{:S(2)}, u32[]{:S(2)}) collective-permute-start(f32[128,128]{1,0:T(8,128)S(1)} %get-tuple-element.25), channel_id=1, source_target_pairs={{2,4},{4,2},{3,5},{5,3},{10,12},{12,10},{11,13},{13,11},{18,20},{2... | collective-permute-start | bytes 196616 | tf_op jit(solution)/shard_map/ppermute | solution.py:393
  4.9 10.9 %collective-permute-start.3 = (f32[128,128]{1,0:T(8,128)S(1)}, f32[128,128]{1,0:T(8,128)S(1)}, u32[]{:S(2)}, u32[]{:S(2)}) collective-permute-start(f32[128,128]{1,0:T(8,128)S(1)} %get-tuple-element.25), channel_id=1, source_target_pairs={{0,2},{2,0},{4,6},{6,4},{1,3},{3,1},{5,7},{7,5},{8,10},{10,8},{12,... | collective-permute-start | bytes 196616 | tf_op jit(solution)/shard_map/ppermute | solution.py:392
  8.8 7.0 %collective-permute-start = (f32[64,128]{1,0:T(8,128)S(1)}, f32[64,128]{1,0:T(8,128)S(1)}, u32[]{:S(2)}, u32[]{:S(2)}) collective-permute-start(f32[64,128]{1,0:T(8,128)S(1)} %get-tuple-element.21), channel_id=1, source_target_pairs={{0,8},{8,0},{16,24},{24,16},{1,9},{9,1},{17,25},{25,17},{2,10},{10... | collective-permute-start | bytes 98312 | tf_op jit(solution)/shard_map/ppermute | solution.py:387
  10.3 5.5 %collective-permute-start.1 = (f32[64,128]{1,0:T(8,128)S(1)}, f32[64,128]{1,0:T(8,128)S(1)}, u32[]{:S(2)}, u32[]{:S(2)}) collective-permute-start(f32[64,128]{1,0:T(8,128)S(1)} %get-tuple-element.22), channel_id=1, source_target_pairs={{8,16},{16,8},{9,17},{17,9},{10,18},{18,10},{11,19},{19,11},{12,20... | collective-permute-start | bytes 98312 | tf_op jit(solution)/shard_map/ppermute | solution.py:388
  17.3 3.9 %collective-permute-start.5 = (f32[4,64,128]{2,1,0:T(8,128)S(1)}, f32[4,64,128]{2,1,0:T(8,128)S(1)}, u32[]{:S(2)}, u32[]{:S(2)}) collective-permute-start(f32[4,64,128]{2,1,0:T(8,128)S(1)} %get-tuple-element.32), channel_id=1, source_target_pairs={{0,1},{1,0},{2,3},{3,2},{4,5},{5,4},{6,7},{7,6},{8,9},{9,8},{10,11... | collective-permute-start | bytes 393224 | tf_op jit(solution)/shard_map/ppermute | solution.py:403

commit v4 on v3

--- a/solution.py
+++ b/solution.py
@@ -35,7 +35,7 @@
     return first, second
 
 
-def faces_kernel(counts, order, density, colors, extinction, padded, y_out, xa, xb, za, zb, tables, flags, place, hues, thick, arrived):
+def faces_kernel(counts, order, density, colors, extinction, padded, ya, yb, xa, xb, za, zb, tables, flags, place, hues, thick, arrived):
     planes, rows, _ = density.shape
     parts = arrived.shape[0] - 3
     step = rows // parts
@@ -62,7 +62,8 @@
             for z in range(planes):
                 plane = padded[REACH + z, PAD + row : PAD + row + SUBLANES, :]
                 packed = jnp.where(slot == z, pltpu.roll(plane, (4 * z + REACH) % LANES, 1), packed)
-            y_out[row : row + SUBLANES, :] = packed
+            ya[row : row + SUBLANES, :] = packed
+            yb[row : row + SUBLANES, :] = packed
     odd_x, odd_z = is_odd("bx"), is_odd("bz")
     low_x, high_x = PAD, PAD + rows - REACH
     low_z, high_z = REACH, planes
@@ -98,20 +99,22 @@
     planes, rows, cols = density.shape
     shape = lambda *dims: pltpu.VMEM(dims, jnp.float32)
     z_rows = rows if counts["bz"] > 2 else SUBLANES
+    face = REACH * rows
     return pl.pallas_call(
         functools.partial(faces_kernel, counts),
         out_shape=(
             shape(planes + 2 * REACH, rows + 2 * PAD, cols),
-            shape(rows, LANES),
-            shape(REACH * planes, cols),
-            shape(REACH * planes, cols),
+            shape(face + 16, LANES),
+            shape(rows + 8, LANES),
+            shape(face + 24, cols),
+            shape(rows + 16, cols),
             shape(REACH, rows, cols),
             shape(REACH, z_rows, cols),
             pltpu.VMEM((4, SUBLANES, LANES), jnp.int32),
             shape(counts["bz"].bit_length(), SUBLANES, LANES),
         ),
         in_specs=[HBM] * 4,
-        out_specs=(VMEM,) * 8,
+        out_specs=(VMEM,) * 9,
         scratch_shapes=[
             pltpu.SMEM(order.shape, jnp.int32),
             pltpu.VMEM(colors.shape, colors.dtype),
@@ -380,7 +383,7 @@
     planes, rows, cols = density.shape
     counts = {axis: lax.axis_size(axis) for axis in ("bx", "by", "bz")}
     slabs = counts["bz"]
-    padded, y_own, xa, xb, za, zb, tables, flags = faces(
+    padded, ya, yb, xa, xb, za, zb, tables, flags = faces(
         order, density, color_table, extinction_table, counts
     )
     pairs = {axis: swaps(counts[axis]) for axis in counts}
@@ -389,8 +392,8 @@
     za = lax.ppermute(za, "bz", pairs["bz"][0])
     if slabs > 2:
         zb = lax.ppermute(zb, "bz", pairs["bz"][1])
-    ya = lax.ppermute(y_own, "by", pairs["by"][0])
-    yb = lax.ppermute(y_own, "by", pairs["by"][1])
+    ya = lax.ppermute(ya, "by", pairs["by"][0])
+    yb = lax.ppermute(yb, "by", pairs["by"][1])
     lit, slope_y, through = local_give(padded, material, tables, flags, planes * slabs)
     halos = (xa, xb, za, zb, ya, yb)
     padded, edge, give = shade_give(padded, halos, lit, slope_y, through)

time: 22 us -> 20.9 us (0.950)
  the two profiles are of different devices: /device:TPU:1 before, /device:TPU:9 now
where the time goes in v4:
time: 20.9 us; the launch traced here: 20.8 us
  starting transfers between devices  10.4 us (50%)
  Pallas kernels  9.82 us (47%)
  waiting for transfers between devices  0.44 us (2%)
    ppermute x1, starting transfers between devices, shards(): yb = lax.ppermute(yb, 'by', pairs['by'][1])  4.33 us
    ppermute x1, starting transfers between devices, shards(): xb = lax.ppermute(xb, 'bx', pairs['bx'][1])  3.62 us
    pallas_call x1, Pallas kernels, shade_keep(): pl.pallas_call(functools.partial(keep_kernel, total_planes), out_shape=pl...  3.16 us
    pallas_call x1, Pallas kernels, local_give(): pl.pallas_call(functools.partial(local_give_kernel, total_planes), out_sh...  2.48 us
    pallas_call x1, Pallas kernels, faces(): pl.pallas_call(functools.partial(faces_kernel, counts), out_shape=(shape(...  2.11 us
    ppermute x1, starting transfers between devices, shards(): za = lax.ppermute(za, 'bz', pairs['bz'][0])  1.42 us
    pallas_call x1, Pallas kernels, shade_give(): pl.pallas_call(shade_give_kernel, out_shape=(shape(*padded.shape), shape(...  1.4 us
    ppermute x1, starting transfers between devices, shards(): xa = lax.ppermute(xa, 'bx', pairs['bx'][0])  0.74 us
  transfers between devices with their start and end apart: 6, of which 1 were waited for; matrix products, arithmetic and copies ran while one was open for 0% of the time, Pallas kernels for 27%

profile of v4, /device:TPU:9, one launch (start us, length us, event | category | flops | bytes accessed | tf_op | source)
XLA Modules:
  0.0 20.8 jit_solution(7950038091868758730)
XLA Ops:
  0.0 0.0 copy-start
  0.0 2.1 %faces.1 = (f32[36,144,128]{2,1,0:T(8,128)S(1)}, f32[272,128]{1,0:T(8,128)S(1)}, f32[136,128]{1,0:T(8,128)S(1)}, f32[280,128]{1,0:T(8,128)S(1)}, f32[144,128]{1,...) custom-call(s32[1,1,2]{2,1,0:T(1,128)} %order.1, ...), custom_call_target="tpu_custom_call" | custom-call | tf_op jit(solution)/shard_map/faces/pallas_call | solution.py:103
  2.1 0.7 %collective-permute-start = (f32[280,128]{1,0:T(8,128)S(1)}, f32[280,128]{1,0:T(8,128)S(1)}, u32[]{:S(2)}, u32[]{:S(2)}) collective-permute-start(f32[280,128]{1,0:T(8,128)S(1)} %get-tuple-element.22), channel_id=1, source_target_pairs={{0,8},{8,0},{16,24},{24,16},{1,9},{9,1},{17,25},{25,17},{2,10},{10... | collective-permute-start | bytes 430088 | tf_op jit(solution)/shard_map/ppermute | solution.py:390
  2.9 0.0 collective-permute-start.3
  2.9 1.4 %collective-permute-start.2 = (f32[2,128,128]{2,1,0:T(8,128)S(1)}, f32[2,128,128]{2,1,0:T(8,128)S(1)}, u32[]{:S(2)}, u32[]{:S(2)}) collective-permute-start(f32[2,128,128]{2,1,0:T(8,128)S(1)} %get-tuple-element.24), channel_id=1, source_target_pairs={{0,1},{1,0},{2,3},{3,2},{4,5},{5,4},{6,7},{7,6},{8,9},{9,8},{10,11... | collective-permute-start | bytes 393224 | tf_op jit(solution)/shard_map/ppermute | solution.py:392
  4.3 3.6 %collective-permute-start.1 = (f32[144,128]{1,0:T(8,128)S(1)}, f32[144,128]{1,0:T(8,128)S(1)}, u32[]{:S(2)}, u32[]{:S(2)}) collective-permute-start(f32[144,128]{1,0:T(8,128)S(1)} %get-tuple-element.23), channel_id=1, source_target_pairs={{8,16},{16,8},{9,17},{17,9},{10,18},{18,10},{11,19},{19,11},{12,20... | collective-permute-start | bytes 221192 | tf_op jit(solution)/shard_map/ppermute | solution.py:391
  7.9 4.3 %collective-permute-start.4 = (f32[136,128]{1,0:T(8,128)S(1)}, f32[136,128]{1,0:T(8,128)S(1)}, u32[]{:S(2)}, u32[]{:S(2)}) collective-permute-start(f32[136,128]{1,0:T(8,128)S(1)} %get-tuple-element.27), channel_id=1, source_target_pairs={{2,4},{4,2},{3,5},{5,3},{10,12},{12,10},{11,13},{13,11},{18,20},{2... | collective-permute-start | bytes 208904 | tf_op jit(solution)/shard_map/ppermute | solution.py:396
  12.2 0.0 copy-done
  12.3 2.5 %local_give.1 = (f32[3,32,64,128]{3,2,1,0:T(8,128)S(1)}, f32[32,64,128]{2,1,0:T(8,128)S(1)}, f32[64,128]{1,0:T(8,128)S(1)}) custom-call(f32[36,144,128]{2,1,0:T(8,128)S(1)} %get-tuple-element.21.padded.padded_in, s32[32,128,128]{2,1,0:T(8,128)S(1)} %copy-done, s32[4,8,128]{2,1,0:T(8,128)S(1)} %get-tuple-element.28.tables, ...), custom_call_target="tpu_custom_call" | custom-call | flops 10485760 | bytes 4194304 | tf_op jit(solution)/shard_map/local_give/pallas_call | solution.py:225
  14.7 0.0 collective-permute-done.4.yb
  14.7 0.0 collective-permute-done.1.xb
  14.8 0.0 collective-permute-done.2.za
  14.8 0.0 collective-permute-done.3.ya
  14.8 0.0 collective-permute-done.xa
  14.8 1.4 %shade_give.1 = (f32[36,144,128]{2,1,0:T(8,128)S(1)}, f32[128,128]{1,0:T(8,128)S(1)}, f32[4,64,128]{2,1,0:T(8,128)S(1)}) custom-call(f32[36,144,128]{2,1,0:T(8,128)S(1)} %get-tuple-element.21.padded.padded_in, f32[280,128]{1,0:T(8,128)S(1)} %collective-permute-done.xa, f32[144,128]{1,0:T(8,128)S(1)} %collective-permute-done.1.xb, ...), custom_call_target="tpu_custom_call", output_to_operand_aliasing={{0}: (0, {})} | custom-call | tf_op jit(solution)/shard_map/shade_give/pallas_call | solution.py:300
  16.2 0.3 %collective-permute-start.5 = (f32[4,64,128]{2,1,0:T(8,128)S(1)}, f32[4,64,128]{2,1,0:T(8,128)S(1)}, u32[]{:S(2)}, u32[]{:S(2)}) collective-permute-start(f32[4,64,128]{2,1,0:T(8,128)S(1)} %get-tuple-element.34), channel_id=1, source_target_pairs={{0,1},{1,0},{2,3},{3,2},{4,5},{5,4},{6,7},{7,6},{8,9},{9,8},{10,11... | collective-permute-start | bytes 393224 | tf_op jit(solution)/shard_map/ppermute | solution.py:406
  16.5 3.2 %keep.1.mine = f32[4,64,128]{2,1,0:T(8,128)S(1)} custom-call(f32[36,144,128]{2,1,0:T(8,128)S(1)} %get-tuple-element.32.padded, f32[128,128]{1,0:T(8,128)S(1)} %get-tuple-element.33.edge, s32[32,128,128]{2,1,0:T(8,128)S(1)} %copy-done, s32[4,8,128]{2,1,0:T(8,128)S(1)} %get-tuple-element.28.tables, f32[2,8,128]{2,1,0:T(8,128)S(1)} %get-tuple-element.20.flags), custom_call_target="tpu_custom_call" | custom-call | flops 20971520 | bytes 4194304 | tf_op jit(solution)/shard_map/keep/pallas_call | solution.py:343
  19.7 0.4 %collective-permute-done.5.other = f32[4,64,128]{2,1,0:T(8,128)S(1)} collective-permute-done((f32[4,64,128]{2,1,0:T(8,128)S(1)}, f32[4,64,128]{2,1,0:T(8,128)S(1)}, u32[]{:S(2)}, u32[]{:S(2)}) %collective-permute-start.5) | collective-permute-done | bytes 131104 | tf_op jit(solution)/shard_map/ppermute | solution.py:406
  20.1 0.7 %blend.1 = f32[4,64,128]{2,1,0:T(8,128)} custom-call(f32[2,8,128]{2,1,0:T(8,128)S(1)} %get-tuple-element.20.flags, f32[4,64,128]{2,1,0:T(8,128)S(1)} %keep.1.mine, f32[4,64,128]{2,1,0:T(8,128)S(1)} %collective-permute-done.5.other), custom_call_target="tpu_custom_call" | custom-call | tf_op jit(solution)/shard_map/blend/pallas_call | solution.py:372
Async XLA Ops:
  0.0 12.3 %copy-start = (s32[32,128,128]{2,1,0:T(8,128)S(1)}, s32[32,128,128]{2,1,0:T(8,128)}, u32[]{:S(2)}) copy-start(s32[32,128,128]{2,1,0:T(8,128)} %material.3) | copy-start | bytes 6291460
  2.1 12.7 %collective-permute-start = (f32[280,128]{1,0:T(8,128)S(1)}, f32[280,128]{1,0:T(8,128)S(1)}, u32[]{:S(2)}, u32[]{:S(2)}) collective-permute-start(f32[280,128]{1,0:T(8,128)S(1)} %get-tuple-element.22), channel_id=1, source_target_pairs={{0,8},{8,0},{16,24},{24,16},{1,9},{9,1},{17,25},{25,17},{2,10},{10... | collective-permute-start | bytes 430088 | tf_op jit(solution)/shard_map/ppermute | solution.py:390
  2.9 11.9 %collective-permute-start.3 = (f32[272,128]{1,0:T(8,128)S(1)}, f32[272,128]{1,0:T(8,128)S(1)}, u32[]{:S(2)}, u32[]{:S(2)}) collective-permute-start(f32[272,128]{1,0:T(8,128)S(1)} %get-tuple-element.26), channel_id=1, source_target_pairs={{0,2},{2,0},{4,6},{6,4},{1,3},{3,1},{5,7},{7,5},{8,10},{10,8},{12,... | collective-permute-start | bytes 417800 | tf_op jit(solution)/shard_map/ppermute | solution.py:395
  2.9 11.9 %collective-permute-start.2 = (f32[2,128,128]{2,1,0:T(8,128)S(1)}, f32[2,128,128]{2,1,0:T(8,128)S(1)}, u32[]{:S(2)}, u32[]{:S(2)}) collective-permute-start(f32[2,128,128]{2,1,0:T(8,128)S(1)} %get-tuple-element.24), channel_id=1, source_target_pairs={{0,1},{1,0},{2,3},{3,2},{4,5},{5,4},{6,7},{7,6},{8,9},{9,8},{10,11... | collective-permute-start | bytes 393224 | tf_op jit(solution)/shard_map/ppermute | solution.py:392
  4.3 10.5 %collective-permute-start.1 = (f32[144,128]{1,0:T(8,128)S(1)}, f32[144,128]{1,0:T(8,128)S(1)}, u32[]{:S(2)}, u32[]{:S(2)}) collective-permute-start(f32[144,128]{1,0:T(8,128)S(1)} %get-tuple-element.23), channel_id=1, source_target_pairs={{8,16},{16,8},{9,17},{17,9},{10,18},{18,10},{11,19},{19,11},{12,20... | collective-permute-start | bytes 221192 | tf_op jit(solution)/shard_map/ppermute | solution.py:391
  7.9 6.8 %collective-permute-start.4 = (f32[136,128]{1,0:T(8,128)S(1)}, f32[136,128]{1,0:T(8,128)S(1)}, u32[]{:S(2)}, u32[]{:S(2)}) collective-permute-start(f32[136,128]{1,0:T(8,128)S(1)} %get-tuple-element.27), channel_id=1, source_target_pairs={{2,4},{4,2},{3,5},{5,3},{10,12},{12,10},{11,13},{13,11},{18,20},{2... | collective-permute-start | bytes 208904 | tf_op jit(solution)/shard_map/ppermute | solution.py:396
  16.2 3.9 %collective-permute-start.5 = (f32[4,64,128]{2,1,0:T(8,128)S(1)}, f32[4,64,128]{2,1,0:T(8,128)S(1)}, u32[]{:S(2)}, u32[]{:S(2)}) collective-permute-start(f32[4,64,128]{2,1,0:T(8,128)S(1)} %get-tuple-element.34), channel_id=1, source_target_pairs={{0,1},{1,0},{2,3},{3,2},{4,5},{5,4},{6,7},{7,6},{8,9},{9,8},{10,11... | collective-permute-start | bytes 393224 | tf_op jit(solution)/shard_map/ppermute | solution.py:406

commit v5 on v4

--- a/solution.py
+++ b/solution.py
@@ -35,49 +35,28 @@
     return first, second
 
 
-def faces_kernel(counts, order, density, colors, extinction, padded, ya, yb, xa, xb, za, zb, tables, flags, place, hues, thick, arrived):
+def x_face(out, source, start, planes):
+    for z in range(planes):
+        out[REACH * z : REACH * (z + 1), :] = source(z, start)
+
+
+def early_kernel(counts, order, density, colors, extinction, xa, za, zb, tables, flags, place, hues, thick, rows_x, arrived):
     planes, rows, _ = density.shape
-    parts = arrived.shape[0] - 3
-    step = rows // parts
+    odd_x, odd_z, top = is_odd("bx"), is_odd("bz"), planes - REACH
+    ends = [(za, jnp.where(odd_z, 0, top))]
+    if counts["bz"] > 2:
+        ends.append((zb, jnp.where(odd_z, top, 0)))
+    low_x = pl.multiple_of(jnp.where(odd_x, 0, rows - SUBLANES), SUBLANES)
+    pairs = [(density.at[:, pl.ds(low_x, SUBLANES), :], rows_x)]
+    pairs += [(density.at[pl.ds(start, REACH)], out) for out, start in ends]
+    pairs += [(order, place), (colors, hues), (extinction, thick)]
     copies = [
-        pltpu.make_async_copy(
-            density.at[:, pl.ds(k * step, step), :],
-            padded.at[pl.ds(REACH, planes), pl.ds(PAD + k * step, step), :],
-            arrived.at[k],
-        )
-        for k in range(parts)
+        pltpu.make_async_copy(source, target, arrived.at[k])
+        for k, (source, target) in enumerate(pairs)
     ]
-    small = [
-        pltpu.make_async_copy(source, target, arrived.at[parts + k])
-        for k, (source, target) in enumerate(((order, place), (colors, hues), (extinction, thick)))
-    ]
-    for copy in copies + small:
+    for copy in copies:
         copy.start()
-    slot = jnp.right_shift(lane_index(), 2)
-    for k in range(parts):
-        copies[k].wait()
-        for tile in range(step // SUBLANES):
-            row = k * step + tile * SUBLANES
-            packed = jnp.zeros((SUBLANES, LANES), jnp.float32)
-            for z in range(planes):
-                plane = padded[REACH + z, PAD + row : PAD + row + SUBLANES, :]
-                packed = jnp.where(slot == z, pltpu.roll(plane, (4 * z + REACH) % LANES, 1), packed)
-            ya[row : row + SUBLANES, :] = packed
-            yb[row : row + SUBLANES, :] = packed
-    odd_x, odd_z = is_odd("bx"), is_odd("bz")
-    low_x, high_x = PAD, PAD + rows - REACH
-    low_z, high_z = REACH, planes
-    for out, start in ((xa, jnp.where(odd_x, low_x, high_x)), (xb, jnp.where(odd_x, high_x, low_x))):
-        for z in range(planes):
-            out[REACH * z : REACH * (z + 1), :] = padded[REACH + z, pl.ds(start, REACH), :]
-    for out, start in ((za, jnp.where(odd_z, low_z, high_z)), (zb, jnp.where(odd_z, high_z, low_z))):
-        if out is zb and counts["bz"] == 2:
-            continue
-        for layer in range(REACH):
-            out[layer] = padded[start + layer, PAD : PAD + rows, :]
-    if counts["bz"] == 2:
-        zb[...] = jnp.zeros(zb.shape, jnp.float32)
-    for copy in small:
+    for copy in copies[-3:]:
         copy.wait()
     slabs = counts["bz"]
     backward = (place[0, 0, 0] > place[0, 0, slabs - 1]).astype(jnp.float32)
@@ -93,6 +72,31 @@
             tables[2 * k + part] = jnp.broadcast_to(
                 table[:, part * LANES : (part + 1) * LANES], (SUBLANES, LANES)
             )
+    if counts["bz"] == 2:
+        zb[...] = jnp.zeros(zb.shape, jnp.float32)
+    for copy in copies[:-3]:
+        copy.wait()
+    start = jnp.where(odd_x, 0, SUBLANES - REACH)
+    x_face(xa, lambda z, at: rows_x[z, pl.ds(at, REACH), :], start, planes)
+
+
+def pack_kernel(density, padded, ya, yb, xb, arrived):
+    planes, rows, _ = density.shape
+    whole = pltpu.make_async_copy(
+        density, padded.at[pl.ds(REACH, planes), pl.ds(PAD, rows), :], arrived
+    )
+    whole.start()
+    start = jnp.where(is_odd("bx"), rows - REACH, 0)
+    x_face(xb, lambda z, at: density[z, pl.ds(at, REACH), :], start, planes)
+    slot = jnp.right_shift(lane_index(), 2)
+    for row in range(0, rows, SUBLANES):
+        packed = jnp.zeros((SUBLANES, LANES), jnp.float32)
+        for z in range(planes):
+            plane = density[z, row : row + SUBLANES, :]
+            packed = jnp.where(slot == z, pltpu.roll(plane, (4 * z + REACH) % LANES, 1), packed)
+        ya[row : row + SUBLANES, :] = packed
+        yb[row : row + SUBLANES, :] = packed
+    whole.wait()
 
 
 def faces(order, density, colors, extinction, counts):
@@ -100,30 +104,47 @@
     shape = lambda *dims: pltpu.VMEM(dims, jnp.float32)
     z_rows = rows if counts["bz"] > 2 else SUBLANES
     face = REACH * rows
-    return pl.pallas_call(
-        functools.partial(faces_kernel, counts),
+    params = pltpu.CompilerParams(vmem_limit_bytes=VMEM_LIMIT)
+    fixed = [
+        pltpu.with_memory_space_constraint(a, pltpu.HBM)
+        for a in (order, density, colors, extinction)
+    ]
+    xa, za, zb, tables, flags = pl.pallas_call(
+        functools.partial(early_kernel, counts),
         out_shape=(
-            shape(planes + 2 * REACH, rows + 2 * PAD, cols),
-            shape(face + 16, LANES),
-            shape(rows + 8, LANES),
             shape(face + 24, cols),
-            shape(rows + 16, cols),
             shape(REACH, rows, cols),
             shape(REACH, z_rows, cols),
             pltpu.VMEM((4, SUBLANES, LANES), jnp.int32),
             shape(counts["bz"].bit_length(), SUBLANES, LANES),
         ),
         in_specs=[HBM] * 4,
-        out_specs=(VMEM,) * 9,
+        out_specs=(VMEM,) * 5,
         scratch_shapes=[
             pltpu.SMEM(order.shape, jnp.int32),
             pltpu.VMEM(colors.shape, colors.dtype),
             pltpu.VMEM(extinction.shape, extinction.dtype),
-            pltpu.SemaphoreType.DMA((7,)),
+            pltpu.VMEM((planes, SUBLANES, cols), jnp.float32),
+            pltpu.SemaphoreType.DMA((6,)),
         ],
-        compiler_params=pltpu.CompilerParams(vmem_limit_bytes=VMEM_LIMIT),
-        name="faces",
-    )(*(pltpu.with_memory_space_constraint(a, pltpu.HBM) for a in (order, density, colors, extinction)))
+        compiler_params=params,
+        name="early",
+    )(*fixed)
+    padded, ya, yb, xb = pl.pallas_call(
+        pack_kernel,
+        out_shape=(
+            shape(planes + 2 * REACH, rows + 2 * PAD, cols),
+            shape(rows + 24, LANES),
+            shape(rows + 8, LANES),
+            shape(rows + 16, cols),
+        ),
+        in_specs=[VMEM],
+        out_specs=(VMEM,) * 4,
+        scratch_shapes=[pltpu.SemaphoreType.DMA],
+        compiler_params=params,
+        name="pack",
+    )(density)
+    return padded, ya, yb, xa, xb, za, zb, tables, flags
 
 
 def half_rows(tile_rows, index, rows, giving):
@@ -277,8 +298,9 @@
     at_edge = edge_lanes()
 
     def tile(index, carry):
-        to, row = half_rows(TILE, index, rows, True)
-        for part in range(0, TILE, SUBLANES):
+        for step in range(2 * (TILE // SUBLANES)):
+            to, row = half_rows(TILE, 2 * index + step // 2, rows, True)
+            part = step % 2 * SUBLANES
             beside = edge[pl.ds(row + part, SUBLANES), :]
             place = pl.ds(to + part, SUBLANES)
             sums = [jnp.zeros((SUBLANES, LANES), jnp.float32) for _ in range(3)]
@@ -291,7 +313,7 @@
             give[3, place, :] = through[place, :]
         return carry
 
-    lax.fori_loop(0, half // TILE, tile, 0)
+    lax.fori_loop(0, half // TILE // 2, tile, 0)
 
 
 def shade_give(padded, halos, lit, slope_y, through):

time: 20.9 us -> 20.8 us (level)
  Pallas kernels: 9.82 us -> 9.59 us
    ppermute x1, starting transfers between devices: 0.01 us -> 0.23 us  [shards(): ya = lax.ppermute(ya, 'by', pairs['by'][0])]
    pallas_call x1 -> x2, Pallas kernels: 2.11 us -> 1.96 us  [the longest x1 1.18 us: faces(): pl.pallas_call(functools.partial(early_kernel, counts), out_shape=(shape(...]
  transfers between devices with their start and end apart: 6 -> 6, of which waited for: 1 -> 1; matrix products, arithmetic and copies ran while one was open for 0% -> 0% of each run, Pallas kernels for 27% -> 31%
where the time goes in v5:
time: 20.8 us; the launch traced here: 20.6 us
  starting transfers between devices  10.5 us (50%)
  Pallas kernels  9.59 us (46%)
  waiting for transfers between devices  0.47 us (2%)
    ppermute x1, starting transfers between devices, shards(): yb = lax.ppermute(yb, 'by', pairs['by'][1])  4.33 us
    ppermute x1, starting transfers between devices, shards(): xb = lax.ppermute(xb, 'bx', pairs['bx'][1])  3.62 us
    pallas_call x1, Pallas kernels, shade_keep(): pl.pallas_call(functools.partial(keep_kernel, total_planes), out_shape=pl...  3.13 us
    pallas_call x1, Pallas kernels, local_give(): pl.pallas_call(functools.partial(local_give_kernel, total_planes), out_sh...  2.47 us
    pallas_call x1, Pallas kernels, shade_give(): pl.pallas_call(shade_give_kernel, out_shape=(shape(*padded.shape), shape(...  1.35 us
    ppermute x1, starting transfers between devices, shards(): za = lax.ppermute(za, 'bz', pairs['bz'][0])  1.25 us
    pallas_call x1, Pallas kernels, faces(): pl.pallas_call(functools.partial(early_kernel, counts), out_shape=(shape(...  1.18 us
    pallas_call x1, Pallas kernels, faces(): pl.pallas_call(pack_kernel, out_shape=(shape(planes + 2 * REACH, rows + 2...  0.78 us
  transfers between devices with their start and end apart: 6, of which 1 were waited for; matrix products, arithmetic and copies ran while one was open for 0% of the time, Pallas kernels for 31%

profile of v5, /device:TPU:9, one launch (start us, length us, event | category | flops | bytes accessed | tf_op | source)
XLA Modules:
  0.0 20.6 jit_solution(14610362566172839711)
XLA Ops:
  0.0 0.0 copy-start.1
  0.0 0.0 copy-start
  0.0 1.2 %early.1 = (f32[280,128]{1,0:T(8,128)S(1)}, f32[2,128,128]{2,1,0:T(8,128)S(1)}, f32[2,8,128]{2,1,0:T(8,128)S(1)}, s32[4,8,128]{2,1,0:T(8,128)S(1)}, f32[2,8,128]{2,1,0:T(8,128)S(1)}) custom-call(s32[1,1,2]{2,1,0:T(1,128)} %order.1, f32[32,128,128]{2,1,0:T(8,128)} %density.3, bf16[3,256]{1,0:T(4,128)(2,1)} %colors.1, bf16[256]{0:T(256)(128)(2,1)} %extinction.1), custom_call_target="tpu_custom_call" | custom-call | tf_op jit(solution)/shard_map/early/pallas_call | solution.py:112
  1.2 0.7 %collective-permute-start = (f32[280,128]{1,0:T(8,128)S(1)}, f32[280,128]{1,0:T(8,128)S(1)}, u32[]{:S(2)}, u32[]{:S(2)}) collective-permute-start(f32[280,128]{1,0:T(8,128)S(1)} %get-tuple-element.22), channel_id=1, source_target_pairs={{0,8},{8,0},{16,24},{24,16},{1,9},{9,1},{17,25},{25,17},{2,10},{10... | collective-permute-start | bytes 430088 | tf_op jit(solution)/shard_map/ppermute | solution.py:412
  1.9 1.3 %collective-permute-start.2 = (f32[2,128,128]{2,1,0:T(8,128)S(1)}, f32[2,128,128]{2,1,0:T(8,128)S(1)}, u32[]{:S(2)}, u32[]{:S(2)}) collective-permute-start(f32[2,128,128]{2,1,0:T(8,128)S(1)} %get-tuple-element.24), channel_id=1, source_target_pairs={{0,1},{1,0},{2,3},{3,2},{4,5},{5,4},{6,7},{7,6},{8,9},{9,8},{10,11... | collective-permute-start | bytes 393224 | tf_op jit(solution)/shard_map/ppermute | solution.py:414
  3.2 0.0 copy-done.1
  3.2 0.8 %pack.1 = (f32[36,144,128]{2,1,0:T(8,128)S(1)}, f32[152,128]{1,0:T(8,128)S(1)}, f32[136,128]{1,0:T(8,128)S(1)}, f32[144,128]{1,0:T(8,128)S(1)}) custom-call(f32[32,128,128]{2,1,0:T(8,128)S(1)} %copy-done.1), custom_call_target="tpu_custom_call" | custom-call | tf_op jit(solution)/shard_map/pack/pallas_call | solution.py:133
  4.0 0.2 %collective-permute-start.3 = (f32[152,128]{1,0:T(8,128)S(1)}, f32[152,128]{1,0:T(8,128)S(1)}, u32[]{:S(2)}, u32[]{:S(2)}) collective-permute-start(f32[152,128]{1,0:T(8,128)S(1)} %get-tuple-element.26), channel_id=1, source_target_pairs={{0,2},{2,0},{4,6},{6,4},{1,3},{3,1},{5,7},{7,5},{8,10},{10,8},{12,... | collective-permute-start | bytes 233480 | tf_op jit(solution)/shard_map/ppermute | solution.py:417
  4.2 3.6 %collective-permute-start.1 = (f32[144,128]{1,0:T(8,128)S(1)}, f32[144,128]{1,0:T(8,128)S(1)}, u32[]{:S(2)}, u32[]{:S(2)}) collective-permute-start(f32[144,128]{1,0:T(8,128)S(1)} %get-tuple-element.23), channel_id=1, source_target_pairs={{8,16},{16,8},{9,17},{17,9},{10,18},{18,10},{11,19},{19,11},{12,20... | collective-permute-start | bytes 221192 | tf_op jit(solution)/shard_map/ppermute | solution.py:413
  7.8 4.3 %collective-permute-start.4 = (f32[136,128]{1,0:T(8,128)S(1)}, f32[136,128]{1,0:T(8,128)S(1)}, u32[]{:S(2)}, u32[]{:S(2)}) collective-permute-start(f32[136,128]{1,0:T(8,128)S(1)} %get-tuple-element.27), channel_id=1, source_target_pairs={{2,4},{4,2},{3,5},{5,3},{10,12},{12,10},{11,13},{13,11},{18,20},{2... | collective-permute-start | bytes 208904 | tf_op jit(solution)/shard_map/ppermute | solution.py:418
  12.2 0.0 copy-done
  12.2 2.5 %local_give.1 = (f32[3,32,64,128]{3,2,1,0:T(8,128)S(1)}, f32[32,64,128]{2,1,0:T(8,128)S(1)}, f32[64,128]{1,0:T(8,128)S(1)}) custom-call(f32[36,144,128]{2,1,0:T(8,128)S(1)} %get-tuple-element.21.padded.padded_in, s32[32,128,128]{2,1,0:T(8,128)S(1)} %copy-done, s32[4,8,128]{2,1,0:T(8,128)S(1)} %get-tuple-element.28.tables, ...), custom_call_target="tpu_custom_call" | custom-call | flops 10485760 | bytes 4194304 | tf_op jit(solution)/shard_map/local_give/pallas_call | solution.py:246
  14.7 0.0 collective-permute-done.4.yb
  14.7 0.0 collective-permute-done.1.xb
  14.7 0.0 collective-permute-done.3.ya
  14.7 0.0 collective-permute-done.2.za
  14.7 0.0 collective-permute-done.xa
  14.7 1.4 %shade_give.1 = (f32[36,144,128]{2,1,0:T(8,128)S(1)}, f32[128,128]{1,0:T(8,128)S(1)}, f32[4,64,128]{2,1,0:T(8,128)S(1)}) custom-call(f32[36,144,128]{2,1,0:T(8,128)S(1)} %get-tuple-element.21.padded.padded_in, f32[280,128]{1,0:T(8,128)S(1)} %collective-permute-done.xa, f32[144,128]{1,0:T(8,128)S(1)} %collective-permute-done.1.xb, ...), custom_call_target="tpu_custom_call", output_to_operand_aliasing={{0}: (0, {})} | custom-call | tf_op jit(solution)/shard_map/shade_give/pallas_call | solution.py:322
  16.1 0.3 %collective-permute-start.5 = (f32[4,64,128]{2,1,0:T(8,128)S(1)}, f32[4,64,128]{2,1,0:T(8,128)S(1)}, u32[]{:S(2)}, u32[]{:S(2)}) collective-permute-start(f32[4,64,128]{2,1,0:T(8,128)S(1)} %get-tuple-element.34), channel_id=1, source_target_pairs={{0,1},{1,0},{2,3},{3,2},{4,5},{5,4},{6,7},{7,6},{8,9},{9,8},{10,11... | collective-permute-start | bytes 393224 | tf_op jit(solution)/shard_map/ppermute | solution.py:428
  16.4 3.1 %keep.1.mine = f32[4,64,128]{2,1,0:T(8,128)S(1)} custom-call(f32[36,144,128]{2,1,0:T(8,128)S(1)} %get-tuple-element.32.padded, f32[128,128]{1,0:T(8,128)S(1)} %get-tuple-element.33.edge, s32[32,128,128]{2,1,0:T(8,128)S(1)} %copy-done, s32[4,8,128]{2,1,0:T(8,128)S(1)} %get-tuple-element.28.tables, f32[2,8,128]{2,1,0:T(8,128)S(1)} %get-tuple-element.20.flags), custom_call_target="tpu_custom_call" | custom-call | flops 20971520 | bytes 4194304 | tf_op jit(solution)/shard_map/keep/pallas_call | solution.py:365
  19.5 0.5 %collective-permute-done.5.other = f32[4,64,128]{2,1,0:T(8,128)S(1)} collective-permute-done((f32[4,64,128]{2,1,0:T(8,128)S(1)}, f32[4,64,128]{2,1,0:T(8,128)S(1)}, u32[]{:S(2)}, u32[]{:S(2)}) %collective-permute-start.5) | collective-permute-done | bytes 131104 | tf_op jit(solution)/shard_map/ppermute | solution.py:428
  20.0 0.7 %blend.1 = f32[4,64,128]{2,1,0:T(8,128)} custom-call(f32[2,8,128]{2,1,0:T(8,128)S(1)} %get-tuple-element.20.flags, f32[4,64,128]{2,1,0:T(8,128)S(1)} %keep.1.mine, f32[4,64,128]{2,1,0:T(8,128)S(1)} %collective-permute-done.5.other), custom_call_target="tpu_custom_call" | custom-call | tf_op jit(solution)/shard_map/blend/pallas_call | solution.py:394
Async XLA Ops:
  0.0 3.2 %copy-start.1 = (f32[32,128,128]{2,1,0:T(8,128)S(1)}, f32[32,128,128]{2,1,0:T(8,128)}, u32[]{:S(2)}) copy-start(f32[32,128,128]{2,1,0:T(8,128)} %density.3) | copy-start | bytes 6291460
  0.0 12.2 %copy-start = (s32[32,128,128]{2,1,0:T(8,128)S(1)}, s32[32,128,128]{2,1,0:T(8,128)}, u32[]{:S(2)}) copy-start(s32[32,128,128]{2,1,0:T(8,128)} %material.3) | copy-start | bytes 6291460
  1.2 13.5 %collective-permute-start = (f32[280,128]{1,0:T(8,128)S(1)}, f32[280,128]{1,0:T(8,128)S(1)}, u32[]{:S(2)}, u32[]{:S(2)}) collective-permute-start(f32[280,128]{1,0:T(8,128)S(1)} %get-tuple-element.22), channel_id=1, source_target_pairs={{0,8},{8,0},{16,24},{24,16},{1,9},{9,1},{17,25},{25,17},{2,10},{10... | collective-permute-start | bytes 430088 | tf_op jit(solution)/shard_map/ppermute | solution.py:412
  1.9 12.8 %collective-permute-start.2 = (f32[2,128,128]{2,1,0:T(8,128)S(1)}, f32[2,128,128]{2,1,0:T(8,128)S(1)}, u32[]{:S(2)}, u32[]{:S(2)}) collective-permute-start(f32[2,128,128]{2,1,0:T(8,128)S(1)} %get-tuple-element.24), channel_id=1, source_target_pairs={{0,1},{1,0},{2,3},{3,2},{4,5},{5,4},{6,7},{7,6},{8,9},{9,8},{10,11... | collective-permute-start | bytes 393224 | tf_op jit(solution)/shard_map/ppermute | solution.py:414
  4.0 10.7 %collective-permute-start.3 = (f32[152,128]{1,0:T(8,128)S(1)}, f32[152,128]{1,0:T(8,128)S(1)}, u32[]{:S(2)}, u32[]{:S(2)}) collective-permute-start(f32[152,128]{1,0:T(8,128)S(1)} %get-tuple-element.26), channel_id=1, source_target_pairs={{0,2},{2,0},{4,6},{6,4},{1,3},{3,1},{5,7},{7,5},{8,10},{10,8},{12,... | collective-permute-start | bytes 233480 | tf_op jit(solution)/shard_map/ppermute | solution.py:417
  4.2 10.5 %collective-permute-start.1 = (f32[144,128]{1,0:T(8,128)S(1)}, f32[144,128]{1,0:T(8,128)S(1)}, u32[]{:S(2)}, u32[]{:S(2)}) collective-permute-start(f32[144,128]{1,0:T(8,128)S(1)} %get-tuple-element.23), channel_id=1, source_target_pairs={{8,16},{16,8},{9,17},{17,9},{10,18},{18,10},{11,19},{19,11},{12,20... | collective-permute-start | bytes 221192 | tf_op jit(solution)/shard_map/ppermute | solution.py:413
  7.8 6.8 %collective-permute-start.4 = (f32[136,128]{1,0:T(8,128)S(1)}, f32[136,128]{1,0:T(8,128)S(1)}, u32[]{:S(2)}, u32[]{:S(2)}) collective-permute-start(f32[136,128]{1,0:T(8,128)S(1)} %get-tuple-element.27), channel_id=1, source_target_pairs={{2,4},{4,2},{3,5},{5,3},{10,12},{12,10},{11,13},{13,11},{18,20},{2... | collective-permute-start | bytes 208904 | tf_op jit(solution)/shard_map/ppermute | solution.py:418
  16.1 3.9 %collective-permute-start.5 = (f32[4,64,128]{2,1,0:T(8,128)S(1)}, f32[4,64,128]{2,1,0:T(8,128)S(1)}, u32[]{:S(2)}, u32[]{:S(2)}) collective-permute-start(f32[4,64,128]{2,1,0:T(8,128)S(1)} %get-tuple-element.34), channel_id=1, source_target_pairs={{0,1},{1,0},{2,3},{3,2},{4,5},{5,4},{6,7},{7,6},{8,9},{9,8},{10,11... | collective-permute-start | bytes 393224 | tf_op jit(solution)/shard_map/ppermute | solution.py:428

commit v6 on v5

--- a/solution.py
+++ b/solution.py
@@ -80,7 +80,7 @@
     x_face(xa, lambda z, at: rows_x[z, pl.ds(at, REACH), :], start, planes)
 
 
-def pack_kernel(density, padded, ya, yb, xb, arrived):
+def pack_kernel(density, padded, ya, yb, xb, columns, arrived):
     planes, rows, _ = density.shape
     whole = pltpu.make_async_copy(
         density, padded.at[pl.ds(REACH, planes), pl.ds(PAD, rows), :], arrived
@@ -94,8 +94,17 @@
         for z in range(planes):
             plane = density[z, row : row + SUBLANES, :]
             packed = jnp.where(slot == z, pltpu.roll(plane, (4 * z + REACH) % LANES, 1), packed)
-        ya[row : row + SUBLANES, :] = packed
-        yb[row : row + SUBLANES, :] = packed
+        columns[row : row + SUBLANES, :] = packed
+    side = jnp.bitwise_and(lane_index(), 3)
+    odd_y = is_odd("by")
+    for row in range(0, rows // 2, SUBLANES):
+        upper = columns[row : row + SUBLANES, :]
+        lower = pltpu.roll(columns[rows // 2 + row : rows // 2 + row + SUBLANES, :], 2, 1)
+        high_face = jnp.where(side < 2, upper, lower)
+        lower = pltpu.roll(lower, LANES - 4, 1)
+        low_face = jnp.where(side < 2, lower, upper)
+        ya[row : row + SUBLANES, :] = jnp.where(odd_y, low_face, high_face)
+        yb[row : row + SUBLANES, :] = jnp.where(odd_y, high_face, low_face)
     whole.wait()
 
 
@@ -104,6 +113,7 @@
     shape = lambda *dims: pltpu.VMEM(dims, jnp.float32)
     z_rows = rows if counts["bz"] > 2 else SUBLANES
     face = REACH * rows
+    size = max(REACH * planes, rows // 2)
     params = pltpu.CompilerParams(vmem_limit_bytes=VMEM_LIMIT)
     fixed = [
         pltpu.with_memory_space_constraint(a, pltpu.HBM)
@@ -134,13 +144,13 @@
         pack_kernel,
         out_shape=(
             shape(planes + 2 * REACH, rows + 2 * PAD, cols),
-            shape(rows + 24, LANES),
-            shape(rows + 8, LANES),
-            shape(rows + 16, cols),
+            shape(size + 16, LANES),
+            shape(size, LANES),
+            shape(size + 8, cols),
         ),
         in_specs=[VMEM],
         out_specs=(VMEM,) * 4,
-        scratch_shapes=[pltpu.SemaphoreType.DMA],
+        scratch_shapes=[pltpu.VMEM((rows, LANES), jnp.float32), pltpu.SemaphoreType.DMA],
         compiler_params=params,
         name="pack",
     )(density)
@@ -223,21 +233,22 @@
     scale = scale_of(total_planes)
 
     def tile(index, carry):
-        to, row = half_rows(TILE, index, rows, True)
-        slopes = slopes_along_y(padded, band, row, planes)
-        for z in range(planes):
-            slope_y[z, pl.ds(to, TILE), :] = slopes[TILE * z : TILE * (z + 1)]
-        for part in range(0, TILE, SUBLANES):
-            clear = jnp.ones((SUBLANES, LANES), jnp.float32)
-            for visit in range(planes):
-                z = jnp.where(backward, planes - 1 - visit, visit)
-                light, clear = absorb(padded, material, tables, z, row + part, clear, scale)
-                for c in range(3):
-                    lit[c, z, pl.ds(to + part, SUBLANES), :] = light[c]
-            through[pl.ds(to + part, SUBLANES), :] = clear
+        for step in range(2):
+            to, row = half_rows(TILE, 2 * index + step, rows, True)
+            slopes = slopes_along_y(padded, band, row, planes)
+            for z in range(planes):
+                slope_y[z, pl.ds(to, TILE), :] = slopes[TILE * z : TILE * (z + 1)]
+            for part in range(0, TILE, SUBLANES):
+                clear = jnp.ones((SUBLANES, LANES), jnp.float32)
+                for visit in range(planes):
+                    z = jnp.where(backward, planes - 1 - visit, visit)
+                    light, clear = absorb(padded, material, tables, z, row + part, clear, scale)
+                    for c in range(3):
+                        lit[c, z, pl.ds(to + part, SUBLANES), :] = light[c]
+                through[pl.ds(to + part, SUBLANES), :] = clear
         return carry
 
-    lax.fori_loop(0, rows // 2 // TILE, tile, 0)
+    lax.fori_loop(0, rows // 2 // TILE // 2, tile, 0)
 
 
 def local_give(padded, material, tables, flags, total_planes):
@@ -275,8 +286,14 @@
         padded[REACH + planes + layer, PAD : PAD + rows, :] = jnp.where(odd_z, second, first)
     side = jnp.bitwise_and(lane_index(), 3)
     for row in range(0, rows, SUBLANES):
-        first, second = ya[row : row + SUBLANES, :], yb[row : row + SUBLANES, :]
-        near = jnp.where((side < 2) == odd_y, first, second)
+        source = row % (rows // 2)
+        first, second = ya[source : source + SUBLANES, :], yb[source : source + SUBLANES, :]
+        from_low = jnp.where(odd_y, first, second)
+        from_high = jnp.where(odd_y, second, first)
+        if row >= rows // 2:
+            from_low = pltpu.roll(from_low, LANES - 2, 1)
+            from_high = pltpu.roll(from_high, 2, 1)
+        near = jnp.where(side < 2, from_low, from_high)
         ahead1, ahead2 = pltpu.roll(near, LANES - 1, 1), pltpu.roll(near, LANES - 2, 1)
         behind1, behind2 = pltpu.roll(near, 1, 1), pltpu.roll(near, 2, 1)
         edge[row : row + SUBLANES, :] = jnp.where(

time: 20.8 us -> 20.8 us (level)
    pallas_call x1, Pallas kernels: 2.47 us -> 2.26 us  [local_give(): pl.pallas_call(functools.partial(local_give_kernel, total_planes), out_sh...]
where the time goes in v6:
time: 20.8 us; the launch traced here: 20.6 us
  starting transfers between devices  10.5 us (50%)
  Pallas kernels  9.57 us (46%)
  waiting for transfers between devices  0.46 us (2%)
    ppermute x1, starting transfers between devices, shards(): yb = lax.ppermute(yb, 'by', pairs['by'][1])  4.33 us
    ppermute x1, starting transfers between devices, shards(): xb = lax.ppermute(xb, 'bx', pairs['bx'][1])  3.62 us
    pallas_call x1, Pallas kernels, shade_keep(): pl.pallas_call(functools.partial(keep_kernel, total_planes), out_shape=pl...  3.14 us
    pallas_call x1, Pallas kernels, local_give(): pl.pallas_call(functools.partial(local_give_kernel, total_planes), out_sh...  2.26 us
    pallas_call x1, Pallas kernels, shade_give(): pl.pallas_call(shade_give_kernel, out_shape=(shape(*padded.shape), shape(...  1.4 us
    ppermute x1, starting transfers between devices, shards(): za = lax.ppermute(za, 'bz', pairs['bz'][0])  1.25 us
    pallas_call x1, Pallas kernels, faces(): pl.pallas_call(functools.partial(early_kernel, counts), out_shape=(shape(...  1.18 us
    pallas_call x1, Pallas kernels, faces(): pl.pallas_call(pack_kernel, out_shape=(shape(planes + 2 * REACH, rows + 2...  0.91 us
  transfers between devices with their start and end apart: 6, of which 1 were waited for; matrix products, arithmetic and copies ran while one was open for 0% of the time, Pallas kernels for 31%

profile of v6, /device:TPU:9, one launch (start us, length us, event | category | flops | bytes accessed | tf_op | source)
XLA Modules:
  0.0 20.6 jit_solution(10432383506531874970)
XLA Ops:
  0.0 0.0 copy-start.1
  0.0 0.0 copy-start
  0.0 1.2 %early.1 = (f32[280,128]{1,0:T(8,128)S(1)}, f32[2,128,128]{2,1,0:T(8,128)S(1)}, f32[2,8,128]{2,1,0:T(8,128)S(1)}, s32[4,8,128]{2,1,0:T(8,128)S(1)}, f32[2,8,128]{2,1,0:T(8,128)S(1)}) custom-call(s32[1,1,2]{2,1,0:T(1,128)} %order.1, f32[32,128,128]{2,1,0:T(8,128)} %density.3, bf16[3,256]{1,0:T(4,128)(2,1)} %colors.1, bf16[256]{0:T(256)(128)(2,1)} %extinction.1), custom_call_target="tpu_custom_call" | custom-call | tf_op jit(solution)/shard_map/early/pallas_call | solution.py:122
  1.2 0.7 %collective-permute-start = (f32[280,128]{1,0:T(8,128)S(1)}, f32[280,128]{1,0:T(8,128)S(1)}, u32[]{:S(2)}, u32[]{:S(2)}) collective-permute-start(f32[280,128]{1,0:T(8,128)S(1)} %get-tuple-element.22), channel_id=1, source_target_pairs={{0,8},{8,0},{16,24},{24,16},{1,9},{9,1},{17,25},{25,17},{2,10},{10... | collective-permute-start | bytes 430088 | tf_op jit(solution)/shard_map/ppermute | solution.py:429
  1.9 1.3 %collective-permute-start.2 = (f32[2,128,128]{2,1,0:T(8,128)S(1)}, f32[2,128,128]{2,1,0:T(8,128)S(1)}, u32[]{:S(2)}, u32[]{:S(2)}) collective-permute-start(f32[2,128,128]{2,1,0:T(8,128)S(1)} %get-tuple-element.24), channel_id=1, source_target_pairs={{0,1},{1,0},{2,3},{3,2},{4,5},{5,4},{6,7},{7,6},{8,9},{9,8},{10,11... | collective-permute-start | bytes 393224 | tf_op jit(solution)/shard_map/ppermute | solution.py:431
  3.2 0.0 copy-done.1
  3.2 0.9 %pack.1 = (f32[36,144,128]{2,1,0:T(8,128)S(1)}, f32[80,128]{1,0:T(8,128)S(1)}, f32[64,128]{1,0:T(8,128)S(1)}, f32[72,128]{1,0:T(8,128)S(1)}) custom-call(f32[32,128,128]{2,1,0:T(8,128)S(1)} %copy-done.1), custom_call_target="tpu_custom_call" | custom-call | tf_op jit(solution)/shard_map/pack/pallas_call | solution.py:143
  4.1 0.2 %collective-permute-start.3 = (f32[80,128]{1,0:T(8,128)S(1)}, f32[80,128]{1,0:T(8,128)S(1)}, u32[]{:S(2)}, u32[]{:S(2)}) collective-permute-start(f32[80,128]{1,0:T(8,128)S(1)} %get-tuple-element.26), channel_id=1, source_target_pairs={{0,2},{2,0},{4,6},{6,4},{1,3},{3,1},{5,7},{7,5},{8,10},{10,8},{12,... | collective-permute-start | bytes 122888 | tf_op jit(solution)/shard_map/ppermute | solution.py:434
  4.3 3.6 %collective-permute-start.1 = (f32[72,128]{1,0:T(8,128)S(1)}, f32[72,128]{1,0:T(8,128)S(1)}, u32[]{:S(2)}, u32[]{:S(2)}) collective-permute-start(f32[72,128]{1,0:T(8,128)S(1)} %get-tuple-element.23), channel_id=1, source_target_pairs={{8,16},{16,8},{9,17},{17,9},{10,18},{18,10},{11,19},{19,11},{12,20... | collective-permute-start | bytes 110600 | tf_op jit(solution)/shard_map/ppermute | solution.py:430
  8.0 4.3 %collective-permute-start.4 = (f32[64,128]{1,0:T(8,128)S(1)}, f32[64,128]{1,0:T(8,128)S(1)}, u32[]{:S(2)}, u32[]{:S(2)}) collective-permute-start(f32[64,128]{1,0:T(8,128)S(1)} %get-tuple-element.27), channel_id=1, source_target_pairs={{2,4},{4,2},{3,5},{5,3},{10,12},{12,10},{11,13},{13,11},{18,20},{2... | collective-permute-start | bytes 98312 | tf_op jit(solution)/shard_map/ppermute | solution.py:435
  12.3 0.0 copy-done
  12.3 2.3 %local_give.1 = (f32[3,32,64,128]{3,2,1,0:T(8,128)S(1)}, f32[32,64,128]{2,1,0:T(8,128)S(1)}, f32[64,128]{1,0:T(8,128)S(1)}) custom-call(f32[36,144,128]{2,1,0:T(8,128)S(1)} %get-tuple-element.21.padded.padded_in, s32[32,128,128]{2,1,0:T(8,128)S(1)} %copy-done, s32[4,8,128]{2,1,0:T(8,128)S(1)} %get-tuple-element.28.tables, ...), custom_call_target="tpu_custom_call" | custom-call | flops 10485760 | bytes 4194304 | tf_op jit(solution)/shard_map/local_give/pallas_call | solution.py:257
  14.6 0.0 collective-permute-done.4.yb
  14.6 0.0 collective-permute-done.1.xb
  14.6 0.0 collective-permute-done.3.ya
  14.6 0.0 collective-permute-done.2.za
  14.6 0.0 collective-permute-done.xa
  14.6 1.4 %shade_give.1 = (f32[36,144,128]{2,1,0:T(8,128)S(1)}, f32[128,128]{1,0:T(8,128)S(1)}, f32[4,64,128]{2,1,0:T(8,128)S(1)}) custom-call(f32[36,144,128]{2,1,0:T(8,128)S(1)} %get-tuple-element.21.padded.padded_in, f32[280,128]{1,0:T(8,128)S(1)} %collective-permute-done.xa, f32[72,128]{1,0:T(8,128)S(1)} %collective-permute-done.1.xb, ...), custom_call_target="tpu_custom_call", output_to_operand_aliasing={{0}: (0, {})} | custom-call | tf_op jit(solution)/shard_map/shade_give/pallas_call | solution.py:339
  16.0 0.3 %collective-permute-start.5 = (f32[4,64,128]{2,1,0:T(8,128)S(1)}, f32[4,64,128]{2,1,0:T(8,128)S(1)}, u32[]{:S(2)}, u32[]{:S(2)}) collective-permute-start(f32[4,64,128]{2,1,0:T(8,128)S(1)} %get-tuple-element.34), channel_id=1, source_target_pairs={{0,1},{1,0},{2,3},{3,2},{4,5},{5,4},{6,7},{7,6},{8,9},{9,8},{10,11... | collective-permute-start | bytes 393224 | tf_op jit(solution)/shard_map/ppermute | solution.py:445
  16.3 3.1 %keep.1.mine = f32[4,64,128]{2,1,0:T(8,128)S(1)} custom-call(f32[36,144,128]{2,1,0:T(8,128)S(1)} %get-tuple-element.32.padded, f32[128,128]{1,0:T(8,128)S(1)} %get-tuple-element.33.edge, s32[32,128,128]{2,1,0:T(8,128)S(1)} %copy-done, s32[4,8,128]{2,1,0:T(8,128)S(1)} %get-tuple-element.28.tables, f32[2,8,128]{2,1,0:T(8,128)S(1)} %get-tuple-element.20.flags), custom_call_target="tpu_custom_call" | custom-call | flops 20971520 | bytes 4194304 | tf_op jit(solution)/shard_map/keep/pallas_call | solution.py:382
  19.5 0.4 %collective-permute-done.5.other = f32[4,64,128]{2,1,0:T(8,128)S(1)} collective-permute-done((f32[4,64,128]{2,1,0:T(8,128)S(1)}, f32[4,64,128]{2,1,0:T(8,128)S(1)}, u32[]{:S(2)}, u32[]{:S(2)}) %collective-permute-start.5) | collective-permute-done | bytes 131104 | tf_op jit(solution)/shard_map/ppermute | solution.py:445
  19.9 0.7 %blend.1 = f32[4,64,128]{2,1,0:T(8,128)} custom-call(f32[2,8,128]{2,1,0:T(8,128)S(1)} %get-tuple-element.20.flags, f32[4,64,128]{2,1,0:T(8,128)S(1)} %keep.1.mine, f32[4,64,128]{2,1,0:T(8,128)S(1)} %collective-permute-done.5.other), custom_call_target="tpu_custom_call" | custom-call | tf_op jit(solution)/shard_map/blend/pallas_call | solution.py:411
Async XLA Ops:
  0.0 3.2 %copy-start.1 = (f32[32,128,128]{2,1,0:T(8,128)S(1)}, f32[32,128,128]{2,1,0:T(8,128)}, u32[]{:S(2)}) copy-start(f32[32,128,128]{2,1,0:T(8,128)} %density.3) | copy-start | bytes 6291460
  0.0 12.3 %copy-start = (s32[32,128,128]{2,1,0:T(8,128)S(1)}, s32[32,128,128]{2,1,0:T(8,128)}, u32[]{:S(2)}) copy-start(s32[32,128,128]{2,1,0:T(8,128)} %material.3) | copy-start | bytes 6291460
  1.2 13.4 %collective-permute-start = (f32[280,128]{1,0:T(8,128)S(1)}, f32[280,128]{1,0:T(8,128)S(1)}, u32[]{:S(2)}, u32[]{:S(2)}) collective-permute-start(f32[280,128]{1,0:T(8,128)S(1)} %get-tuple-element.22), channel_id=1, source_target_pairs={{0,8},{8,0},{16,24},{24,16},{1,9},{9,1},{17,25},{25,17},{2,10},{10... | collective-permute-start | bytes 430088 | tf_op jit(solution)/shard_map/ppermute | solution.py:429
  1.9 12.7 %collective-permute-start.2 = (f32[2,128,128]{2,1,0:T(8,128)S(1)}, f32[2,128,128]{2,1,0:T(8,128)S(1)}, u32[]{:S(2)}, u32[]{:S(2)}) collective-permute-start(f32[2,128,128]{2,1,0:T(8,128)S(1)} %get-tuple-element.24), channel_id=1, source_target_pairs={{0,1},{1,0},{2,3},{3,2},{4,5},{5,4},{6,7},{7,6},{8,9},{9,8},{10,11... | collective-permute-start | bytes 393224 | tf_op jit(solution)/shard_map/ppermute | solution.py:431
  4.1 10.5 %collective-permute-start.3 = (f32[80,128]{1,0:T(8,128)S(1)}, f32[80,128]{1,0:T(8,128)S(1)}, u32[]{:S(2)}, u32[]{:S(2)}) collective-permute-start(f32[80,128]{1,0:T(8,128)S(1)} %get-tuple-element.26), channel_id=1, source_target_pairs={{0,2},{2,0},{4,6},{6,4},{1,3},{3,1},{5,7},{7,5},{8,10},{10,8},{12,... | collective-permute-start | bytes 122888 | tf_op jit(solution)/shard_map/ppermute | solution.py:434
  4.3 10.3 %collective-permute-start.1 = (f32[72,128]{1,0:T(8,128)S(1)}, f32[72,128]{1,0:T(8,128)S(1)}, u32[]{:S(2)}, u32[]{:S(2)}) collective-permute-start(f32[72,128]{1,0:T(8,128)S(1)} %get-tuple-element.23), channel_id=1, source_target_pairs={{8,16},{16,8},{9,17},{17,9},{10,18},{18,10},{11,19},{19,11},{12,20... | collective-permute-start | bytes 110600 | tf_op jit(solution)/shard_map/ppermute | solution.py:430
  8.0 6.6 %collective-permute-start.4 = (f32[64,128]{1,0:T(8,128)S(1)}, f32[64,128]{1,0:T(8,128)S(1)}, u32[]{:S(2)}, u32[]{:S(2)}) collective-permute-start(f32[64,128]{1,0:T(8,128)S(1)} %get-tuple-element.27), channel_id=1, source_target_pairs={{2,4},{4,2},{3,5},{5,3},{10,12},{12,10},{11,13},{13,11},{18,20},{2... | collective-permute-start | bytes 98312 | tf_op jit(solution)/shard_map/ppermute | solution.py:435
  16.0 3.9 %collective-permute-start.5 = (f32[4,64,128]{2,1,0:T(8,128)S(1)}, f32[4,64,128]{2,1,0:T(8,128)S(1)}, u32[]{:S(2)}, u32[]{:S(2)}) collective-permute-start(f32[4,64,128]{2,1,0:T(8,128)S(1)} %get-tuple-element.34), channel_id=1, source_target_pairs={{0,1},{1,0},{2,3},{3,2},{4,5},{5,4},{6,7},{7,6},{8,9},{9,8},{10,11... | collective-permute-start | bytes 393224 | tf_op jit(solution)/shard_map/ppermute | solution.py:445

commit v7 on v6

--- a/solution.py
+++ b/solution.py
@@ -29,9 +29,11 @@
     return jnp.bitwise_and(lax.axis_index(axis), 1) == 1
 
 
-def swaps(count):
+def swaps(count, closed=False):
     first = [(i, i ^ 1) for i in range(count)]
     second = [(i, i + 1 if i % 2 else i - 1) for i in range(1, count - 1)]
+    if closed:
+        second = [(0, count - 1)] + second + [(count - 1, 0)]
     return first, second
 
 
@@ -275,8 +277,11 @@
 
 def put_halo(padded, xa, xb, za, zb, ya, yb, edge, planes, rows):
     odd_x, odd_y, odd_z = is_odd("bx"), is_odd("by"), is_odd("bz")
+    place_x = lax.axis_index("bx")
+    end_x = jnp.logical_or(place_x == 0, place_x == lax.axis_size("bx") - 1)
     for z in range(planes):
         first, second = xa[REACH * z : REACH * (z + 1), :], xb[REACH * z : REACH * (z + 1), :]
+        second = jnp.where(end_x, 0.0, second)
         padded[REACH + z, PAD - REACH : PAD, :] = jnp.where(odd_x, first, second)
         padded[REACH + z, PAD + rows : PAD + rows + REACH, :] = jnp.where(odd_x, second, first)
     for layer in range(REACH):
@@ -425,7 +430,7 @@
     padded, ya, yb, xa, xb, za, zb, tables, flags = faces(
         order, density, color_table, extinction_table, counts
     )
-    pairs = {axis: swaps(counts[axis]) for axis in counts}
+    pairs = {axis: swaps(counts[axis], axis == "bx") for axis in counts}
     xa = lax.ppermute(xa, "bx", pairs["bx"][0])
     xb = lax.ppermute(xb, "bx", pairs["bx"][1])
     za = lax.ppermute(za, "bz", pairs["bz"][0])

time: 20.8 us -> 20.3 us (0.976)
  the two profiles are of different devices: /device:TPU:9 before, /device:TPU:8 now
where the time goes in v7:
time: 20.3 us; the launch traced here: 20.1 us
  Pallas kernels  9.58 us (47%)
  starting transfers between devices  8.33 us (41%)
  waiting for transfers between devices  2.11 us (10%)
    ppermute x1, starting transfers between devices, shards(): yb = lax.ppermute(yb, 'by', pairs['by'][1])  4.6 us
    pallas_call x1, Pallas kernels, shade_keep(): pl.pallas_call(functools.partial(keep_kernel, total_planes), out_shape=pl...  3.14 us
    pallas_call x1, Pallas kernels, local_give(): pl.pallas_call(functools.partial(local_give_kernel, total_planes), out_sh...  2.26 us
    ppermute x1, waiting for transfers between devices, shards(): received = lax.ppermute(give, 'bz', flip)  2.09 us
    ppermute x1, starting transfers between devices, shards(): za = lax.ppermute(za, 'bz', pairs['bz'][0])  1.58 us
    pallas_call x1, Pallas kernels, shade_give(): pl.pallas_call(shade_give_kernel, out_shape=(shape(*padded.shape), shape(...  1.41 us
    pallas_call x1, Pallas kernels, faces(): pl.pallas_call(functools.partial(early_kernel, counts), out_shape=(shape(...  1.18 us
    ppermute x1, starting transfers between devices, shards(): xb = lax.ppermute(xb, 'bx', pairs['bx'][1])  0.98 us
  transfers between devices with their start and end apart: 6, of which 1 were waited for; matrix products, arithmetic and copies ran while one was open for 0% of the time, Pallas kernels for 31%

profile of v7, /device:TPU:8, one launch (start us, length us, event | category | flops | bytes accessed | tf_op | source)
XLA Modules:
  0.0 20.1 jit_solution(10944644154961300451)
XLA Ops:
  0.0 0.0 copy-start.1
  0.0 0.0 copy-start
  0.0 1.2 %early.1 = (f32[280,128]{1,0:T(8,128)S(1)}, f32[2,128,128]{2,1,0:T(8,128)S(1)}, f32[2,8,128]{2,1,0:T(8,128)S(1)}, s32[4,8,128]{2,1,0:T(8,128)S(1)}, f32[2,8,128]{2,1,0:T(8,128)S(1)}) custom-call(s32[1,1,2]{2,1,0:T(1,128)} %order.1, f32[32,128,128]{2,1,0:T(8,128)} %density.3, bf16[3,256]{1,0:T(4,128)(2,1)} %colors.1, bf16[256]{0:T(256)(128)(2,1)} %extinction.1), custom_call_target="tpu_custom_call" | custom-call | tf_op jit(solution)/shard_map/early/pallas_call | solution.py:124
  1.2 0.1 collective-permute-start
  1.3 1.6 %collective-permute-start.2 = (f32[2,128,128]{2,1,0:T(8,128)S(1)}, f32[2,128,128]{2,1,0:T(8,128)S(1)}, u32[]{:S(2)}, u32[]{:S(2)}) collective-permute-start(f32[2,128,128]{2,1,0:T(8,128)S(1)} %get-tuple-element.24), channel_id=1, source_target_pairs={{0,1},{1,0},{2,3},{3,2},{4,5},{5,4},{6,7},{7,6},{8,9},{9,8},{10,11... | collective-permute-start | bytes 393224 | tf_op jit(solution)/shard_map/ppermute | solution.py:436
  2.9 0.0 copy-done.1
  2.9 0.9 %pack.1 = (f32[36,144,128]{2,1,0:T(8,128)S(1)}, f32[80,128]{1,0:T(8,128)S(1)}, f32[64,128]{1,0:T(8,128)S(1)}, f32[72,128]{1,0:T(8,128)S(1)}) custom-call(f32[32,128,128]{2,1,0:T(8,128)S(1)} %copy-done.1), custom_call_target="tpu_custom_call" | custom-call | tf_op jit(solution)/shard_map/pack/pallas_call | solution.py:145
  3.8 0.5 %collective-permute-start.3 = (f32[80,128]{1,0:T(8,128)S(1)}, f32[80,128]{1,0:T(8,128)S(1)}, u32[]{:S(2)}, u32[]{:S(2)}) collective-permute-start(f32[80,128]{1,0:T(8,128)S(1)} %get-tuple-element.26), channel_id=1, source_target_pairs={{0,2},{2,0},{4,6},{6,4},{1,3},{3,1},{5,7},{7,5},{8,10},{10,8},{12,... | collective-permute-start | bytes 122888 | tf_op jit(solution)/shard_map/ppermute | solution.py:439
  4.3 1.0 %collective-permute-start.1 = (f32[72,128]{1,0:T(8,128)S(1)}, f32[72,128]{1,0:T(8,128)S(1)}, u32[]{:S(2)}, u32[]{:S(2)}) collective-permute-start(f32[72,128]{1,0:T(8,128)S(1)} %get-tuple-element.23), channel_id=1, source_target_pairs={{0,24},{8,16},{16,8},{24,0},{1,25},{9,17},{17,9},{25,1},{2,26},{10... | collective-permute-start | bytes 110600 | tf_op jit(solution)/shard_map/ppermute | solution.py:435
  5.3 4.6 %collective-permute-start.4 = (f32[64,128]{1,0:T(8,128)S(1)}, f32[64,128]{1,0:T(8,128)S(1)}, u32[]{:S(2)}, u32[]{:S(2)}) collective-permute-start(f32[64,128]{1,0:T(8,128)S(1)} %get-tuple-element.27), channel_id=1, source_target_pairs={{2,4},{4,2},{3,5},{5,3},{10,12},{12,10},{11,13},{13,11},{18,20},{2... | collective-permute-start | bytes 98312 | tf_op jit(solution)/shard_map/ppermute | solution.py:440
  9.9 0.0 copy-done
  9.9 2.3 %local_give.1 = (f32[3,32,64,128]{3,2,1,0:T(8,128)S(1)}, f32[32,64,128]{2,1,0:T(8,128)S(1)}, f32[64,128]{1,0:T(8,128)S(1)}) custom-call(f32[36,144,128]{2,1,0:T(8,128)S(1)} %get-tuple-element.21.padded.padded_in, s32[32,128,128]{2,1,0:T(8,128)S(1)} %copy-done, s32[4,8,128]{2,1,0:T(8,128)S(1)} %get-tuple-element.28.tables, ...), custom_call_target="tpu_custom_call" | custom-call | flops 10485760 | bytes 4194304 | tf_op jit(solution)/shard_map/local_give/pallas_call | solution.py:259
  12.2 0.0 collective-permute-done.4.yb
  12.2 0.0 collective-permute-done.1.xb
  12.2 0.0 collective-permute-done.3.ya
  12.2 0.0 collective-permute-done.2.za
  12.2 0.0 collective-permute-done.xa
  12.2 1.4 %shade_give.1 = (f32[36,144,128]{2,1,0:T(8,128)S(1)}, f32[128,128]{1,0:T(8,128)S(1)}, f32[4,64,128]{2,1,0:T(8,128)S(1)}) custom-call(f32[36,144,128]{2,1,0:T(8,128)S(1)} %get-tuple-element.21.padded.padded_in, f32[280,128]{1,0:T(8,128)S(1)} %collective-permute-done.xa, f32[72,128]{1,0:T(8,128)S(1)} %collective-permute-done.1.xb, ...), custom_call_target="tpu_custom_call", output_to_operand_aliasing={{0}: (0, {})} | custom-call | tf_op jit(solution)/shard_map/shade_give/pallas_call | solution.py:344
  13.6 0.6 %collective-permute-start.5 = (f32[4,64,128]{2,1,0:T(8,128)S(1)}, f32[4,64,128]{2,1,0:T(8,128)S(1)}, u32[]{:S(2)}, u32[]{:S(2)}) collective-permute-start(f32[4,64,128]{2,1,0:T(8,128)S(1)} %get-tuple-element.34), channel_id=1, source_target_pairs={{0,1},{1,0},{2,3},{3,2},{4,5},{5,4},{6,7},{7,6},{8,9},{9,8},{10,11... | collective-permute-start | bytes 393224 | tf_op jit(solution)/shard_map/ppermute | solution.py:450
  14.2 3.1 %keep.1.mine = f32[4,64,128]{2,1,0:T(8,128)S(1)} custom-call(f32[36,144,128]{2,1,0:T(8,128)S(1)} %get-tuple-element.32.padded, f32[128,128]{1,0:T(8,128)S(1)} %get-tuple-element.33.edge, s32[32,128,128]{2,1,0:T(8,128)S(1)} %copy-done, s32[4,8,128]{2,1,0:T(8,128)S(1)} %get-tuple-element.28.tables, f32[2,8,128]{2,1,0:T(8,128)S(1)} %get-tuple-element.20.flags), custom_call_target="tpu_custom_call" | custom-call | flops 20971520 | bytes 4194304 | tf_op jit(solution)/shard_map/keep/pallas_call | solution.py:387
  17.3 2.1 %collective-permute-done.5.other = f32[4,64,128]{2,1,0:T(8,128)S(1)} collective-permute-done((f32[4,64,128]{2,1,0:T(8,128)S(1)}, f32[4,64,128]{2,1,0:T(8,128)S(1)}, u32[]{:S(2)}, u32[]{:S(2)}) %collective-permute-start.5) | collective-permute-done | bytes 131104 | tf_op jit(solution)/shard_map/ppermute | solution.py:450
  19.4 0.7 %blend.1 = f32[4,64,128]{2,1,0:T(8,128)} custom-call(f32[2,8,128]{2,1,0:T(8,128)S(1)} %get-tuple-element.20.flags, f32[4,64,128]{2,1,0:T(8,128)S(1)} %keep.1.mine, f32[4,64,128]{2,1,0:T(8,128)S(1)} %collective-permute-done.5.other), custom_call_target="tpu_custom_call" | custom-call | tf_op jit(solution)/shard_map/blend/pallas_call | solution.py:416
Async XLA Ops:
  0.0 2.9 %copy-start.1 = (f32[32,128,128]{2,1,0:T(8,128)S(1)}, f32[32,128,128]{2,1,0:T(8,128)}, u32[]{:S(2)}) copy-start(f32[32,128,128]{2,1,0:T(8,128)} %density.3) | copy-start | bytes 6291460
  0.0 9.9 %copy-start = (s32[32,128,128]{2,1,0:T(8,128)S(1)}, s32[32,128,128]{2,1,0:T(8,128)}, u32[]{:S(2)}) copy-start(s32[32,128,128]{2,1,0:T(8,128)} %material.3) | copy-start | bytes 6291460
  1.2 11.0 %collective-permute-start = (f32[280,128]{1,0:T(8,128)S(1)}, f32[280,128]{1,0:T(8,128)S(1)}, u32[]{:S(2)}, u32[]{:S(2)}) collective-permute-start(f32[280,128]{1,0:T(8,128)S(1)} %get-tuple-element.22), channel_id=1, source_target_pairs={{0,8},{8,0},{16,24},{24,16},{1,9},{9,1},{17,25},{25,17},{2,10},{10... | collective-permute-start | bytes 430088 | tf_op jit(solution)/shard_map/ppermute | solution.py:434
  1.3 10.9 %collective-permute-start.2 = (f32[2,128,128]{2,1,0:T(8,128)S(1)}, f32[2,128,128]{2,1,0:T(8,128)S(1)}, u32[]{:S(2)}, u32[]{:S(2)}) collective-permute-start(f32[2,128,128]{2,1,0:T(8,128)S(1)} %get-tuple-element.24), channel_id=1, source_target_pairs={{0,1},{1,0},{2,3},{3,2},{4,5},{5,4},{6,7},{7,6},{8,9},{9,8},{10,11... | collective-permute-start | bytes 393224 | tf_op jit(solution)/shard_map/ppermute | solution.py:436
  3.8 8.4 %collective-permute-start.3 = (f32[80,128]{1,0:T(8,128)S(1)}, f32[80,128]{1,0:T(8,128)S(1)}, u32[]{:S(2)}, u32[]{:S(2)}) collective-permute-start(f32[80,128]{1,0:T(8,128)S(1)} %get-tuple-element.26), channel_id=1, source_target_pairs={{0,2},{2,0},{4,6},{6,4},{1,3},{3,1},{5,7},{7,5},{8,10},{10,8},{12,... | collective-permute-start | bytes 122888 | tf_op jit(solution)/shard_map/ppermute | solution.py:439
  4.3 7.9 %collective-permute-start.1 = (f32[72,128]{1,0:T(8,128)S(1)}, f32[72,128]{1,0:T(8,128)S(1)}, u32[]{:S(2)}, u32[]{:S(2)}) collective-permute-start(f32[72,128]{1,0:T(8,128)S(1)} %get-tuple-element.23), channel_id=1, source_target_pairs={{0,24},{8,16},{16,8},{24,0},{1,25},{9,17},{17,9},{25,1},{2,26},{10... | collective-permute-start | bytes 110600 | tf_op jit(solution)/shard_map/ppermute | solution.py:435
  5.3 6.9 %collective-permute-start.4 = (f32[64,128]{1,0:T(8,128)S(1)}, f32[64,128]{1,0:T(8,128)S(1)}, u32[]{:S(2)}, u32[]{:S(2)}) collective-permute-start(f32[64,128]{1,0:T(8,128)S(1)} %get-tuple-element.27), channel_id=1, source_target_pairs={{2,4},{4,2},{3,5},{5,3},{10,12},{12,10},{11,13},{13,11},{18,20},{2... | collective-permute-start | bytes 98312 | tf_op jit(solution)/shard_map/ppermute | solution.py:440
  13.6 5.8 %collective-permute-start.5 = (f32[4,64,128]{2,1,0:T(8,128)S(1)}, f32[4,64,128]{2,1,0:T(8,128)S(1)}, u32[]{:S(2)}, u32[]{:S(2)}) collective-permute-start(f32[4,64,128]{2,1,0:T(8,128)S(1)} %get-tuple-element.34), channel_id=1, source_target_pairs={{0,1},{1,0},{2,3},{3,2},{4,5},{5,4},{6,7},{7,6},{8,9},{9,8},{10,11... | collective-permute-start | bytes 393224 | tf_op jit(solution)/shard_map/ppermute | solution.py:450

commit v8 on v7

--- a/solution.py
+++ b/solution.py
@@ -148,7 +148,7 @@
             shape(planes + 2 * REACH, rows + 2 * PAD, cols),
             shape(size + 16, LANES),
             shape(size, LANES),
-            shape(size + 8, cols),
+            shape(size + 24, cols),
         ),
         in_specs=[VMEM],
         out_specs=(VMEM,) * 4,

time: 20.3 us -> 20 us (0.985)
  waiting for transfers between devices: 2.11 us -> 1.55 us
  starting transfers between devices: 8.33 us -> 8.6 us
    ppermute x1, waiting for transfers between devices: 2.09 us -> 1.53 us  [shards(): received = lax.ppermute(give, 'bz', flip)]
    ppermute x1, starting transfers between devices: 0.98 us -> 1.33 us  [shards(): xb = lax.ppermute(xb, 'bx', pairs['bx'][1])]
  transfers between devices with their start and end apart: 6 -> 6, of which waited for: 1 -> 1; matrix products, arithmetic and copies ran while one was open for 0% -> 0% of each run, Pallas kernels for 31% -> 32%
where the time goes in v8:
time: 20 us; the launch traced here: 19.8 us
  Pallas kernels  9.56 us (48%)
  starting transfers between devices  8.6 us (43%)
  waiting for transfers between devices  1.55 us (8%)
    ppermute x1, starting transfers between devices, shards(): yb = lax.ppermute(yb, 'by', pairs['by'][1])  4.6 us
    pallas_call x1, Pallas kernels, shade_keep(): pl.pallas_call(functools.partial(keep_kernel, total_planes), out_shape=pl...  3.14 us
    pallas_call x1, Pallas kernels, local_give(): pl.pallas_call(functools.partial(local_give_kernel, total_planes), out_sh...  2.26 us
    ppermute x1, starting transfers between devices, shards(): za = lax.ppermute(za, 'bz', pairs['bz'][0])  1.58 us
    ppermute x1, waiting for transfers between devices, shards(): received = lax.ppermute(give, 'bz', flip)  1.53 us
    pallas_call x1, Pallas kernels, shade_give(): pl.pallas_call(shade_give_kernel, out_shape=(shape(*padded.shape), shape(...  1.38 us
    ppermute x1, starting transfers between devices, shards(): xb = lax.ppermute(xb, 'bx', pairs['bx'][1])  1.33 us
    pallas_call x1, Pallas kernels, faces(): pl.pallas_call(functools.partial(early_kernel, counts), out_shape=(shape(...  1.18 us
  transfers between devices with their start and end apart: 6, of which 1 were waited for; matrix products, arithmetic and copies ran while one was open for 0% of the time, Pallas kernels for 32%

profile of v8, /device:TPU:8, one launch (start us, length us, event | category | flops | bytes accessed | tf_op | source)
XLA Modules:
  0.0 19.8 jit_solution(6841416164605505953)
XLA Ops:
  0.0 0.0 copy-start.1
  0.0 0.0 copy-start
  0.0 1.2 %early.1 = (f32[280,128]{1,0:T(8,128)S(1)}, f32[2,128,128]{2,1,0:T(8,128)S(1)}, f32[2,8,128]{2,1,0:T(8,128)S(1)}, s32[4,8,128]{2,1,0:T(8,128)S(1)}, f32[2,8,128]{2,1,0:T(8,128)S(1)}) custom-call(s32[1,1,2]{2,1,0:T(1,128)} %order.1, f32[32,128,128]{2,1,0:T(8,128)} %density.3, bf16[3,256]{1,0:T(4,128)(2,1)} %colors.1, bf16[256]{0:T(256)(128)(2,1)} %extinction.1), custom_call_target="tpu_custom_call" | custom-call | tf_op jit(solution)/shard_map/early/pallas_call | solution.py:124
  1.2 0.1 collective-permute-start
  1.3 1.6 %collective-permute-start.2 = (f32[2,128,128]{2,1,0:T(8,128)S(1)}, f32[2,128,128]{2,1,0:T(8,128)S(1)}, u32[]{:S(2)}, u32[]{:S(2)}) collective-permute-start(f32[2,128,128]{2,1,0:T(8,128)S(1)} %get-tuple-element.24), channel_id=1, source_target_pairs={{0,1},{1,0},{2,3},{3,2},{4,5},{5,4},{6,7},{7,6},{8,9},{9,8},{10,11... | collective-permute-start | bytes 393224 | tf_op jit(solution)/shard_map/ppermute | solution.py:436
  2.9 0.0 copy-done.1
  2.9 0.9 %pack.1 = (f32[36,144,128]{2,1,0:T(8,128)S(1)}, f32[80,128]{1,0:T(8,128)S(1)}, f32[64,128]{1,0:T(8,128)S(1)}, f32[88,128]{1,0:T(8,128)S(1)}) custom-call(f32[32,128,128]{2,1,0:T(8,128)S(1)} %copy-done.1), custom_call_target="tpu_custom_call" | custom-call | tf_op jit(solution)/shard_map/pack/pallas_call | solution.py:145
  3.8 1.3 %collective-permute-start.1 = (f32[88,128]{1,0:T(8,128)S(1)}, f32[88,128]{1,0:T(8,128)S(1)}, u32[]{:S(2)}, u32[]{:S(2)}) collective-permute-start(f32[88,128]{1,0:T(8,128)S(1)} %get-tuple-element.23), channel_id=1, source_target_pairs={{0,24},{8,16},{16,8},{24,0},{1,25},{9,17},{17,9},{25,1},{2,26},{10... | collective-permute-start | bytes 135176 | tf_op jit(solution)/shard_map/ppermute | solution.py:435
  5.1 0.4 %collective-permute-start.3 = (f32[80,128]{1,0:T(8,128)S(1)}, f32[80,128]{1,0:T(8,128)S(1)}, u32[]{:S(2)}, u32[]{:S(2)}) collective-permute-start(f32[80,128]{1,0:T(8,128)S(1)} %get-tuple-element.26), channel_id=1, source_target_pairs={{0,2},{2,0},{4,6},{6,4},{1,3},{3,1},{5,7},{7,5},{8,10},{10,8},{12,... | collective-permute-start | bytes 122888 | tf_op jit(solution)/shard_map/ppermute | solution.py:439
  5.6 4.6 %collective-permute-start.4 = (f32[64,128]{1,0:T(8,128)S(1)}, f32[64,128]{1,0:T(8,128)S(1)}, u32[]{:S(2)}, u32[]{:S(2)}) collective-permute-start(f32[64,128]{1,0:T(8,128)S(1)} %get-tuple-element.27), channel_id=1, source_target_pairs={{2,4},{4,2},{3,5},{5,3},{10,12},{12,10},{11,13},{13,11},{18,20},{2... | collective-permute-start | bytes 98312 | tf_op jit(solution)/shard_map/ppermute | solution.py:440
  10.2 0.0 copy-done
  10.2 2.3 %local_give.1 = (f32[3,32,64,128]{3,2,1,0:T(8,128)S(1)}, f32[32,64,128]{2,1,0:T(8,128)S(1)}, f32[64,128]{1,0:T(8,128)S(1)}) custom-call(f32[36,144,128]{2,1,0:T(8,128)S(1)} %get-tuple-element.21.padded.padded_in, s32[32,128,128]{2,1,0:T(8,128)S(1)} %copy-done, s32[4,8,128]{2,1,0:T(8,128)S(1)} %get-tuple-element.28.tables, ...), custom_call_target="tpu_custom_call" | custom-call | flops 10485760 | bytes 4194304 | tf_op jit(solution)/shard_map/local_give/pallas_call | solution.py:259
  12.4 0.0 collective-permute-done.4.yb
  12.5 0.0 collective-permute-done.3.ya
  12.5 0.0 collective-permute-done.1.xb
  12.5 0.0 collective-permute-done.2.za
  12.5 0.0 collective-permute-done.xa
  12.5 1.4 %shade_give.1 = (f32[36,144,128]{2,1,0:T(8,128)S(1)}, f32[128,128]{1,0:T(8,128)S(1)}, f32[4,64,128]{2,1,0:T(8,128)S(1)}) custom-call(f32[36,144,128]{2,1,0:T(8,128)S(1)} %get-tuple-element.21.padded.padded_in, f32[280,128]{1,0:T(8,128)S(1)} %collective-permute-done.xa, f32[88,128]{1,0:T(8,128)S(1)} %collective-permute-done.1.xb, ...), custom_call_target="tpu_custom_call", output_to_operand_aliasing={{0}: (0, {})} | custom-call | tf_op jit(solution)/shard_map/shade_give/pallas_call | solution.py:344
  13.9 0.6 %collective-permute-start.5 = (f32[4,64,128]{2,1,0:T(8,128)S(1)}, f32[4,64,128]{2,1,0:T(8,128)S(1)}, u32[]{:S(2)}, u32[]{:S(2)}) collective-permute-start(f32[4,64,128]{2,1,0:T(8,128)S(1)} %get-tuple-element.34), channel_id=1, source_target_pairs={{0,1},{1,0},{2,3},{3,2},{4,5},{5,4},{6,7},{7,6},{8,9},{9,8},{10,11... | collective-permute-start | bytes 393224 | tf_op jit(solution)/shard_map/ppermute | solution.py:450
  14.5 3.1 %keep.1.mine = f32[4,64,128]{2,1,0:T(8,128)S(1)} custom-call(f32[36,144,128]{2,1,0:T(8,128)S(1)} %get-tuple-element.32.padded, f32[128,128]{1,0:T(8,128)S(1)} %get-tuple-element.33.edge, s32[32,128,128]{2,1,0:T(8,128)S(1)} %copy-done, s32[4,8,128]{2,1,0:T(8,128)S(1)} %get-tuple-element.28.tables, f32[2,8,128]{2,1,0:T(8,128)S(1)} %get-tuple-element.20.flags), custom_call_target="tpu_custom_call" | custom-call | flops 20971520 | bytes 4194304 | tf_op jit(solution)/shard_map/keep/pallas_call | solution.py:387
  17.6 1.5 %collective-permute-done.5.other = f32[4,64,128]{2,1,0:T(8,128)S(1)} collective-permute-done((f32[4,64,128]{2,1,0:T(8,128)S(1)}, f32[4,64,128]{2,1,0:T(8,128)S(1)}, u32[]{:S(2)}, u32[]{:S(2)}) %collective-permute-start.5) | collective-permute-done | bytes 131104 | tf_op jit(solution)/shard_map/ppermute | solution.py:450
  19.1 0.7 %blend.1 = f32[4,64,128]{2,1,0:T(8,128)} custom-call(f32[2,8,128]{2,1,0:T(8,128)S(1)} %get-tuple-element.20.flags, f32[4,64,128]{2,1,0:T(8,128)S(1)} %keep.1.mine, f32[4,64,128]{2,1,0:T(8,128)S(1)} %collective-permute-done.5.other), custom_call_target="tpu_custom_call" | custom-call | tf_op jit(solution)/shard_map/blend/pallas_call | solution.py:416
Async XLA Ops:
  0.0 2.9 %copy-start.1 = (f32[32,128,128]{2,1,0:T(8,128)S(1)}, f32[32,128,128]{2,1,0:T(8,128)}, u32[]{:S(2)}) copy-start(f32[32,128,128]{2,1,0:T(8,128)} %density.3) | copy-start | bytes 6291460
  0.0 10.2 %copy-start = (s32[32,128,128]{2,1,0:T(8,128)S(1)}, s32[32,128,128]{2,1,0:T(8,128)}, u32[]{:S(2)}) copy-start(s32[32,128,128]{2,1,0:T(8,128)} %material.3) | copy-start | bytes 6291460
  1.2 11.3 %collective-permute-start = (f32[280,128]{1,0:T(8,128)S(1)}, f32[280,128]{1,0:T(8,128)S(1)}, u32[]{:S(2)}, u32[]{:S(2)}) collective-permute-start(f32[280,128]{1,0:T(8,128)S(1)} %get-tuple-element.22), channel_id=1, source_target_pairs={{0,8},{8,0},{16,24},{24,16},{1,9},{9,1},{17,25},{25,17},{2,10},{10... | collective-permute-start | bytes 430088 | tf_op jit(solution)/shard_map/ppermute | solution.py:434
  1.3 11.2 %collective-permute-start.2 = (f32[2,128,128]{2,1,0:T(8,128)S(1)}, f32[2,128,128]{2,1,0:T(8,128)S(1)}, u32[]{:S(2)}, u32[]{:S(2)}) collective-permute-start(f32[2,128,128]{2,1,0:T(8,128)S(1)} %get-tuple-element.24), channel_id=1, source_target_pairs={{0,1},{1,0},{2,3},{3,2},{4,5},{5,4},{6,7},{7,6},{8,9},{9,8},{10,11... | collective-permute-start | bytes 393224 | tf_op jit(solution)/shard_map/ppermute | solution.py:436
  3.8 8.7 %collective-permute-start.1 = (f32[88,128]{1,0:T(8,128)S(1)}, f32[88,128]{1,0:T(8,128)S(1)}, u32[]{:S(2)}, u32[]{:S(2)}) collective-permute-start(f32[88,128]{1,0:T(8,128)S(1)} %get-tuple-element.23), channel_id=1, source_target_pairs={{0,24},{8,16},{16,8},{24,0},{1,25},{9,17},{17,9},{25,1},{2,26},{10... | collective-permute-start | bytes 135176 | tf_op jit(solution)/shard_map/ppermute | solution.py:435
  5.1 7.3 %collective-permute-start.3 = (f32[80,128]{1,0:T(8,128)S(1)}, f32[80,128]{1,0:T(8,128)S(1)}, u32[]{:S(2)}, u32[]{:S(2)}) collective-permute-start(f32[80,128]{1,0:T(8,128)S(1)} %get-tuple-element.26), channel_id=1, source_target_pairs={{0,2},{2,0},{4,6},{6,4},{1,3},{3,1},{5,7},{7,5},{8,10},{10,8},{12,... | collective-permute-start | bytes 122888 | tf_op jit(solution)/shard_map/ppermute | solution.py:439
  5.6 6.9 %collective-permute-start.4 = (f32[64,128]{1,0:T(8,128)S(1)}, f32[64,128]{1,0:T(8,128)S(1)}, u32[]{:S(2)}, u32[]{:S(2)}) collective-permute-start(f32[64,128]{1,0:T(8,128)S(1)} %get-tuple-element.27), channel_id=1, source_target_pairs={{2,4},{4,2},{3,5},{5,3},{10,12},{12,10},{11,13},{13,11},{18,20},{2... | collective-permute-start | bytes 98312 | tf_op jit(solution)/shard_map/ppermute | solution.py:440
  13.9 5.3 %collective-permute-start.5 = (f32[4,64,128]{2,1,0:T(8,128)S(1)}, f32[4,64,128]{2,1,0:T(8,128)S(1)}, u32[]{:S(2)}, u32[]{:S(2)}) collective-permute-start(f32[4,64,128]{2,1,0:T(8,128)S(1)} %get-tuple-element.34), channel_id=1, source_target_pairs={{0,1},{1,0},{2,3},{3,2},{4,5},{5,4},{6,7},{7,6},{8,9},{9,8},{10,11... | collective-permute-start | bytes 393224 | tf_op jit(solution)/shard_map/ppermute | solution.py:450
